TPU v7x, 32 devices: a whole 2x2x4 slice. The times are simulated.
32 devices in a mesh: rep: 4 (over x, core), shard: 8 (over z, y).
Axes of the slice: x: 2, y: 2, z: 4, core: 2. Of those that a mesh axis runs over, the one named last changes fastest.
Arguments:
- tokens: bfloat16 [16384, 2048], P(('rep', 'shard')), may hold values from -6 to 6
- cotangent: bfloat16 [16384, 2048], P(('rep', 'shard')), may hold values from -6 to 6
- lengths: int32 [64], replicated, may hold values from 128 to 384, as said below
- order: int32 [64], P(('rep', 'shard')), may hold values from 0 to 63, as said below
- mask: int32 [16384], P(('rep', 'shard')), may hold values from 0 to 1, as said below
- in_weight: float32 [2048, 8512], P('shard'), may hold values from -0.125 to 0.125
- out_weight: float32 [4096, 2048], P('shard'), may hold values from -0.09375 to 0.09375
- conv_weight: float32 [4, 4352], replicated, may hold values from -3 to 3
- conv_bias: float32 [4352], replicated, may hold values from -3 to 3
- dt_bias: float32 [64], replicated, may hold values from -7 to -2
- a_log: float32 [64], replicated, may hold values from -1 to 2.5
- skip_gain: float32 [64], replicated, may hold values from 0.5 to 2
- gain_outer: float32 [2048], replicated, may hold values from 0.5 to 1.5
- gain_inner: float32 [4096], replicated, may hold values from 0.5 to 1.5
Outputs:
- layer_out: bfloat16 [16384, 2048], P(('rep', 'shard'))
- grad_tokens: float32 [16384, 2048], P(('rep', 'shard'))
- grad_in_weight: float32 [2048, 8512], P('shard')
- grad_out_weight: float32 [4096, 2048], P('shard')
- grad_conv_weight: float32 [4, 4352], replicated
- grad_conv_bias: float32 [4352], replicated
- grad_dt_bias: float32 [64], replicated
- grad_a_log: float32 [64], replicated
- grad_skip_gain: float32 [64], replicated
- grad_gain_outer: float32 [2048], replicated
- grad_gain_inner: float32 [4096], replicated
Inputs may be any that keep to these rules, and one draw needn't show every extreme that they name: Each block of 512 rows holds 2 sequences whose lengths sum to at most 512. `order`: A permutation of the sequences. `mask`: 1 exactly on the rows that a block's sequences fill, 0 on the rest of the block.
All inputs are finite; a program needn't handle non-finite values.
Results may differ from a plain program's by a relative error of at most 0.012.
Values may be sent and summed in bfloat16 or wider, within the bound.
No kernel may reach another device: no remote copies, remote signals or barrier semaphores. Data moves between devices by JAX's collectives and lax.ppermute only.
A program may use at most 384 MiB of HBM per device.

v0:
```python
import jax
import jax.numpy as jnp
from jax import lax
from jax.sharding import PartitionSpec as P

DIN = 4096
P_SIZE = 64
N = 128
KCONV = 4
Q = 256
H = 64


EPSILON = 1e-05
HIGHEST = lax.Precision.HIGHEST
CONTRACT_LAST = (((1,), (1,)), ((), ()))
CONTRACT_FIRST = (((0,), (0,)), ((), ()))


def segment_ids(order_here, lengths, total_rows):
    catalog = jnp.arange(lengths.shape[0], dtype=jnp.int32)
    picked = jnp.sum(
        jnp.where(order_here[:, None] == catalog[None, :], lengths[None, :], 0), axis=1
    )
    bounds = jnp.cumsum(picked)
    row_index = jnp.arange(total_rows, dtype=jnp.int32)
    return jnp.sum((row_index[:, None] >= bounds[None, :]).astype(jnp.int32), axis=1)


def convolve(channels, segment, conv_weight, conv_bias):
    total_rows = channels.shape[0]
    result = conv_bias[None, :] + conv_weight[KCONV - 1][None, :] * channels
    for back_step in range(1, KCONV):
        shifted = jnp.concatenate(
            [
                jnp.zeros((back_step, channels.shape[1]), jnp.float32),
                channels[: total_rows - back_step],
            ],
            0,
        )
        earlier = jnp.concatenate(
            [jnp.full((back_step,), -1, jnp.int32), segment[: total_rows - back_step]]
        )
        linked = (earlier == segment).astype(jnp.float32)
        result = result + conv_weight[KCONV - 1 - back_step][None, :] * shifted * linked[:, None]
    return jax.nn.silu(result)


def block_step(state, pieces):
    values, bmat, cmat, step_size, decay, segment, prev_segment = pieces
    cumul = jnp.cumsum(decay, axis=0)
    final = cumul[-1]
    size_q = segment.shape[0]
    row_index = jnp.arange(size_q, dtype=jnp.int32)
    allowed = (segment[:, None] == segment[None, :]) & (row_index[:, None] >= row_index[None, :])
    spread = cumul.T[:, :, None] - cumul.T[:, None, :]
    weights = jnp.exp(jnp.where(allowed[None], spread, -1e30))
    scores = jnp.dot(cmat, bmat.T, precision=HIGHEST)
    mixing = weights * scores[None] * step_size.T[:, None, :]
    output = jnp.einsum("hij,jhp->ihp", mixing, values, precision=HIGHEST)
    entering = jnp.exp(cumul) * (segment == prev_segment).astype(jnp.float32)[:, None]
    output = (
        output + jnp.einsum("in,hpn->ihp", cmat, state, precision=HIGHEST) * entering[:, :, None]
    )
    tail_keep = (segment == segment[-1])[:, None]
    tail = jnp.exp(jnp.where(tail_keep, final[None, :] - cumul, -1e30)) * step_size
    carried = jnp.exp(final) * (segment[-1] == prev_segment).astype(jnp.float32)
    state = state * carried[:, None, None] + jnp.einsum(
        "jh,jhp,jn->hpn", tail, values, bmat, precision=HIGHEST
    )
    return (state, output)


def mixer(projected, segment, conv_weight, conv_bias, dt_bias, a_log, skip_gain, gain_inner):
    total_rows = projected.shape[0]
    gate_part = projected[:, :DIN]
    conv_out = convolve(projected[:, DIN : 2 * DIN + 2 * N], segment, conv_weight, conv_bias)
    dt_raw = projected[:, 2 * DIN + 2 * N :]
    step_size = jax.nn.softplus(dt_raw + dt_bias[None, :])
    decay = -jnp.exp(a_log)[None, :] * step_size
    values = conv_out[:, :DIN].reshape(total_rows, H, P_SIZE)
    bmat = conv_out[:, DIN : DIN + N]
    cmat = conv_out[:, DIN + N :]
    blocks = total_rows // Q
    prev_segment = jnp.concatenate(
        [jnp.full((1,), -1, jnp.int32), segment[Q - 1 : total_rows - 1 : Q]]
    )
    pieces = (
        values.reshape(blocks, Q, H, P_SIZE),
        bmat.reshape(blocks, Q, N),
        cmat.reshape(blocks, Q, N),
        step_size.reshape(blocks, Q, H),
        decay.reshape(blocks, Q, H),
        segment.reshape(blocks, Q),
        prev_segment,
    )
    _, outputs = lax.scan(
        jax.checkpoint(block_step), jnp.zeros((H, P_SIZE, N), jnp.float32), pieces
    )
    scanned = outputs.reshape(total_rows, H, P_SIZE) + skip_gain[None, :, None] * values
    gated = scanned.reshape(total_rows, DIN) * jax.nn.silu(gate_part)
    return (
        gated
        * lax.rsqrt(jnp.mean(gated * gated, axis=1, keepdims=True) + EPSILON)
        * gain_inner[None, :]
    )


def norm_outer(activ, gain):
    return (
        activ * lax.rsqrt(jnp.mean(activ * activ, axis=1, keepdims=True) + EPSILON) * gain[None, :]
    )


def term_rows(source, upstream):
    return lax.dot_general(source, upstream, CONTRACT_FIRST, preferred_element_type=jnp.float32)


def shards(
    tokens,
    cotangent,
    lengths,
    order,
    mask,
    in_weight,
    out_weight,
    conv_weight,
    conv_bias,
    dt_bias,
    a_log,
    skip_gain,
    gain_outer,
    gain_inner,
):
    tok_rows = tokens.shape[0]
    segment = segment_ids(order, lengths, tok_rows)
    activ = tokens.astype(jnp.float32)
    keep = mask.astype(jnp.float32)
    w_in16 = in_weight.astype(jnp.bfloat16)
    w_out16 = out_weight.astype(jnp.bfloat16)
    normed, norm_back = jax.vjp(norm_outer, activ, gain_outer)
    normed16 = normed.astype(jnp.bfloat16)
    columns = normed16
    proj = jnp.dot(
        columns,
        lax.all_gather(w_in16, "shard", axis=0, tiled=True),
        preferred_element_type=jnp.float32,
    )
    proj16 = proj.astype(jnp.bfloat16)
    small = (conv_weight, conv_bias, dt_bias, a_log, skip_gain, gain_inner)

    def local_mixer(projected, params):
        return mixer(projected, segment, *params)

    inner, mixer_back = jax.vjp(local_mixer, proj16.astype(jnp.float32), small)
    inner16 = inner.astype(jnp.bfloat16)
    columns = inner16
    branch = jnp.dot(
        columns,
        lax.all_gather(w_out16, "shard", axis=0, tiled=True),
        preferred_element_type=jnp.float32,
    )
    layer_out = (keep[:, None] * (activ + branch)).astype(jnp.bfloat16)
    cot_masked = cotangent.astype(jnp.float32) * keep[:, None]
    gout = cot_masked.astype(jnp.bfloat16)
    grad_inner = lax.dot_general(
        gout,
        lax.all_gather(w_out16, "shard", axis=0, tiled=True),
        CONTRACT_LAST,
        preferred_element_type=jnp.float32,
    )
    grad_proj, grad_small = mixer_back(grad_inner)
    gproj = grad_proj.astype(jnp.bfloat16)
    grad_normed = lax.dot_general(
        gproj,
        lax.all_gather(w_in16, "shard", axis=0, tiled=True),
        CONTRACT_LAST,
        preferred_element_type=jnp.float32,
    )
    grad_from_norm, grad_gain_outer = norm_back(grad_normed)
    grad_tokens = cot_masked + grad_from_norm
    share_in = lax.psum_scatter(
        term_rows(normed16, gproj), "shard", scatter_dimension=0, tiled=True
    )
    share_out = lax.psum_scatter(term_rows(inner16, gout), "shard", scatter_dimension=0, tiled=True)
    grad_in_weight, grad_out_weight = lax.psum((share_in, share_out), "rep")
    g_cw, g_cb, g_db, g_al, g_sk, g_gi = grad_small
    g_cw, g_cb, g_db, g_al, g_sk, g_gi, g_go = lax.psum(
        (g_cw, g_cb, g_db, g_al, g_sk, g_gi, grad_gain_outer), ("rep", "shard")
    )
    return (
        layer_out,
        grad_tokens,
        grad_in_weight,
        grad_out_weight,
        g_cw,
        g_cb,
        g_db,
        g_al,
        g_sk,
        g_go,
        g_gi,
    )


def solution(mesh):
    placed = (
        P(("rep", "shard"), None),
        P(("rep", "shard"), None),
        P(),
        P(("rep", "shard")),
        P(("rep", "shard")),
        P("shard", None),
        P("shard", None),
        P(),
        P(),
        P(),
        P(),
        P(),
        P(),
        P(),
    )
    return jax.shard_map(
        shards,
        mesh=mesh,
        in_specs=placed,
        out_specs=(
            P(("rep", "shard"), None),
            P(("rep", "shard"), None),
            P("shard", None),
            P("shard", None),
            P(),
            P(),
            P(),
            P(),
            P(),
            P(),
            P(),
        ),
        check_vma=False,
    )
```

profile of v0, /device:TPU:0, one launch (start us, length us, event | category | flops | bytes accessed | tf_op | source)
XLA Modules:
  0.0 3212.8 jit_solution(2805036007195462335)
XLA Ops:
  22.2 656.9 %all-gather.3.cloned.1.call-done = bf16[2048,8512]{0,1:T(8,128)(2,1)} async-done(((bf16[256,8512]{0,1:T(8,128)(2,1)}), bf16[2048,8512]{0,1:T(8,128)(2,1)}) %all-gather.3.cloned.1.call-update) | async-done | bytes 34865168 | tf_op jit(solution)/shard_map/all_gather | solution.py:146
  679.1 26.9 fusion.90
  727.1 18.9 fusion.93
  779.8 276.8 %while.41 = (s32[]{:T(128)}, f32[64,64,128]{2,1,0:T(8,128)S(1)}, f32[2,256,64,64]{1,0,3,2:T(2,128)}, f32[2,64,64,128]{3,2,1,0:T(8,128)}, f32[2,256,64]{1,2,0:T(8...) while((s32[]{:T(128)}, f32[64,64,128]{2,1,0:T(8,128)S(1)}, ...), condition=%wide.region_7.8_spmd.clone, body=%wide.region_4.7_spmd.clone.sunk | while | flops 6568035328 | bytes 50740480 | solution.py:97
  786.7 20.4 fusion.200
  821.3 84.4 %dynamic_update_slice.78 = f32[2,256,64,64]{1,0,3,2:T(2,128)} dynamic-update-slice(f32[2,256,64,64]{1,0,3,2:T(2,128)} %get-tuple-element.1078, f32[1,256,64,64]{1,0,3,2:T(1,128)} %copy.303, s32[]{:T(128)S(6)} %copy.332, s32[]{:T(128)} %constant.139.clone.1..sunk, s32[]{:T(128)} %constant.139.clone.1..sunk, s32[]{:T(128)} %constant.139.clone.1..sunk) | dynamic-update-slice | bytes 8388612 | tf_op jit(solution)/shard_map/jvp()/while/body/jit(dynamic_update_index_in_dim)/dynamic_update_slice | solution.py:97
  919.3 20.4 fusion.200
  953.9 84.3 %dynamic_update_slice.78 = f32[2,256,64,64]{1,0,3,2:T(2,128)} dynamic-update-slice(f32[2,256,64,64]{1,0,3,2:T(2,128)} %get-tuple-element.1078, f32[1,256,64,64]{1,0,3,2:T(1,128)} %copy.303, s32[]{:T(128)S(6)} %copy.332, s32[]{:T(128)} %constant.139.clone.1..sunk, s32[]{:T(128)} %constant.139.clone.1..sunk, s32[]{:T(128)} %constant.139.clone.1..sunk) | dynamic-update-slice | bytes 8388612 | tf_op jit(solution)/shard_map/jvp()/while/body/jit(dynamic_update_index_in_dim)/dynamic_update_slice | solution.py:97
  1075.5 18.8 fusion.109
  1110.2 18.4 multiply_reduce_fusion.10
  1149.7 460.9 %while.42 = (s32[]{:T(128)}, f32[64,64,128]{2,1,0:T(8,128)}, f32[2,256,64,64]{1,0,3,2:T(2,128)}, f32[2,256,128]{2,1,0:T(8,128)}, f32[2,256,128]{2,1,0:T(8,128)},...) while((s32[]{:T(128)}, f32[64,64,128]{2,1,0:T(8,128)}, ...), condition=%wide.region_22.23_spmd.clone, body=%wide.region_10.22_spmd.clone.sunk | while | flops 14885585920 | bytes 143937616 | solution.py:97
  1188.3 27.5 fusion.223
  1254.5 17.6 fusion.226
  1291.0 84.5 %dynamic_update_slice.82 = f32[2,256,64,64]{1,0,3,2:T(2,128)} dynamic-update-slice(f32[2,256,64,64]{1,0,3,2:T(2,128)} %get-tuple-element.1127, f32[1,256,64,64]{1,0,3,2:T(1,128)} %copy.317, s32[]{:T(128)S(6)} %sub.244, s32[]{:T(128)} %constant.139.clone.1..sunk.1, s32[]{:T(128)} %constant.139.clone.1..sunk.1, s32[]{:T(128)} %constant.139.clone.1..sunk.1) | dynamic-update-slice | bytes 8388612 | tf_op jit(solution)/shard_map/transpose(jvp())/while/body/jit(dynamic_update_index_in_dim)/dynamic_update_slice | solution.py:97
  1415.5 27.6 fusion.223
  1481.8 17.8 fusion.226
  1518.5 84.6 %dynamic_update_slice.82 = f32[2,256,64,64]{1,0,3,2:T(2,128)} dynamic-update-slice(f32[2,256,64,64]{1,0,3,2:T(2,128)} %get-tuple-element.1127, f32[1,256,64,64]{1,0,3,2:T(1,128)} %copy.317, s32[]{:T(128)S(6)} %sub.244, s32[]{:T(128)} %constant.139.clone.1..sunk.1, s32[]{:T(128)} %constant.139.clone.1..sunk.1, s32[]{:T(128)} %constant.139.clone.1..sunk.1) | dynamic-update-slice | bytes 8388612 | tf_op jit(solution)/shard_map/transpose(jvp())/while/body/jit(dynamic_update_index_in_dim)/dynamic_update_slice | solution.py:97
  1688.8 19.3 fusion.127
  1708.1 33.9 %fusion.113 = f32[2048,8512]{0,1:T(8,128)} fusion(bf16[512,2048]{1,0:T(8,128)(2,1)S(1)} %copy-done.6, f32[2048]{0:T(1024)S(1)} %copy-done.50, f32[512]{0:T(512)S(1)} %copy-done.54, f32[512,4096]{0,1:T(8,128)} %get-tuple-element.823, f32[512,4352]{0,1:T(8,128)} %get-tuple-element.824, f32[512,64]{0,1:T(8,128)S(1)} %get-tuple-element.792), kind=kOutput, calls=%fused_computation.193 | convolution fusion | flops 17868226560 | bytes 89270272 | tf_op jit(solution)/shard_map/dot_general | solution.py:116
  1743.0 1097.4 %reduce-scatter.3.cloned.1.call-done = f32[256,8512]{0,1:T(8,128)} async-done(((f32[2048,8512]{0,1:T(8,128)}), f32[256,8512]{0,1:T(8,128)}) %reduce-scatter.3.cloned.1.call-update) | async-done | bytes 8716304 | tf_op jit(solution)/shard_map/reduce_scatter | solution.py:182
  2840.7 33.2 %fusion.100 = (f32[2048]{0:T(1024)S(1)}, f32[512]{0:T(512)S(1)}, f32[512,2048]{1,0:T(8,128)}) fusion(bf16[512,2048]{1,0:T(8,128)(2,1)S(1)} %copy-done.6, f32[512]{0:T(512)S(1)} %copy-done.54, f32[2048]{0:T(1024)S(1)} %copy-done.50, bf16[2048,8512]{0,1:T(8,128)(2,1)} %all-gather.3.cloned.1.call-done, f32[512,4096]{0,1:T(8,128)} %get-tuple-element.823, ...), kind=kOutput, calls=%fused_computation.181 | convolution fusion | flops 17871370240 | bytes 58609664 | tf_op jit(solution)/shard_map/dot_general | solution.py:174
  2873.9 40.7 %all-reduce.19 = (f32[4352]{0:T(1024)}, f32[64]{0:T(128)}, f32[64]{0:T(128)}, f32[64]{0:T(128)}, f32[2048]{0:T(1024)}, /*index=5*/f32[4096]{0:T(1024)}) all-reduce(f32[4352]{0:T(1024)S(1)} %get-tuple-element.719, f32[64]{0:T(128)S(1)} %copy-done.59, ...), channel_id=1, replica_groups=mesh['rep'=4,'shard'=8] {'rep','shard'}, use_global_device_ids=true, to_apply=%region_34.35 | all-reduce | flops 10688 | bytes 85504 | tf_op jit(solution)/shard_map/psum | solution.py:188
  2936.8 27.6 all-reduce.24.cloned.1.call-done
  2964.4 231.3 %all-reduce.26.cloned.1.call-done = (f32[256,8512]{0,1:T(8,128)}, f32[512,2048]{1,0:T(8,128)}) async-done(((f32[256,8512]{0,1:T(8,128)}, f32[512,2048]{1,0:T(8,128)}), (f32[256,8512]{0,1:T(8,128)}, f32[512,2048]{1,0:T(8,128)})) %all-reduce.26.cloned.1.call-update) | async-done | bytes 12910608 | tf_op jit(solution)/shard_map/psum | solution.py:186
  (416 shorter events, 479.5 us)
Async XLA Ops:
  7.2 671.9 %all-gather.3.cloned.1.call-start = ((), (), s32[]{:S(2)}) async-start(), calls=%async_computation.2 | async-start | bytes 39223296 | tf_op jit(solution)/shard_map/all_gather | solution.py:146
  12.6 666.5 %copy-start.49 = (f32[2048]{0:T(1024)S(1)}, f32[2048]{0:T(1024)}, u32[]{:S(2)}) copy-start(f32[2048]{0:T(1024)} %param.30) | copy-start | bytes 24580
  12.6 1081.8 %all-gather.5.cloned.1.call-start = ((), (), s32[]{:S(2)}) async-start(), calls=%async_computation.3 | async-start | bytes 18874368 | tf_op jit(solution)/shard_map/all_gather | solution.py:160
  16.5 1726.4 %reduce-scatter.5.cloned.1.call-start = ((), (), s32[]{:S(2)}) async-start(), calls=%async_computation.5 | async-start | bytes 37748736 | tf_op jit(solution)/shard_map/reduce_scatter | solution.py:185
  19.9 707.0 %copy-start.23 = (f32[4352]{0:T(1024)}, f32[4352]{0:T(1024)S(1)}, u32[]{:S(2)}) copy-start(f32[4352]{0:T(1024)S(1)} %get-tuple-element.723) | copy-start | bytes 52228
  19.9 707.0 %copy-start.25 = (f32[4352]{0:T(1024)}, f32[4352]{0:T(1024)S(1)}, u32[]{:S(2)}) copy-start(f32[4352]{0:T(1024)S(1)} %get-tuple-element.725) | copy-start | bytes 52228
  20.0 707.0 %copy-start.27 = (f32[4352]{0:T(1024)}, f32[4352]{0:T(1024)S(1)}, u32[]{:S(2)}) copy-start(f32[4352]{0:T(1024)S(1)} %get-tuple-element.724) | copy-start | bytes 52228
  20.0 707.0 %copy-start.29 = (f32[4352]{0:T(1024)}, f32[4352]{0:T(1024)S(1)}, u32[]{:S(2)}) copy-start(f32[4352]{0:T(1024)S(1)} %get-tuple-element.726) | copy-start | bytes 52228
  20.0 706.7 %copy-start.57 = (f32[64]{0:T(128)}, f32[64]{0:T(128)S(1)}, u32[]{:S(2)}) copy-start(f32[64]{0:T(128)S(1)} %exponential_negate_fusion) | copy-start | bytes 772
  22.1 683.9 %copy-start.41 = (f32[512]{0:T(512)}, f32[512]{0:T(512)S(1)}, u32[]{:S(2)}) copy-start(f32[512]{0:T(512)S(1)} %fusion.102) | copy-start | bytes 6148
  22.1 683.9 %copy-start.53 = (f32[512]{0:T(512)}, f32[512]{0:T(512)S(1)}, u32[]{:S(2)}) copy-start(f32[512]{0:T(512)S(1)} %fusion.123) | copy-start | bytes 6148
  22.2 704.8 %copy-start.35 = (f32[512]{0:T(512)}, f32[512]{0:T(512)S(1)}, u32[]{:S(2)}) copy-start(f32[512]{0:T(512)S(1)} %get-tuple-element.830) | copy-start | bytes 6148
  22.2 704.8 %copy-start.37 = (f32[512]{0:T(512)}, f32[512]{0:T(512)S(1)}, u32[]{:S(2)}) copy-start(f32[512]{0:T(512)S(1)} %get-tuple-element.832) | copy-start | bytes 6148
  22.2 704.8 %copy-start.39 = (f32[512]{0:T(512)}, f32[512]{0:T(512)S(1)}, u32[]{:S(2)}) copy-start(f32[512]{0:T(512)S(1)} %get-tuple-element.831) | copy-start | bytes 6148
  1094.3 1746.0 %reduce-scatter.3.cloned.1.call-start = ((), (), s32[]{:S(2)}) async-start(), calls=%async_computation.4 | async-start | bytes 78446592 | tf_op jit(solution)/shard_map/reduce_scatter | solution.py:182
  1278.2 97.4 %copy-start.13 = (f32[2,256,64]{1,0,2:T(2,128)S(1)}, f32[2,256,64]{1,0,2:T(2,128)}, u32[]{:S(2)}) copy-start(f32[2,256,64]{1,0,2:T(2,128)} %copy-done.12) | copy-start | bytes 393220 | tf_op jit(solution)/shard_map/transpose(jvp())/while
  1278.2 97.4 %copy-start.67 = (s32[2]{0:T(128)S(1)}, s32[2]{0:T(128)}, u32[]{:S(2)}) copy-start(s32[2]{0:T(128)} %copy-done.66) | copy-start | bytes 28 | tf_op jit(solution)/shard_map/transpose(jvp())/while
  1505.7 97.4 %copy-start.11 = (f32[2,256,64]{1,2,0:T(8,128)S(1)}, f32[2,256,64]{1,2,0:T(8,128)}, u32[]{:S(2)}) copy-start(f32[2,256,64]{1,2,0:T(8,128)} %copy-done.10) | copy-start | bytes 393220 | tf_op jit(solution)/shard_map/transpose(jvp())/while
  1505.7 97.4 %copy-start.13 = (f32[2,256,64]{1,0,2:T(2,128)S(1)}, f32[2,256,64]{1,0,2:T(2,128)}, u32[]{:S(2)}) copy-start(f32[2,256,64]{1,0,2:T(2,128)} %copy-done.12) | copy-start | bytes 393220 | tf_op jit(solution)/shard_map/transpose(jvp())/while
  1505.7 97.4 %copy-start.67 = (s32[2]{0:T(128)S(1)}, s32[2]{0:T(128)}, u32[]{:S(2)}) copy-start(s32[2]{0:T(128)} %copy-done.66) | copy-start | bytes 28 | tf_op jit(solution)/shard_map/transpose(jvp())/while
  1742.0 1098.4 %copy-start.65 = (f32[64]{0:T(128)S(1)}, f32[64]{0:T(128)}, u32[]{:S(2)}) copy-start(f32[64]{0:T(128)} %param.28) | copy-start | bytes 772
  1742.0 1098.4 %copy-start.33 = (f32[4096]{0:T(1024)S(1)}, f32[4096]{0:T(1024)}, u32[]{:S(2)}) copy-start(f32[4096]{0:T(1024)} %get-tuple-element.789) | copy-start | bytes 49156
  1742.1 1222.4 %all-reduce.24.cloned.1.call-start = ((), (), s32[]{:S(2)}) async-start(), calls=%async_computation.6 | async-start | bytes 139264 | tf_op jit(solution)/shard_map/psum | solution.py:188
  1742.9 1452.8 %all-reduce.26.cloned.1.call-start = ((), (), s32[]{:S(2)}) async-start(), calls=%async_computation.7 | async-start | bytes 25821184 | tf_op jit(solution)/shard_map/psum | solution.py:186
  (74 other events, 1484.6 us)
Sparse Core Ops, SparseCore 0:
  12.8 666.3 all-gather.2
  681.8 227.6 all-gather.4
  1094.5 542.8 reduce-scatter.4
  1742.2 1098.1 reduce-scatter.2
  2847.3 117.0 all-reduce.23
  2967.1 228.5 all-reduce.25
where the time goes:
time: 3250 us; the launch traced here: 3210 us
  waiting for transfers between devices  2010 us (62%)
  local copies, waits for them, and re-layouts  549 us (17%)
  matrix products  376 us (12%)
  other arithmetic  193 us (6%)
  blocking collectives  40.7 us (1%)
    reduce_scatter x1, waiting for transfers between devices, shards(): lax.psum_scatter(term_rows(normed16, gproj), 'shard', scatter_dimension=0...  1100 us
    all_gather x1, waiting for transfers between devices, shards(): lax.all_gather(w_in16, 'shard', axis=0, tiled=True)  657 us
    dynamic_update_slice x12, local copies, waits for them, and re-layouts, mixer(): lax.scan(jax.checkpoint(block_step), jnp.zeros((H, P_SIZE, N), jnp.float3...  376 us
    psum x1, waiting for transfers between devices, shards(): grad_in_weight, grad_out_weight = lax.psum((share_in, share_out), 'rep')  231 us
    dot_general x6, matrix products, block_step(): output = jnp.einsum('hij,jhp->ihp', mixing, values, precision=HIGHEST)  131 us
  transfers between devices with their start and end apart: 6, of which 4 were waited for; matrix products, arithmetic and copies ran while one was open for 34% of the time, Pallas kernels for 0%

commit v1 on v0

v1 whole, which is shorter than its diff:
```python
import functools

import jax
import jax.numpy as jnp
from jax import lax
from jax.experimental import pallas as pl
from jax.experimental.pallas import tpu as pltpu
from jax.sharding import PartitionSpec as P

D = 2048
DIN = 4096
P_SIZE = 64
N = 128
Q = 256
H = 64
CONVCH = DIN + 2 * N
EPSILON = 1e-05
LOG2E = 1.4426950408889634
LANES = 128
TOK = 512
HIGHEST = lax.Precision.HIGHEST
BF = jnp.bfloat16
F32 = jnp.float32
NT = (((1,), (1,)), ((), ()))
TN = (((0,), (0,)), ((), ()))
VMEM_LIMIT = 48 * 1024 * 1024
RING = (0, 2, 4, 6, 7, 5, 3, 1)


def mm(a, b):
    return jnp.dot(a, b, preferred_element_type=F32)


def mm_nt(a, b):
    return lax.dot_general(a, b, NT, preferred_element_type=F32)


def iota(shape, dim):
    return lax.broadcasted_iota(jnp.int32, shape, dim)


def start_of(rows, b1, b2):
    return jnp.where(rows >= b2, b2, jnp.where(rows >= b1, b1, 0))


def sigmoid(v):
    return 0.5 * jnp.tanh(0.5 * v) + 0.5


def conv_pre(x, taps, bias, lk):
    pre = bias + taps[3] * x
    for k in range(1, 4):
        pre = pre + taps[3 - k] * (pltpu.roll(x, k, 0) * lk[k - 1])
    return pre


def taps_of(cw_ref, lanes):
    return [cw_ref[k : k + 1, lanes] for k in range(4)], cw_ref[4:5, lanes]


def prepare(b1, b2, bc_ref, dt_ref, cwb_ref, hp_ref, sel_ref, lk, score, bmat, cmat, btrans, ctrans,
            dts, sig, cum, cumt, ecol, tcol, transposed):
    rows = iota((TOK, LANES), 0)
    pos = rows - start_of(rows, b1, b2)
    for k in range(1, 4):
        lk[k - 1] = (pos >= k).astype(F32)
    links = [lk[0], lk[1], lk[2]]
    for half, keep in ((0, bmat), (1, cmat)):
        lanes = slice(half * LANES, (half + 1) * LANES)
        taps, bias = taps_of(cwb_ref, lanes)
        pre = conv_pre(bc_ref[:, lanes].astype(F32), taps, bias, links)
        act = pre * sigmoid(pre)
        keep[...] = act.astype(BF)
        if half == 0:
            btrans[...] = act[:Q].T.astype(BF)
        elif ctrans is not None:
            ctrans[...] = act[Q:].T.astype(BF)
    for c in range(2):
        part = slice(c * Q, (c + 1) * Q)
        if transposed:
            s = mm_nt(bmat[part, :], cmat[part, :])
        else:
            s = mm_nt(cmat[part, :], bmat[part, :])
        score[c] = jnp.where(allowed(c, b1, b2, transposed), s, 0.0)
    raw = mm(dt_ref[...], sel_ref[...]) + hp_ref[0:1, :]
    step = jnp.maximum(raw, 0.0) + jnp.log1p(jnp.exp(-jnp.abs(raw)))
    dts[...] = step
    if sig is not None:
        sig[...] = sigmoid(raw)
    decay = step * (hp_ref[1:2, :] * LOG2E)
    lower = (iota((Q, Q), 0) >= iota((Q, Q), 1)).astype(F32)
    for c in range(2):
        part = slice(c * Q, (c + 1) * Q)
        total = jnp.dot(lower, decay[part], precision=HIGHEST, preferred_element_type=F32)
        cum[part, :] = total
        cumt[:, part] = total.T
        if c == 0:
            last = start_of(Q - 1, b1, b2)
            tcol[...] = jnp.where(rows[:Q] >= last, jnp.exp2(total[Q - 1 : Q, :] - total), 0.0)
        else:
            linked = start_of(rows[Q:], b1, b2) <= Q - 1
            ecol[...] = jnp.where(linked, jnp.exp2(total), 0.0)


def allowed(c, b1, b2, transposed):
    late = iota((Q, Q), 1 if transposed else 0) + c * Q
    early = iota((Q, Q), 0 if transposed else 1) + c * Q
    return (early <= late) & (early >= start_of(late, b1, b2))


def pair(ref_value, first):
    return jnp.where(first, ref_value[:, 0:1], ref_value[:, 1:2])


def fwd_kernel(bnd, xs_ref, bc_ref, dt_ref, cwx_ref, cwb_ref, hp_ref, sel_ref, out_ref,
               lk, score, bmat, cmat, btrans, dts, cum, cumt, ecol, tcol):
    b, t = pl.program_id(0), pl.program_id(1)

    @pl.when(t == 0)
    def _():
        prepare(bnd[b, 0], bnd[b, 1], bc_ref, dt_ref, cwb_ref, hp_ref, sel_ref, lk, score, bmat, cmat,
                btrans, None, dts, None, cum, cumt, ecol, tcol, False)

    turn = lax.rem(LANES - 2 * t, LANES)
    taps, bias = taps_of(cwx_ref, slice(None))
    pre = conv_pre(xs_ref[...].astype(F32), taps, bias, [lk[0], lk[1], lk[2]])
    x = pre * sigmoid(pre)
    first = iota((TOK, LANES), 1) < P_SIZE
    xt = x * pair(pltpu.roll(dts[...], turn, 1), first)
    xt16 = xt.astype(BF)
    mine = [jnp.where(first, xt16, jnp.zeros_like(xt16)), jnp.where(first, jnp.zeros_like(xt16), xt16)]
    cumr = pltpu.roll(cum[...], turn, 1)
    half = Q // 2
    outs = []
    for c in range(2):
        o = c * Q
        top = bottom = None
        for h in range(2):
            row = cumt[pl.ds(2 * t + h, 1), o : o + Q]
            col = cumr[o : o + Q, h : h + 1]
            w = jnp.exp2(jnp.minimum(col[:half] - row[:, :half], 0.0)) * score[c, :half, :half]
            y = mm(w.astype(BF), mine[h][o : o + half])
            top = y if top is None else top + y
            w = jnp.exp2(jnp.minimum(col[half:] - row, 0.0)) * score[c, half:, :]
            y = mm(w.astype(BF), mine[h][o : o + Q])
            bottom = y if bottom is None else bottom + y
        outs.append(jnp.concatenate([top, bottom], 0))
    tx = pair(pltpu.roll(tcol[...], turn, 1), first[:Q])
    ex = pair(pltpu.roll(ecol[...], turn, 1), first[:Q])
    state = mm(btrans[...], (tx * xt[:Q]).astype(BF))
    outs[1] = outs[1] + mm(cmat[Q:, :], state.astype(BF)) * ex
    skip = cwx_ref[5:6, :]
    out_ref[...] = jnp.concatenate(outs, 0) + skip * x


def bwd_kernel(bnd, xs_ref, bc_ref, dt_ref, cwx_ref, cwb_ref, hp_ref, sel_ref, scan_ref, dscan_ref,
               out_ref, dcw_ref, dhp_ref,
               lk, score, bmat, cmat, btrans, ctrans, dts, sig, cum, cumt, ecol, tcol, dscore, rsum, rsum3, dball, dcall):
    b, t = pl.program_id(0), pl.program_id(1)
    tiles = pl.num_programs(1)
    b1, b2 = bnd[b, 0], bnd[b, 1]

    @pl.when(t == 0)
    def _():
        prepare(b1, b2, bc_ref, dt_ref, cwb_ref, hp_ref, sel_ref, lk, score, bmat, cmat,
                btrans, ctrans, dts, sig, cum, cumt, ecol, tcol, True)
        dscore[...] = jnp.zeros_like(dscore)
        rsum[...] = jnp.zeros_like(rsum)
        rsum3[...] = jnp.zeros_like(rsum3)
        dball[...] = jnp.zeros_like(dball)
        dcall[...] = jnp.zeros_like(dcall)

    @pl.when((t == 0) & (b == 0))
    def _():
        dcw_ref[...] = jnp.zeros_like(dcw_ref)
        dhp_ref[...] = jnp.zeros_like(dhp_ref)

    turn = lax.rem(LANES - 2 * t, LANES)
    taps, bias = taps_of(cwx_ref, slice(None))
    links = [lk[0], lk[1], lk[2]]
    xin = xs_ref[...].astype(F32)
    pre = conv_pre(xin, taps, bias, links)
    sg = sigmoid(pre)
    x = pre * sg
    first = iota((TOK, LANES), 1) < P_SIZE
    dtx = pair(pltpu.roll(dts[...], turn, 1), first)
    xt = x * dtx
    xt16 = xt.astype(BF)
    xtf = xt16.astype(F32)
    skip = cwx_ref[5:6, :]
    dy = dscan_ref[...]
    dy16 = dy.astype(BF)
    dyf = dy16.astype(F32)
    mine = [jnp.where(first, dy16, jnp.zeros_like(dy16)), jnp.where(first, jnp.zeros_like(dy16), dy16)]
    cumr = pltpu.roll(cum[...], turn, 1)
    half = Q // 2
    parts = []
    for c in range(2):
        o = c * Q
        top = bottom = None
        for h in range(2):
            row = cumt[pl.ds(2 * t + h, 1), o : o + Q]
            col = cumr[o : o + Q, h : h + 1]
            w = jnp.exp2(jnp.minimum(row - col[:half], 0.0))
            dscore[c, :half, :] += w * mm_nt(xt16[o : o + half], mine[h][o : o + Q])
            y = mm((w * score[c, :half, :]).astype(BF), mine[h][o : o + Q])
            top = y if top is None else top + y
            w = jnp.exp2(jnp.minimum(row[:, half:] - col[half:], 0.0))
            dscore[c, half:, half:] += w * mm_nt(xt16[o + half : o + Q], mine[h][o + half : o + Q])
            y = mm((w * score[c, half:, half:]).astype(BF), mine[h][o + half : o + Q])
            bottom = y if bottom is None else bottom + y
        parts.append(jnp.concatenate([top, bottom], 0))
    tx = pair(pltpu.roll(tcol[...], turn, 1), first[:Q])
    ex = pair(pltpu.roll(ecol[...], turn, 1), first[:Q])
    txt16 = (tx * xt[:Q]).astype(BF)
    state = mm(btrans[...], txt16).astype(BF)
    dye = (ex * dy[Q:]).astype(BF)
    dstate = mm(ctrans[...], dye).astype(BF)
    dcall[...] += mm_nt(dye, state)
    dball[...] += mm_nt(txt16, dstate)
    across = tx * mm(bmat[:Q, :], dstate)
    within = jnp.concatenate(parts, 0)
    dxt = jnp.concatenate([parts[0] + across, parts[1]], 0)
    r1 = dyf * (scan_ref[...] - skip * x) - xtf * within
    r2 = x * dxt
    r3 = xtf[:Q] * across

    def split(v):
        hi = v.astype(BF)
        return [hi, (v - hi.astype(F32)).astype(BF)]

    def to_heads(width, offset):
        lane, head = iota((LANES, width), 0), iota((LANES, width), 1)
        return (head == offset + 2 * t + jnp.where(lane >= P_SIZE, 1, 0)).astype(BF)

    e1, e2 = to_heads(2 * LANES, 0), to_heads(2 * LANES, LANES)
    rsum[...] += mm(jnp.concatenate(split(r1), 1), jnp.concatenate([e1, e1], 0)) + mm(
        jnp.concatenate(split(r2), 1), jnp.concatenate([e2, e2], 0)
    )
    e3 = to_heads(LANES, 0)
    rsum3[...] += mm(jnp.concatenate(split(r3), 1), jnp.concatenate([e3, e3], 0))

    def conv_back(dact, pre, sg, xin, taps):
        dpre = dact * (sg * (1.0 + pre * (1.0 - sg)))
        g = taps[3] * dpre
        sums = [None] * 5
        sums[3] = jnp.sum(dpre * xin, axis=0, keepdims=True)
        sums[4] = jnp.sum(dpre, axis=0, keepdims=True)
        for k in range(1, 4):
            q = links[k - 1] * dpre
            g = g + taps[3 - k] * pltpu.roll(q, TOK - k, 0)
            sums[3 - k] = jnp.sum(q * pltpu.roll(xin, k, 0), axis=0, keepdims=True)
        return g, sums

    g, sums = conv_back(dxt * dtx + skip * dy, pre, sg, xin, taps)
    sums.append(jnp.sum(dy * x, axis=0, keepdims=True))
    sums.append(jnp.zeros((2, LANES), F32))
    here = pl.ds(pl.multiple_of(t * LANES, LANES), LANES)
    out_ref[:, here] = g.astype(BF)
    dcw_ref[:, here] += jnp.concatenate(sums, 0)

    @pl.when(t == tiles - 1)
    def _():
        db, dc = [], []
        for c in range(2):
            part = slice(c * Q, (c + 1) * Q)
            ds = jnp.where(allowed(c, b1, b2, True), dscore[c], 0.0)
            db.append(mm(ds.astype(BF), cmat[part, :]))
            dc.append(mm(ds.T.astype(BF), bmat[part, :]))
        db[0] = db[0] + dball[...]
        dc[1] = dc[1] + dcall[...]
        base = tiles * LANES
        for i, dact in enumerate((jnp.concatenate(db, 0), jnp.concatenate(dc, 0))):
            lanes = slice(i * LANES, (i + 1) * LANES)
            taps_b, bias_b = taps_of(cwb_ref, lanes)
            xin_b = bc_ref[:, lanes].astype(F32)
            pre_b = conv_pre(xin_b, taps_b, bias_b, links)
            g, sums = conv_back(dact, pre_b, sigmoid(pre_b), xin_b, taps_b)
            sums.append(jnp.zeros((3, LANES), F32))
            at = pl.ds(pl.multiple_of(base + i * LANES, LANES), LANES)
            out_ref[:, at] = g.astype(BF)
            dcw_ref[:, at] += jnp.concatenate(sums, 0)
        upper = (iota((Q, Q), 0) <= iota((Q, Q), 1)).astype(F32)
        below = (iota((Q, Q), 0) > iota((Q, Q), 1)).astype(F32)
        high = functools.partial(jnp.dot, precision=HIGHEST, preferred_element_type=F32)
        rate = hp_ref[1:2, :]
        da = jnp.concatenate(
            [
                high(upper, rsum[:Q, :LANES]) + high(below, rsum3[...]),
                high(upper, rsum[Q:, :LANES]),
            ],
            0,
        )
        step = dts[...]
        draw = (rsum[:, LANES:] + da * rate) * sig[...]
        dhp_ref[0:1, :] += jnp.sum(draw, axis=0, keepdims=True)
        dhp_ref[1:2, :] += jnp.sum(da * (rate * step), axis=0, keepdims=True)
        at = pl.ds(pl.multiple_of(base + 2 * LANES, LANES), LANES)
        out_ref[:, at] = mm_nt(draw.astype(BF), sel_ref[...]).astype(BF)


def stat_kernel(place, scan_ref, gate_ref, gin_ref, gain_ref, out_ref, one, two):
    t = pl.program_id(1)

    @pl.when(t == 0)
    def _():
        one[...] = jnp.zeros_like(one)
        two[...] = jnp.zeros_like(two)

    gate = gate_ref[...].astype(F32)
    gated = scan_ref[...] * (gate * sigmoid(gate))
    one[...] += gated * gated
    two[...] += gated * (gin_ref[...] * gain_ref[...])

    @pl.when(t == pl.num_programs(1) - 1)
    def _():
        a = jnp.sum(one[...].T, axis=0, keepdims=True)
        c = jnp.sum(two[...].T, axis=0, keepdims=True)
        out_ref[0] = jnp.concatenate([a, c, jnp.zeros((6, TOK), F32)], 0)


def gate_kernel(place, sum_ref, scan_ref, gate_ref, gin_ref, gain_ref, inner_ref, dgate_ref, dscan_ref, dgain_ref, rinv, coef):
    b, t = pl.program_id(0), pl.program_id(1)

    @pl.when(t == 0)
    def _():
        r = lax.rsqrt(sum_ref[0, 0:1, :] * (1.0 / DIN) + EPSILON)
        c = r * r * sum_ref[0, 1:2, :] * (1.0 / DIN)
        rinv[...] = jnp.broadcast_to(r, (LANES, TOK)).T
        coef[...] = jnp.broadcast_to(c, (LANES, TOK)).T

    @pl.when((t == 0) & (b == 0))
    def _():
        dgain_ref[...] = jnp.zeros_like(dgain_ref)

    gate = gate_ref[...].astype(F32)
    sg = sigmoid(gate)
    act = gate * sg
    scan = scan_ref[...]
    gain = gain_ref[...]
    gated = scan * act
    scaled = gated * rinv[...]
    gin = gin_ref[...]
    inner_ref[...] = (scaled * gain).astype(BF)
    dgated = rinv[...] * (gin * gain - gated * coef[...])
    dscan_ref[...] = dgated * act
    dgate_ref[...] = (dgated * scan * (sg * (1.0 + gate * (1.0 - sg)))).astype(BF)
    here = pl.ds(pl.multiple_of(t * LANES, LANES), LANES)
    dgain_ref[0:1, here] += jnp.sum(gin * scaled, axis=0, keepdims=True)


def params(*semantics):
    return pltpu.CompilerParams(dimension_semantics=semantics, vmem_limit_bytes=VMEM_LIMIT)


def block_scratch(extra):
    base = [
        pltpu.VMEM((3, TOK, LANES), F32),
        pltpu.VMEM((2, Q, Q), F32),
        pltpu.VMEM((TOK, LANES), BF),
        pltpu.VMEM((TOK, LANES), BF),
        pltpu.VMEM((LANES, Q), BF),
    ]
    column = pltpu.VMEM((TOK, LANES), F32)
    rest = [
        column,
        pltpu.VMEM((LANES, TOK), F32),
        pltpu.VMEM((Q, LANES), F32),
        pltpu.VMEM((Q, LANES), F32),
    ]
    if not extra:
        return base + [column] + rest
    return base + [pltpu.VMEM((LANES, Q), BF), column, column] + rest + [
        pltpu.VMEM((2, Q, Q), F32),
        pltpu.VMEM((TOK, 2 * LANES), F32),
        pltpu.VMEM((Q, LANES), F32),
        pltpu.VMEM((Q, LANES), F32),
        pltpu.VMEM((Q, LANES), F32),
    ]


def mixer_specs(tiles):
    return [
        pl.BlockSpec((TOK, LANES), lambda b, t, *_: (b, t)),
        pl.BlockSpec((TOK, 2 * LANES), lambda b, t, *_: (b, tiles // 2)),
        pl.BlockSpec((TOK, LANES), lambda b, t, *_: (b, tiles + 2)),
        pl.BlockSpec((8, LANES), lambda b, t, *_: (0, t)),
        pl.BlockSpec((8, 2 * LANES), lambda b, t, *_: (0, tiles // 2)),
        pl.BlockSpec((8, LANES), lambda b, t, *_: (0, 0)),
        pl.BlockSpec((LANES, LANES), lambda b, t, *_: (0, 0)),
    ]


def scan_forward(bounds, proj, cw, hp, sel, tiles):
    blocks = proj.shape[0] // TOK
    return pl.pallas_call(
        fwd_kernel,
        out_shape=jax.ShapeDtypeStruct((blocks * TOK, tiles * LANES), F32),
        grid_spec=pltpu.PrefetchScalarGridSpec(
            num_scalar_prefetch=1,
            grid=(blocks, tiles),
            in_specs=mixer_specs(tiles),
            out_specs=pl.BlockSpec((TOK, LANES), lambda b, t, *_: (b, t)),
            scratch_shapes=block_scratch(False),
        ),
        compiler_params=params("arbitrary", "arbitrary"),
        cost_estimate=pl.CostEstimate(flops=blocks * 2_000_000_000, bytes_accessed=blocks * 4_000_000, transcendentals=0),
    )(bounds, proj, proj, proj, cw, cw, hp, sel)


def scan_backward(bounds, proj, cw, hp, sel, scan, dscan, tiles):
    blocks = proj.shape[0] // TOK
    width = (tiles + 3) * LANES
    tile = pl.BlockSpec((TOK, LANES), lambda b, t, *_: (b, t))
    return pl.pallas_call(
        bwd_kernel,
        out_shape=(
            jax.ShapeDtypeStruct((blocks * TOK, width), BF),
            jax.ShapeDtypeStruct((8, (tiles + 2) * LANES), F32),
            jax.ShapeDtypeStruct((8, LANES), F32),
        ),
        grid_spec=pltpu.PrefetchScalarGridSpec(
            num_scalar_prefetch=1,
            grid=(blocks, tiles),
            in_specs=mixer_specs(tiles) + [tile, tile],
            out_specs=(
                pl.BlockSpec((TOK, width), lambda b, t, *_: (b, 0)),
                pl.BlockSpec((8, (tiles + 2) * LANES), lambda b, t, *_: (0, 0)),
                pl.BlockSpec((8, LANES), lambda b, t, *_: (0, 0)),
            ),
            scratch_shapes=block_scratch(True),
        ),
        compiler_params=params("arbitrary", "arbitrary"),
        cost_estimate=pl.CostEstimate(flops=blocks * 8_000_000_000, bytes_accessed=blocks * 6_000_000, transcendentals=0),
    )(bounds, proj, proj, proj, cw, cw, hp, sel, scan, dscan)


def gate_stats(place, scan, gate, ginner, gain):
    blocks, tiles = scan.shape[0] // TOK, scan.shape[1] // LANES
    tile = pl.BlockSpec((TOK, LANES), lambda b, t, *_: (b, t))
    return pl.pallas_call(
        stat_kernel,
        out_shape=jax.ShapeDtypeStruct((blocks, 8, TOK), F32),
        grid_spec=pltpu.PrefetchScalarGridSpec(
            num_scalar_prefetch=1,
            grid=(blocks, tiles),
            in_specs=[
                tile,
                tile,
                pl.BlockSpec((TOK, LANES), lambda b, t, place: (b, place[t])),
                pl.BlockSpec((1, LANES), lambda b, t, *_: (0, t)),
            ],
            out_specs=pl.BlockSpec((1, 8, TOK), lambda b, t, *_: (b, 0, 0)),
            scratch_shapes=[pltpu.VMEM((TOK, LANES), F32)] * 2,
        ),
        compiler_params=params("arbitrary", "arbitrary"),
        cost_estimate=pl.CostEstimate(flops=0, bytes_accessed=blocks * 5_000_000, transcendentals=0),
    )(place, scan, gate, ginner, gain)


def gate_both(place, sums, scan, gate, ginner, gain):
    blocks, tiles = scan.shape[0] // TOK, scan.shape[1] // LANES
    tile = pl.BlockSpec((TOK, LANES), lambda b, t, *_: (b, t))
    moved = pl.BlockSpec((TOK, LANES), lambda b, t, place: (b, place[t]))
    rows = blocks * TOK
    return pl.pallas_call(
        gate_kernel,
        out_shape=(
            jax.ShapeDtypeStruct((rows, tiles * LANES), BF),
            jax.ShapeDtypeStruct((rows, tiles * LANES), BF),
            jax.ShapeDtypeStruct((rows, tiles * LANES), F32),
            jax.ShapeDtypeStruct((8, tiles * LANES), F32),
        ),
        grid_spec=pltpu.PrefetchScalarGridSpec(
            num_scalar_prefetch=1,
            grid=(blocks, tiles),
            in_specs=[
                pl.BlockSpec((1, 8, TOK), lambda b, t, *_: (b, 0, 0)),
                tile,
                tile,
                moved,
                pl.BlockSpec((1, LANES), lambda b, t, *_: (0, t)),
            ],
            out_specs=(moved, tile, tile, pl.BlockSpec((8, tiles * LANES), lambda b, t, *_: (0, 0))),
            scratch_shapes=[pltpu.VMEM((TOK, LANES), F32)] * 2,
        ),
        compiler_params=params("arbitrary", "arbitrary"),
        cost_estimate=pl.CostEstimate(flops=0, bytes_accessed=blocks * 9_000_000, transcendentals=0),
    )(place, sums, scan, gate, ginner, gain)


def pick_kernel(table, w_ref, out_ref, *, width):
    t = pl.program_id(0)
    lane = iota(w_ref.shape, 1) + table[t] * LANES
    out_ref[...] = jnp.where(lane < width, w_ref[...], 0.0).astype(BF)


def pick_columns(table, weight, tiles):
    rows = weight.shape[0]
    return pl.pallas_call(
        functools.partial(pick_kernel, width=weight.shape[1]),
        out_shape=jax.ShapeDtypeStruct((rows, tiles * LANES), BF),
        grid_spec=pltpu.PrefetchScalarGridSpec(
            num_scalar_prefetch=1,
            grid=(tiles,),
            in_specs=[pl.BlockSpec((rows, LANES), lambda t, table: (0, table[t]))],
            out_specs=pl.BlockSpec((rows, LANES), lambda t, table: (0, t)),
        ),
        compiler_params=params("arbitrary"),
        cost_estimate=pl.CostEstimate(flops=0, bytes_accessed=rows * tiles * 768, transcendentals=0),
    )(table, weight)


STEP = 128


def norm_kernel(perm, tok_ref, gain_ref, out_ref):
    x = tok_ref[...].astype(F32)
    inv = lax.rsqrt(jnp.mean(x * x, axis=1, keepdims=True) + EPSILON)
    wide = D // 8
    for k in range(8):
        here = pl.ds(pl.multiple_of(perm[k] * wide, wide), wide)
        out_ref[:, k * wide : (k + 1) * wide] = (
            tok_ref[:, here].astype(F32) * inv * gain_ref[:, here]
        ).astype(BF)


def norm_rows(perm, tokens, gain):
    rows = tokens.shape[0]
    row = pl.BlockSpec((STEP, D), lambda i, *_: (i, 0))
    return pl.pallas_call(
        norm_kernel,
        out_shape=jax.ShapeDtypeStruct((rows, D), BF),
        grid_spec=pltpu.PrefetchScalarGridSpec(
            num_scalar_prefetch=1,
            grid=(rows // STEP,),
            in_specs=[row, pl.BlockSpec((1, D), lambda i, *_: (0, 0))],
            out_specs=row,
        ),
        compiler_params=params("arbitrary"),
        cost_estimate=pl.CostEstimate(flops=0, bytes_accessed=rows * D * 4, transcendentals=0),
    )(perm, tokens, gain)


def last_kernel(perm, tok_ref, cot_ref, keep_ref, gain_ref, one_ref, two_ref, three_ref, out_ref, grad):
    wide = D // 8
    for k in range(8):
        here = pl.ds(pl.multiple_of(perm[k] * wide, wide), wide)
        at = slice(k * wide, (k + 1) * wide)
        grad[:, here] = (
            one_ref[:, at].astype(F32) + two_ref[:, at].astype(F32) + three_ref[:, at].astype(F32)
        ) * gain_ref[:, here]
    x = tok_ref[...].astype(F32)
    inv = lax.rsqrt(jnp.mean(x * x, axis=1, keepdims=True) + EPSILON)
    g = grad[...]
    dot = jnp.mean(g * x, axis=1, keepdims=True)
    out_ref[...] = inv * (g - x * (inv * inv * dot)) + keep_ref[...] * cot_ref[...].astype(F32)


def last_rows(perm, tokens, cotangent, keep, gain, parts):
    rows = tokens.shape[0]
    row = pl.BlockSpec((STEP, D), lambda i, *_: (i, 0))
    return pl.pallas_call(
        last_kernel,
        out_shape=jax.ShapeDtypeStruct((rows, D), F32),
        grid_spec=pltpu.PrefetchScalarGridSpec(
            num_scalar_prefetch=1,
            grid=(rows // STEP,),
            in_specs=[
                row,
                row,
                pl.BlockSpec((STEP, 1), lambda i, *_: (i, 0)),
                pl.BlockSpec((1, D), lambda i, *_: (0, 0)),
                row,
                row,
                row,
            ],
            out_specs=row,
            scratch_shapes=[pltpu.VMEM((STEP, D), F32)],
        ),
        compiler_params=params("arbitrary"),
        cost_estimate=pl.CostEstimate(flops=0, bytes_accessed=rows * D * 14, transcendentals=0),
    )(perm, tokens, cotangent, keep, gain, *parts)


def join_kernel(me, *refs, tiles):
    out_ref = refs[-1]
    gates, rests = refs[:4], refs[4:8]
    r = me[0]
    for k in range(4):
        for t in range(tiles):
            at = slice(t * LANES, (t + 1) * LANES)
            owner = jnp.bitwise_xor(r, k)
            here = pl.ds(pl.multiple_of((4 * t + owner) * LANES, LANES), LANES)
            out_ref[:, here] = gates[k][:, at].astype(F32)
            here = pl.ds(pl.multiple_of((4 * (t + tiles) + owner) * LANES, LANES), LANES)
            out_ref[:, here] = rests[k][:, at].astype(F32)
    shared = sum(rests[k][:, tiles * LANES :].astype(F32) for k in range(4))
    base = 8 * tiles * LANES
    out_ref[:, base:] = shared[:, : out_ref.shape[1] - base]


def join_columns(me, gates, rests, width):
    rows = gates[0].shape[0]
    step = min(rows, 64)
    tiles = gates[0].shape[1] // LANES
    spec = lambda a: pl.BlockSpec((step, a.shape[1]), lambda i, *_: (i, 0))
    return pl.pallas_call(
        functools.partial(join_kernel, tiles=tiles),
        out_shape=jax.ShapeDtypeStruct((rows, width), F32),
        grid_spec=pltpu.PrefetchScalarGridSpec(
            num_scalar_prefetch=1,
            grid=(rows // step,),
            in_specs=[spec(a) for a in gates + rests],
            out_specs=pl.BlockSpec((step, width), lambda i, *_: (i, 0)),
        ),
        compiler_params=params("arbitrary"),
        cost_estimate=pl.CostEstimate(flops=0, bytes_accessed=rows * width * 6, transcendentals=0),
    )(me, *gates, *rests)


def swap(x, d):
    return lax.ppermute(x, "rep", [(i, i ^ d) for i in range(4)])


def share_rep(x):
    core, chip = swap(x, 1), swap(x, 2)
    return [x, core, chip, swap(chip, 1)]


def scatter_rep(parts):
    far = swap(parts[3].astype(BF), 1)
    chip = swap((parts[2].astype(F32) + far.astype(F32)).astype(BF), 2)
    return [parts[0], swap(parts[1].astype(BF), 1), chip]


FORWARD = [(RING[i], RING[(i + 1) % 8]) for i in range(8)]
BACKWARD = [(b, a) for a, b in FORWARD]


def relative(s, n):
    if n != 8:
        return jnp.arange(8, dtype=jnp.int32), jnp.arange(8, dtype=jnp.int32)
    table, inverse = [], []
    for shard in range(8):
        p = RING.index(shard)
        row = [RING[(p + d) % 8] for d in (0, -1, 1, -2, 2, -3, 3, 4)]
        table.append(row)
        inverse.append([row.index(i) for i in range(8)])
    return jnp.asarray(table, jnp.int32)[s], jnp.asarray(inverse, jnp.int32)[s]


def ring_gather(x):
    fw = lambda v: lax.ppermute(v, "shard", FORWARD)
    bw = lambda v: lax.ppermute(v, "shard", BACKWARD)
    pieces, a, b = [x], x, x
    for _ in range(3):
        a, b = fw(a), bw(b)
        pieces += [a, b]
    half = x.shape[0] // 2
    return pieces + [fw(a[:half]), bw(b[half:])]


def ring_scatter(parts):
    fw = lambda v: lax.ppermute(v.astype(BF), "shard", FORWARD).astype(F32)
    bw = lambda v: lax.ppermute(v.astype(BF), "shard", BACKWARD).astype(F32)
    own, f1, b1, f2, b2, f3, b3, far = parts
    half = far.shape[0] // 2
    rf, rb = fw(far[:half]), bw(far[half:])
    sf = jnp.concatenate([b3[:half] + rf, b3[half:]], 0)
    sb = jnp.concatenate([f3[:half], f3[half:] + rb], 0)
    for forward, backward in ((b2, f2), (b1, f1)):
        rf, rb = fw(sf), bw(sb)
        sf, sb = forward + rf, backward + rb
    return own + fw(sf) + bw(sb)


def gather_rows(x, n):
    if n == 8:
        return jnp.concatenate(ring_gather(x), 0)
    return lax.all_gather(x, "shard", axis=0, tiled=True)


def scatter_rows(total, n):
    if n == 8:
        rows = total.shape[0] // 8
        return ring_scatter([total[k * rows : (k + 1) * rows] for k in range(8)])
    return lax.psum_scatter(total, "shard", scatter_dimension=0, tiled=True)


def shards(n, tokens, cotangent, lengths, order, mask, in_weight, out_weight, conv_weight, conv_bias, dt_bias,
           a_log, skip_gain, gain_outer, gain_inner):
    r, s = lax.axis_index("rep"), lax.axis_index("shard")
    tiles = DIN // LANES // 4
    perm, place = relative(s, n)
    keep = mask.astype(F32)[:, None]
    catalog = jnp.arange(lengths.shape[0], dtype=jnp.int32)
    picked = jnp.sum(jnp.where(order[:, None] == catalog[None, :], lengths[None, :], 0), axis=1)
    bounds = jnp.stack([picked[0], picked[0] + picked[1]])[None, :]
    bounds = jnp.concatenate([bounds, swap(bounds, 1), swap(bounds, 2), swap(bounds, 3)], 0)

    mine = jnp.arange(tiles, dtype=jnp.int32) * 4 + r
    shared = jnp.arange(3, dtype=jnp.int32) + 8 * tiles
    rest_table = jnp.concatenate([mine + 4 * tiles, shared])
    w_rest = gather_rows(pick_columns(rest_table, in_weight, tiles + 3), n)
    normed = norm_rows(perm, tokens, gain_outer[None, :])
    normed = jnp.concatenate(share_rep(normed), 0)
    w_gate = gather_rows(pick_columns(mine, in_weight, tiles), n)
    gout = (cotangent.astype(F32) * keep).astype(BF)
    gout = jnp.concatenate(share_rep(gout), 0)
    if n == 8:
        own_rows = lax.dynamic_slice_in_dim(out_weight, r * LANES, LANES, 0).astype(BF)
        w_out = gather_rows(own_rows, n)
    else:
        w_out = lax.all_gather(out_weight.astype(BF), "shard", axis=0, tiled=True)
        w_out = lax.dynamic_index_in_dim(w_out.reshape(tiles, 4, LANES, D), r, 1, False).reshape(tiles * LANES, D)

    def own_lanes(v, width):
        v = lax.dynamic_index_in_dim(v.reshape(v.shape[:-1] + (tiles, 4, width)), r, v.ndim, False)
        return v.reshape(v.shape[:-2] + (tiles * width,))

    heads = H // 4
    rows8 = jnp.concatenate(
        [conv_weight, conv_bias[None], jnp.pad(jnp.broadcast_to(skip_gain[:, None], (H, P_SIZE)).reshape(1, DIN), ((0, 0), (0, 2 * N))),
         jnp.zeros((2, CONVCH), F32)], 0)
    cw = jnp.concatenate([own_lanes(rows8[:, :DIN], LANES), rows8[:, DIN:]], 1)
    hp = jnp.stack([own_lanes(dt_bias, 2), own_lanes(-jnp.exp(a_log), 2)])
    hp = jnp.pad(hp, ((0, 6), (0, LANES - heads)))
    lane = jnp.arange(LANES, dtype=jnp.int32)
    head = 8 * (lane // 2) + 2 * r + lane % 2
    sel = ((lane[:, None] == head[None, :]) & (lane[None, :] < heads)).astype(BF)
    gain = own_lanes(gain_inner, LANES)[None, :]

    proj = mm(normed, w_rest).astype(BF)
    scan = scan_forward(bounds, proj, cw, hp, sel, tiles)
    gate = mm(normed, w_gate).astype(BF)
    ginner = mm_nt(gout, w_out)
    sums = gate_stats(place, scan, gate, ginner, gain)
    there = [swap(sums, d) for d in (1, 2, 3)]
    sums = jnp.stack([sums[k] + there[0][k ^ 1] + there[1][k ^ 2] + there[2][k ^ 3] for k in range(4)])
    inner, dgate, dscan, dgain = gate_both(place, sums, scan, gate, ginner, gain)
    branch = mm(inner, w_out)
    branch = scatter_rep([branch[k * TOK : (k + 1) * TOK] for k in range(4)])
    branch = sum(p.astype(F32) for p in branch)
    layer_out = (keep * (tokens.astype(F32) + branch)).astype(BF)

    share_out = lax.dot_general(inner, gout, TN, preferred_element_type=F32)
    if n == 8:
        share_out = scatter_rows(share_out, n)
        pieces = share_rep(share_out.astype(BF))
        ordered = jnp.stack(pieces)
        grad_out_weight = jnp.concatenate(
            [lax.dynamic_index_in_dim(ordered, jnp.bitwise_xor(r, q), 0, False) for q in range(4)], 0
        ).astype(F32)
    else:
        spread = share_out.reshape(tiles, 1, LANES, D) * (jnp.arange(4)[None, :, None, None] == r)
        share_out = lax.psum_scatter(spread.reshape(DIN, D), "shard", scatter_dimension=0, tiled=True)
        grad_out_weight = lax.psum(share_out, "rep")
    share_gate = scatter_rows(lax.dot_general(normed, dgate, TN, preferred_element_type=F32), n)
    gates = share_rep(share_gate.astype(BF))
    gproj, dcw, dhp = scan_backward(bounds, proj, cw, hp, sel, scan, dscan, tiles)
    share_rest = scatter_rows(lax.dot_general(normed, gproj, TN, preferred_element_type=F32), n)
    rests = share_rep(share_rest.astype(BF))
    grad_in_weight = join_columns(r[None], gates, rests, in_weight.shape[1])
    gnormed = mm_nt(gproj, w_rest) + mm_nt(dgate, w_gate)
    dgo = jnp.sum(gnormed * normed.astype(F32), axis=0).reshape(8, D // 8)[place].reshape(D) / gain_outer
    gnormed = gnormed.astype(BF)
    parts = scatter_rep([gnormed[k * TOK : (k + 1) * TOK] for k in range(4)])
    grad_tokens = last_rows(perm, tokens, cotangent, keep, gain_outer[None, :], parts)

    at_r = (jnp.arange(4) == r).astype(F32)

    def all_lanes(v, width):
        v = v.reshape(v.shape[:-1] + (tiles, 1, width)) * at_r[:, None]
        return v.reshape(v.shape[:-3] + (tiles * 4 * width,))

    wide = jnp.concatenate([all_lanes(dcw[:5, : tiles * LANES], LANES), dcw[:5, tiles * LANES :]], 1)
    dskip = jnp.sum(dcw[5, : tiles * LANES].reshape(heads, P_SIZE), axis=1)
    small = [
        wide[:4].reshape(-1),
        wide[4],
        all_lanes(dhp[0, :heads], 2),
        all_lanes(dhp[1, :heads], 2),
        all_lanes(dskip, 2),
        dgo,
        all_lanes(dgain[0], LANES),
    ]
    sizes = [v.shape[0] for v in small]
    small = lax.psum(jnp.concatenate(small), ("rep", "shard"))
    ends = [sum(sizes[: i + 1]) for i in range(len(sizes))]
    g_cw, g_cb, g_db, g_al, g_sk, g_go, g_gi = [small[e - z : e] for e, z in zip(ends, sizes)]
    return (
        layer_out,
        grad_tokens,
        grad_in_weight,
        grad_out_weight,
        g_cw.reshape(4, CONVCH),
        g_cb,
        g_db,
        g_al,
        g_sk,
        g_go,
        g_gi,
    )


def solution(mesh):
    rows = P(("rep", "shard"), None)
    vector = P(("rep", "shard"))
    owned = P("shard", None)
    return jax.shard_map(
        functools.partial(shards, mesh.shape["shard"]),
        mesh=mesh,
        in_specs=(rows, rows, P(), vector, vector, owned, owned) + (P(),) * 7,
        out_specs=(rows, rows, owned, owned) + (P(),) * 7,
        check_vma=False,
    )
```

time: 3250 us -> 893 us (0.27)
  waiting for transfers between devices: 2010 us -> 319 us
  local copies, waits for them, and re-layouts: 549 us -> 80.5 us
  matrix products: 376 us -> 153 us
  Pallas kernels: 0 us -> 191 us
  other arithmetic: 193 us -> 43.5 us
  starting transfers between devices: 0.25 us -> 81 us
  blocking collectives: 40.7 us -> 0 us
    reduce_scatter x2 -> x0, waiting for transfers between devices: 1100 us -> none  [the longest x1 1100 us: shards(): lax.psum_scatter(term_rows(normed16, gproj), 'shard', scatter_dimension=0...]
    all_gather x2 -> x0, waiting for transfers between devices: 657 us -> none  [the longest x1 657 us: shards(): lax.all_gather(w_in16, 'shard', axis=0, tiled=True)]
    dynamic_update_slice x12 -> x0, local copies, waits for them, and re-layouts: 376 us -> none  [mixer(): lax.scan(jax.checkpoint(block_step), jnp.zeros((H, P_SIZE, N), jnp.float3...]
    dot_general x34 -> x9, matrix products: 376 us -> 153 us  [the longest x3 59.2 us: mm_nt(): return lax.dot_general(a, b, NT, preferred_element_type=F32)]
    ppermute x0 -> x75, waiting for transfers between devices: none -> 199 us  [the longest x12 57.2 us: ring_gather(): fw = lambda v: lax.ppermute(v, 'shard', FORWARD)]
    pallas_call x0 -> x9, Pallas kernels: none -> 191 us  [the longest x1 75.8 us: scan_backward(): pl.pallas_call(bwd_kernel, out_shape=(jax.ShapeDtypeStruct((blocks * TOK,...]
    psum x2 -> x1, waiting for transfers between devices: 259 us -> 119 us  [shards(): small = lax.psum(jnp.concatenate(small), ('rep', 'shard'))]
    reduce_sum x14 -> x2, other arithmetic: 92.1 us -> 0.3 us  [the longest x1 0.18 us: shards(): jnp.sum(jnp.where(order[:, None] == catalog[None, :], lengths[None, :], 0...]
  transfers between devices with their start and end apart: 6 -> 76, of which waited for: 4 -> 31; matrix products, arithmetic and copies ran while one was open for 34% -> 22% of each run, Pallas kernels for 0% -> 7%
where the time goes in v1:
time: 893 us; the launch traced here: 885 us
  waiting for transfers between devices  319 us (36%)
  Pallas kernels  191 us (21%)
  matrix products  153 us (17%)
  starting transfers between devices  81 us (9%)
  local copies, waits for them, and re-layouts  80.5 us (9%)
  other arithmetic  43.5 us (5%)
  between operations  16.8 us (2%)
    psum x1, waiting for transfers between devices, shards(): small = lax.psum(jnp.concatenate(small), ('rep', 'shard'))  119 us
    pallas_call x1, Pallas kernels, scan_backward(): pl.pallas_call(bwd_kernel, out_shape=(jax.ShapeDtypeStruct((blocks * TOK,...  75.8 us
    dot_general x3, matrix products, mm_nt(): return lax.dot_general(a, b, NT, preferred_element_type=F32)  59.2 us
    ppermute x12, waiting for transfers between devices, ring_gather(): fw = lambda v: lax.ppermute(v, 'shard', FORWARD)  57.2 us
    ppermute x12, waiting for transfers between devices, ring_scatter(): fw = lambda v: lax.ppermute(v.astype(BF), 'shard', FORWARD).astype(F32)  53.4 us
    ppermute x12, waiting for transfers between devices, ring_scatter(): bw = lambda v: lax.ppermute(v.astype(BF), 'shard', BACKWARD).astype(F32)  50.1 us
    unnamed x135, local copies, waits for them, and re-layouts  47.1 us
    dot_general x3, matrix products, mm(): return jnp.dot(a, b, preferred_element_type=F32)  44.7 us
  transfers between devices with their start and end apart: 76, of which 31 were waited for; matrix products, arithmetic and copies ran while one was open for 22% of the time, Pallas kernels for 7%

profile of v1, /device:TPU:0, one launch (start us, length us, event | category | flops | bytes accessed | tf_op | source)
XLA Modules:
  0.0 884.9 jit_solution(1499644663674760405)
XLA Ops:
  93.1 11.8 %collective-permute-done.8 = bf16[256,1408]{1,0:T(8,128)(2,1)S(1)} collective-permute-done((bf16[256,1408]{1,0:T(8,128)(2,1)}, bf16[256,1408]{1,0:T(8,128)(2,1)S(1)}, u32[]{:S(2)}, u32[]{:S(2)}) %collective-permute-start.8) | collective-permute-done | bytes 720928 | tf_op jit(solution)/shard_map/ppermute | solution.py:654
  144.7 12.4 %collective-permute-done.10 = bf16[256,1408]{1,0:T(8,128)(2,1)S(1)} collective-permute-done((bf16[256,1408]{1,0:T(8,128)(2,1)S(1)}, bf16[256,1408]{1,0:T(8,128)(2,1)S(1)}, u32[]{:S(2)}, u32[]{:S(2)}) %collective-permute-start.10) | collective-permute-done | bytes 720928 | tf_op jit(solution)/shard_map/ppermute | solution.py:654
  169.3 19.0 %convolution_convert_fusion.xs_ref.bc_ref.dt_ref = bf16[2048,1408]{1,0:T(8,128)(2,1)S(1)} fusion(bf16[2048,1408]{1,0:T(8,128)(2,1)} %constant_dynamic-update-slice_fusion, bf16[512,2048]{1,0:T(8,128)(2,1)} %collective-permute-done.5, bf16[512,2048]{1,0:T(8,128)(2,1)} %copy-done.43, bf16[512,2048]{1,0:T(8,128)(2,1)} %copy-done.45, ...), kind=kOutput, calls=%fused_computation.5 | convolution fusion | flops 11847598080 | bytes 19922944 | tf_op jit(solution)/shard_map/dot_general | solution.py:31
  188.4 44.1 %shard_map.241.scan_ref = f32[2048,1024]{1,0:T(8,128)} custom-call(s32[4,2]{1,0:T(4,128)S(1)} %pad_add_fusion.bnd, bf16[2048,1408]{1,0:T(8,128)(2,1)S(1)} %convolution_convert_fusion.xs_ref.bc_ref.dt_ref, bf16[2048,1408]{1,0:T(8,128)(2,1)S(1)} %convolution_convert_fusion.xs_ref.bc_ref.dt_ref, ...), custom_call_target="tpu_custom_call" | custom-call | flops 8000000000 | bytes 16000000 | tf_op jit(solution)/shard_map/pallas_call | solution.py:396
  234.9 12.7 %convolution_convert_fusion.1.gate_ref = bf16[2048,1024]{1,0:T(8,128)(2,1)S(1)} fusion(bf16[2048,1024]{1,0:T(8,128)(2,1)S(1)} %copy-done.31, bf16[512,2048]{1,0:T(8,128)(2,1)} %collective-permute-done.5, bf16[512,2048]{1,0:T(8,128)(2,1)} %copy-done.43, bf16[512,2048]{1,0:T(8,128)(2,1)} %copy-done.45, bf16[512,2048]{1,0:T(8,128)(2,1)S(1)} %shard_map.239), kind=kOutput, calls=%fused_computation.15 | convolution fusion | flops 8625586176 | bytes 16777216 | tf_op jit(solution)/shard_map/dot_general | solution.py:31
  247.7 17.9 %fusion.12.gin_ref = f32[2048,1024]{1,0:T(8,128)} fusion(bf16[1024,2048]{1,0:T(8,128)(2,1)} %constant_dynamic-update-slice_fusion.18, bf16[512,2048]{1,0:T(8,128)(2,1)} %collective-permute-done.24, bf16[512,2048]{1,0:T(8,128)(2,1)} %collective-permute-done.23, bf16[512,2048]{1,0:T(8,128)(2,1)} %collective-permute-done.22, ...), kind=kOutput, calls=%fused_computation.30 | convolution fusion | flops 8623489024 | bytes 20971520 | tf_op jit(solution)/shard_map/dot_general | solution.py:35
  265.6 20.8 %shard_map.243 = f32[4,8,512]{2,1,0:T(8,128)S(1)} custom-call(s32[8]{0:T(128)S(1)} %fusion.43.place, f32[2048,1024]{1,0:T(8,128)} %shard_map.241.scan_ref, bf16[2048,1024]{1,0:T(8,128)(2,1)S(1)} %convolution_convert_fusion.1.gate_ref, f32[2048,1024]{1,0:T(8,128)} %fusion.12.gin_ref, f32[1,1024]{1,0:T(1,128)S(1)} %dynamic-slice_bitcast_fusion.5.gain_ref), custom_call_target="tpu_custom_call" | custom-call | bytes 20000000 | tf_op jit(solution)/shard_map/pallas_call | solution.py:441
  294.9 27.3 %shard_map.244 = (bf16[2048,1024]{1,0:T(8,128)(2,1)S(1)}, bf16[2048,1024]{1,0:T(8,128)(2,1)}, f32[2048,1024]{1,0:T(8,128)}, f32[8,1024]{1,0:T(8,128)S(1)}) custom-call(s32[8]{0:T(128)S(1)} %fusion.43.place, f32[4,8,512]{2,1,0:T(8,128)S(1)} %pad_maximum_fusion.11.sum_ref, f32[2048,1024]{1,0:T(8,128)} %shard_map.241.scan_ref, bf16[2048,1024]{1,0:T(8,128)(2,1)} %copy-done.4, ...), custom_call_target="tpu_custom_call" | custom-call | bytes 36000000 | tf_op jit(solution)/shard_map/pallas_call | solution.py:466
  324.2 75.8 %shard_map.245 = (bf16[2048,1408]{1,0:T(8,128)(2,1)S(1)}, f32[8,1280]{1,0:T(8,128)S(1)}, f32[8,128]{1,0:T(8,128)S(1)}) custom-call(s32[4,2]{1,0:T(4,128)S(1)} %pad_add_fusion.bnd, bf16[2048,1408]{1,0:T(8,128)(2,1)} %copy-done.13, bf16[2048,1408]{1,0:T(8,128)(2,1)} %copy-done.13, bf16[2048,1408]{1,0:T(8,128)(2,1)} %copy-done.13, ...), custom_call_target="tpu_custom_call" | custom-call | flops 32000000000 | bytes 24000000 | tf_op jit(solution)/shard_map/pallas_call | solution.py:415
  404.5 15.7 %fusion.59 = f32[2048,2048]{1,0:T(8,128)} fusion(bf16[2048,1024]{1,0:T(8,128)(2,1)} %get-tuple-element.21, bf16[2048,1024]{1,0:T(8,128)(2,1)} %copy-done.30), kind=kOutput, calls=%fused_computation.187 | convolution fusion | flops 8589934592 | bytes 25165824 | tf_op jit(solution)/shard_map/dot_general | solution.py:35
  420.2 12.9 %fusion.55 = (bf16[2048,2048]{1,0:T(8,128)(2,1)}, f32[2048,2048]{1,0:T(8,128)}) fusion(bf16[2048,1024]{1,0:T(8,128)(2,1)S(1)} %copy-done.12, bf16[1024,2048]{1,0:T(8,128)(2,1)S(1)} %copy-done.29), kind=kOutput, calls=%fused_computation.183 | convolution fusion | flops 8594128896 | bytes 33554432 | tf_op jit(solution)/shard_map/dot_general | solution.py:31
  433.2 13.4 %fusion.58 = (bf16[1024,2048]{1,0:T(8,128)(2,1)S(1)}, f32[1024,2048]{1,0:T(8,128)}) fusion(bf16[2048,1024]{1,0:T(8,128)(2,1)S(1)} %copy-done.12, bf16[512,2048]{1,0:T(8,128)(2,1)} %collective-permute-done.24, bf16[512,2048]{1,0:T(8,128)(2,1)} %collective-permute-done.23, bf16[512,2048]{1,0:T(8,128)(2,1)} %collective-permute-done.22, ...), kind=kOutput, calls=%fused_computation.186 | convolution fusion | flops 8625586176 | bytes 25165824 | tf_op jit(solution)/shard_map/dot_general | solution.py:747
  449.7 20.8 %fusion.57 = (bf16[2048,1408]{1,0:T(8,128)(2,1)}, f32[2048,1408]{1,0:T(8,128)}) fusion(bf16[2048,1408]{1,0:T(8,128)(2,1)} %copy-done.14, bf16[512,2048]{1,0:T(8,128)(2,1)} %collective-permute-done.5, bf16[512,2048]{1,0:T(8,128)(2,1)} %copy-done.43, bf16[512,2048]{1,0:T(8,128)(2,1)} %copy-done.45, bf16[512,2048]{1,0:T(8,128)(2,1)S(1)} %shard_map.239), kind=kOutput, calls=%fused_computation.185 | convolution fusion | flops 11847598080 | bytes 31457280 | tf_op jit(solution)/shard_map/dot_general | solution.py:762
  473.2 14.9 %fusion.56 = (bf16[2048,1024]{1,0:T(8,128)(2,1)}, f32[2048,1024]{1,0:T(8,128)}) fusion(bf16[2048,1024]{1,0:T(8,128)(2,1)} %get-tuple-element.21, bf16[512,2048]{1,0:T(8,128)(2,1)} %collective-permute-done.5, bf16[512,2048]{1,0:T(8,128)(2,1)S(1)} %copy-done.44, bf16[512,2048]{1,0:T(8,128)(2,1)} %copy-done.45, bf16[512,2048]{1,0:T(8,128)(2,1)S(1)} %shard_map.239), kind=kOutput, calls=%fused_computation.184 | convolution fusion | flops 8625586176 | bytes 25165824 | tf_op jit(solution)/shard_map/dot_general | solution.py:759
  490.6 25.6 %multiply_reduce_fusion = (f32[2048]{0:T(1024)}, bf16[2048,2048]{1,0:T(8,128)(2,1)}) fusion(bf16[512,2048]{1,0:T(8,128)(2,1)} %collective-permute-done.5, bf16[512,2048]{1,0:T(8,128)(2,1)S(1)} %copy-done.44, bf16[512,2048]{1,0:T(8,128)(2,1)} %copy-done.45, bf16[512,2048]{1,0:T(8,128)(2,1)S(1)} %shard_map.239, f32[2048,2048]{1,0:T(8,128)} %fusion.59, ...), kind=kOutput, calls=%fused_computation.1 | convolution fusion | flops 11861489664 | bytes 45096960 | tf_op jit(solution)/shard_map/dot_general | solution.py:35
  533.8 11.3 %collective-permute-done.46 = bf16[128,1024]{1,0:T(8,128)(2,1)S(1)} collective-permute-done((bf16[128,1024]{1,0:T(8,128)(2,1)}, bf16[128,1024]{1,0:T(8,128)(2,1)S(1)}, u32[]{:S(2)}, u32[]{:S(2)}) %collective-permute-start.46) | collective-permute-done | bytes 262176 | tf_op jit(solution)/shard_map/ppermute | solution.py:666
  554.0 14.2 %collective-permute-done.43 = bf16[256,1024]{1,0:T(8,128)(2,1)S(1)} collective-permute-done((bf16[256,1024]{1,0:T(8,128)(2,1)S(1)}, bf16[256,1024]{1,0:T(8,128)(2,1)S(1)}, u32[]{:S(2)}, u32[]{:S(2)}) %collective-permute-start.43) | collective-permute-done | bytes 524320 | tf_op jit(solution)/shard_map/ppermute | solution.py:665
  571.8 12.6 %collective-permute-done.54 = bf16[256,1408]{1,0:T(8,128)(2,1)S(1)} collective-permute-done((bf16[256,1408]{1,0:T(8,128)(2,1)S(1)}, bf16[256,1408]{1,0:T(8,128)(2,1)S(1)}, u32[]{:S(2)}, u32[]{:S(2)}) %collective-permute-start.54) | collective-permute-done | bytes 720928 | tf_op jit(solution)/shard_map/ppermute | solution.py:665
  589.4 9.8 %collective-permute-done.66 = bf16[128,2048]{1,0:T(8,128)(2,1)S(1)} collective-permute-done((bf16[128,2048]{1,0:T(8,128)(2,1)S(1)}, bf16[128,2048]{1,0:T(8,128)(2,1)S(1)}, u32[]{:S(2)}, u32[]{:S(2)}) %collective-permute-start.66) | collective-permute-done | bytes 524320 | tf_op jit(solution)/shard_map/ppermute | solution.py:665
  623.8 14.4 %collective-permute-done.48 = bf16[256,1024]{1,0:T(8,128)(2,1)S(1)} collective-permute-done((bf16[256,1024]{1,0:T(8,128)(2,1)S(1)}, bf16[256,1024]{1,0:T(8,128)(2,1)S(1)}, u32[]{:S(2)}, u32[]{:S(2)}) %collective-permute-start.48) | collective-permute-done | bytes 524320 | tf_op jit(solution)/shard_map/ppermute | solution.py:666
  654.8 16.8 %collective-permute-done.71 = bf16[128,2048]{1,0:T(8,128)(2,1)S(1)} collective-permute-done((bf16[128,2048]{1,0:T(8,128)(2,1)S(1)}, bf16[128,2048]{1,0:T(8,128)(2,1)S(1)}, u32[]{:S(2)}, u32[]{:S(2)}) %collective-permute-start.71) | collective-permute-done | bytes 524320 | tf_op jit(solution)/shard_map/ppermute | solution.py:666
  689.4 119.5 %all-reduce.4.cloned.1.call-done = f32[28096]{0:T(1024)} async-done(((f32[28096]{0:T(1024)}), f32[28096]{0:T(1024)}) %all-reduce.4.cloned.1.call-update) | async-done | bytes 112400 | tf_op jit(solution)/shard_map/psum | solution.py:789
  826.0 24.0 %collective-permute-done.51.refs_2_ = bf16[256,1024]{1,0:T(8,128)(2,1)S(1)} collective-permute-done((bf16[256,1024]{1,0:T(8,128)(2,1)S(1)}, bf16[256,1024]{1,0:T(8,128)(2,1)S(1)}, u32[]{:S(2)}, u32[]{:S(2)}) %collective-permute-start.51) | collective-permute-done | bytes 524320 | tf_op jit(solution)/shard_map/ppermute | solution.py:623
  868.6 9.2 %copy.37 = f32[256,8512]{0,1:T(8,128)} copy(f32[256,8512]{1,0:T(8,128)} %shard_map.247) | data formatting | bytes 17432576
  (396 shorter events, 291.2 us)
Async XLA Ops:
  7.2 801.7 %all-reduce.4.cloned.1.call-start = ((), (), s32[]{:S(2)}) async-start(), calls=%async_computation | async-start | bytes 229376 | tf_op jit(solution)/shard_map/psum | solution.py:789
  9.6 44.8 %collective-permute-start.25 = (bf16[128,2048]{1,0:T(8,128)(2,1)}, bf16[128,2048]{1,0:T(8,128)(2,1)}, u32[]{:S(2)}, u32[]{:S(2)}) collective-permute-start(bf16[128,2048]{1,0:T(8,128)(2,1)} %get-tuple-element.61), channel_id=1, source_target_pairs={{0,2},{2,4},{4,6},{6,7},{7,5},{5,3},{3,1},{1,0},{8,10},{10,12},{12... | collective-permute-start | bytes 1572872 | tf_op jit(solution)/shard_map/ppermute | solution.py:654
  12.6 41.8 %collective-permute-start.26 = (bf16[128,2048]{1,0:T(8,128)(2,1)}, bf16[128,2048]{1,0:T(8,128)(2,1)}, u32[]{:S(2)}, u32[]{:S(2)}) collective-permute-start(bf16[128,2048]{1,0:T(8,128)(2,1)} %get-tuple-element.61), channel_id=1, source_target_pairs={{2,0},{4,2},{6,4},{7,6},{5,7},{3,5},{1,3},{0,1},{10,8},{12,10},{14... | collective-permute-start | bytes 1572872 | tf_op jit(solution)/shard_map/ppermute | solution.py:655
  28.2 42.5 %collective-permute-start.6 = (bf16[256,1408]{1,0:T(8,128)(2,1)S(1)}, bf16[256,1408]{1,0:T(8,128)(2,1)}, u32[]{:S(2)}, u32[]{:S(2)}) collective-permute-start(bf16[256,1408]{1,0:T(8,128)(2,1)S(1)} %shard_map.240), channel_id=1, source_target_pairs={{0,2},{2,4},{4,6},{6,7},{7,5},{5,3},{3,1},{1,0},{8,10},{10,12},{12... | collective-permute-start | bytes 2162696 | tf_op jit(solution)/shard_map/ppermute | solution.py:654
  30.3 41.0 %collective-permute-start.7 = (bf16[256,1408]{1,0:T(8,128)(2,1)S(1)}, bf16[256,1408]{1,0:T(8,128)(2,1)}, u32[]{:S(2)}, u32[]{:S(2)}) collective-permute-start(bf16[256,1408]{1,0:T(8,128)(2,1)S(1)} %shard_map.240), channel_id=1, source_target_pairs={{2,0},{4,2},{6,4},{7,6},{5,7},{3,5},{1,3},{0,1},{10,8},{12,10},{14... | collective-permute-start | bytes 2162696 | tf_op jit(solution)/shard_map/ppermute | solution.py:655
  67.1 69.2 %collective-permute-start.4 = (bf16[512,2048]{1,0:T(8,128)(2,1)S(1)}, bf16[512,2048]{1,0:T(8,128)(2,1)S(1)}, u32[]{:S(2)}, u32[]{:S(2)}) collective-permute-start(bf16[512,2048]{1,0:T(8,128)(2,1)S(1)} %shard_map.239), channel_id=1, source_target_pairs={{0,16},{8,24},{16,0},{24,8},{1,17},{9,25},{17,1},{25,9},{2,18},{10... | collective-permute-start | bytes 6291464 | tf_op jit(solution)/shard_map/ppermute | solution.py:623
  119.2 45.5 %collective-permute-start.23 = (bf16[512,2048]{1,0:T(8,128)(2,1)}, bf16[512,2048]{1,0:T(8,128)(2,1)}, u32[]{:S(2)}, u32[]{:S(2)}) collective-permute-start(bf16[512,2048]{1,0:T(8,128)(2,1)} %multiply_convert_fusion), channel_id=1, source_target_pairs={{0,16},{8,24},{16,0},{24,8},{1,17},{9,25},{17,1},{25,9},{2,18},{10... | collective-permute-start | bytes 6291464 | tf_op jit(solution)/shard_map/ppermute | solution.py:623
  130.4 37.5 %collective-permute-start.3 = (bf16[512,2048]{1,0:T(8,128)(2,1)S(1)}, bf16[512,2048]{1,0:T(8,128)(2,1)S(1)}, u32[]{:S(2)}, u32[]{:S(2)}) collective-permute-start(bf16[512,2048]{1,0:T(8,128)(2,1)S(1)} %shard_map.239), channel_id=1, source_target_pairs={{0,8},{8,0},{16,24},{24,16},{1,9},{9,1},{17,25},{25,17},{2,10},{10... | collective-permute-start | bytes 6291464 | tf_op jit(solution)/shard_map/ppermute | solution.py:623
  164.8 82.9 %collective-permute-start.22 = (bf16[512,2048]{1,0:T(8,128)(2,1)}, bf16[512,2048]{1,0:T(8,128)(2,1)}, u32[]{:S(2)}, u32[]{:S(2)}) collective-permute-start(bf16[512,2048]{1,0:T(8,128)(2,1)} %multiply_convert_fusion), channel_id=1, source_target_pairs={{0,8},{8,0},{16,24},{24,16},{1,9},{9,1},{17,25},{25,17},{2,10},{10... | collective-permute-start | bytes 6291464 | tf_op jit(solution)/shard_map/ppermute | solution.py:623
  165.5 82.2 %collective-permute-start.24 = (bf16[512,2048]{1,0:T(8,128)(2,1)}, bf16[512,2048]{1,0:T(8,128)(2,1)}, u32[]{:S(2)}, u32[]{:S(2)}) collective-permute-start(bf16[512,2048]{1,0:T(8,128)(2,1)} %collective-permute-done.23), channel_id=1, source_target_pairs={{0,8},{8,0},{16,24},{24,16},{1,9},{9,1},{17,25},{25,17},{2,10},{10... | collective-permute-start | bytes 6291464 | tf_op jit(solution)/shard_map/ppermute | solution.py:623
  447.6 82.0 %collective-permute-start.64 = (bf16[64,2048]{1,0:T(8,128)(2,1)}, bf16[64,2048]{1,0:T(8,128)(2,1)}, u32[]{:S(2)}, u32[]{:S(2)}) collective-permute-start(bf16[64,2048]{1,0:T(8,128)(2,1)} %get-tuple-element.85), channel_id=1, source_target_pairs={{0,2},{2,4},{4,6},{6,7},{7,5},{5,3},{3,1},{1,0},{8,10},{10,12},{12... | collective-permute-start | bytes 786440 | tf_op jit(solution)/shard_map/ppermute | solution.py:665
  447.9 83.3 %collective-permute-start.68 = (bf16[64,2048]{1,0:T(8,128)(2,1)}, bf16[64,2048]{1,0:T(8,128)(2,1)}, u32[]{:S(2)}, u32[]{:S(2)}) collective-permute-start(bf16[64,2048]{1,0:T(8,128)(2,1)} %get-tuple-element.86), channel_id=1, source_target_pairs={{2,0},{4,2},{6,4},{7,6},{5,7},{3,5},{1,3},{0,1},{10,8},{12,10},{14... | collective-permute-start | bytes 786440 | tf_op jit(solution)/shard_map/ppermute | solution.py:666
  472.9 77.3 %collective-permute-start.53 = (bf16[128,1408]{1,0:T(8,128)(2,1)}, bf16[128,1408]{1,0:T(8,128)(2,1)}, u32[]{:S(2)}, u32[]{:S(2)}) collective-permute-start(bf16[128,1408]{1,0:T(8,128)(2,1)} %get-tuple-element.81), channel_id=1, source_target_pairs={{0,2},{2,4},{4,6},{6,7},{7,5},{5,3},{3,1},{1,0},{8,10},{10,12},{12... | collective-permute-start | bytes 1081352 | tf_op jit(solution)/shard_map/ppermute | solution.py:665
  490.2 42.7 %collective-permute-start.42 = (bf16[128,1024]{1,0:T(8,128)(2,1)}, bf16[128,1024]{1,0:T(8,128)(2,1)}, u32[]{:S(2)}, u32[]{:S(2)}) collective-permute-start(bf16[128,1024]{1,0:T(8,128)(2,1)} %get-tuple-element.89), channel_id=1, source_target_pairs={{0,2},{2,4},{4,6},{6,7},{7,5},{5,3},{3,1},{1,0},{8,10},{10,12},{12... | collective-permute-start | bytes 786440 | tf_op jit(solution)/shard_map/ppermute | solution.py:665
  531.2 111.8 %collective-permute-start.37 = (bf16[512,2048]{1,0:T(8,128)(2,1)}, bf16[512,2048]{1,0:T(8,128)(2,1)S(1)}, u32[]{:S(2)}, u32[]{:S(2)}) collective-permute-start(bf16[512,2048]{1,0:T(8,128)(2,1)} %get-tuple-element.80), channel_id=1, source_target_pairs={{0,8},{8,0},{16,24},{24,16},{1,9},{9,1},{17,25},{25,17},{2,10},{10... | collective-permute-start | bytes 6291464 | tf_op jit(solution)/shard_map/ppermute | solution.py:623
  533.0 54.8 %collective-permute-start.69 = (bf16[128,2048]{1,0:T(8,128)(2,1)S(1)}, bf16[128,2048]{1,0:T(8,128)(2,1)S(1)}, u32[]{:S(2)}, u32[]{:S(2)}) collective-permute-start(bf16[128,2048]{1,0:T(8,128)(2,1)S(1)} %pad_maximum_fusion.10), channel_id=1, source_target_pairs={{2,0},{4,2},{6,4},{7,6},{5,7},{3,5},{1,3},{0,1},{10,8},{12,10},{14... | collective-permute-start | bytes 1572872 | tf_op jit(solution)/shard_map/ppermute | solution.py:666
  550.2 51.2 %collective-permute-start.47 = (bf16[256,1024]{1,0:T(8,128)(2,1)S(1)}, bf16[256,1024]{1,0:T(8,128)(2,1)S(1)}, u32[]{:S(2)}, u32[]{:S(2)}) collective-permute-start(bf16[256,1024]{1,0:T(8,128)(2,1)S(1)} %pad_maximum_fusion.8), channel_id=1, source_target_pairs={{2,0},{4,2},{6,4},{7,6},{5,7},{3,5},{1,3},{0,1},{10,8},{12,10},{14... | collective-permute-start | bytes 1572872 | tf_op jit(solution)/shard_map/ppermute | solution.py:666
  571.4 41.0 %collective-permute-start.58 = (bf16[256,1408]{1,0:T(8,128)(2,1)S(1)}, bf16[256,1408]{1,0:T(8,128)(2,1)S(1)}, u32[]{:S(2)}, u32[]{:S(2)}) collective-permute-start(bf16[256,1408]{1,0:T(8,128)(2,1)S(1)} %pad_maximum_fusion.6), channel_id=1, source_target_pairs={{2,0},{4,2},{6,4},{7,6},{5,7},{3,5},{1,3},{0,1},{10,8},{12,10},{14... | collective-permute-start | bytes 2162696 | tf_op jit(solution)/shard_map/ppermute | solution.py:666
  601.4 46.4 %collective-permute-start.40 = (bf16[512,2048]{1,0:T(8,128)(2,1)S(1)}, bf16[512,2048]{1,0:T(8,128)(2,1)S(1)}, u32[]{:S(2)}, u32[]{:S(2)}) collective-permute-start(bf16[512,2048]{1,0:T(8,128)(2,1)S(1)} %get-tuple-element.76), channel_id=1, source_target_pairs={{0,8},{8,0},{16,24},{24,16},{1,9},{9,1},{17,25},{25,17},{2,10},{10... | collective-permute-start | bytes 6291464 | tf_op jit(solution)/shard_map/ppermute | solution.py:623
  610.4 211.9 %collective-permute-start.39 = (bf16[512,2048]{1,0:T(8,128)(2,1)}, bf16[512,2048]{1,0:T(8,128)(2,1)}, u32[]{:S(2)}, u32[]{:S(2)}) collective-permute-start(bf16[512,2048]{1,0:T(8,128)(2,1)} %get-tuple-element.77), channel_id=1, source_target_pairs={{0,8},{8,0},{16,24},{24,16},{1,9},{9,1},{17,25},{25,17},{2,10},{10... | collective-permute-start | bytes 6291464 | tf_op jit(solution)/shard_map/ppermute | solution.py:623
  683.6 174.0 %collective-permute-start.36 = (bf16[512,2048]{1,0:T(8,128)(2,1)}, bf16[512,2048]{1,0:T(8,128)(2,1)}, u32[]{:S(2)}, u32[]{:S(2)}) collective-permute-start(bf16[512,2048]{1,0:T(8,128)(2,1)} %get-tuple-element.79), channel_id=1, source_target_pairs={{0,8},{8,0},{16,24},{24,16},{1,9},{9,1},{17,25},{25,17},{2,10},{10... | collective-permute-start | bytes 6291464 | tf_op jit(solution)/shard_map/ppermute | solution.py:623
  683.6 166.4 %collective-permute-start.41 = (bf16[512,2048]{1,0:T(8,128)(2,1)S(1)}, bf16[512,2048]{1,0:T(8,128)(2,1)}, u32[]{:S(2)}, u32[]{:S(2)}) collective-permute-start(bf16[512,2048]{1,0:T(8,128)(2,1)S(1)} %add_convert_fusion), channel_id=1, source_target_pairs={{0,16},{8,24},{16,0},{24,8},{1,17},{9,25},{17,1},{25,9},{2,18},{10... | collective-permute-start | bytes 6291464 | tf_op jit(solution)/shard_map/ppermute | solution.py:623
  684.5 173.6 %collective-permute-start.38 = (bf16[512,2048]{1,0:T(8,128)(2,1)}, bf16[512,2048]{1,0:T(8,128)(2,1)}, u32[]{:S(2)}, u32[]{:S(2)}) collective-permute-start(bf16[512,2048]{1,0:T(8,128)(2,1)} %fusion), channel_id=1, source_target_pairs={{0,16},{8,24},{16,0},{24,8},{1,17},{9,25},{17,1},{25,9},{2,18},{10... | collective-permute-start | bytes 6291464 | tf_op jit(solution)/shard_map/ppermute | solution.py:623
  685.8 131.9 %collective-permute-start.60 = (bf16[256,1408]{1,0:T(8,128)(2,1)}, bf16[256,1408]{1,0:T(8,128)(2,1)}, u32[]{:S(2)}, u32[]{:S(2)}) collective-permute-start(bf16[256,1408]{1,0:T(8,128)(2,1)} %fusion.6), channel_id=1, source_target_pairs={{2,0},{4,2},{6,4},{7,6},{5,7},{3,5},{1,3},{0,1},{10,8},{12,10},{14... | collective-permute-start | bytes 2162696 | tf_op jit(solution)/shard_map/ppermute | solution.py:666
  (105 other events, 1772.9 us)
Sparse Core Ops, SparseCore 0:
  688.7 120.1 all-reduce.3

commit v2 on v1

v2 whole, which is shorter than its diff:
```python
import functools

import jax
import jax.numpy as jnp
from jax import lax
from jax.experimental import pallas as pl
from jax.experimental.pallas import tpu as pltpu
from jax.sharding import PartitionSpec as P

D = 2048
DIN = 4096
P_SIZE = 64
N = 128
Q = 256
H = 64
CONVCH = DIN + 2 * N
EPSILON = 1e-05
LOG2E = 1.4426950408889634
LANES = 128
TOK = 512
TILES = DIN // 128 // 4
REST = TILES * 128 + 2 * N + H // 4
HIGHEST = lax.Precision.HIGHEST
BF = jnp.bfloat16
F32 = jnp.float32
NT = (((1,), (1,)), ((), ()))
TN = (((0,), (0,)), ((), ()))
VMEM_LIMIT = 48 * 1024 * 1024
RING = (0, 2, 4, 6, 7, 5, 3, 1)


def mm(a, b):
    return jnp.dot(a, b, preferred_element_type=F32)


def mm_nt(a, b):
    return lax.dot_general(a, b, NT, preferred_element_type=F32)


def iota(shape, dim):
    return lax.broadcasted_iota(jnp.int32, shape, dim)


def start_of(rows, b1, b2):
    return jnp.where(rows >= b2, b2, jnp.where(rows >= b1, b1, 0))


def sigmoid(v):
    return 0.5 * jnp.tanh(0.5 * v) + 0.5


def conv_pre(x, taps, bias, lk):
    pre = bias + taps[3] * x
    for k in range(1, 4):
        pre = pre + taps[3 - k] * (pltpu.roll(x, k, 0) * lk[k - 1])
    return pre


def taps_of(cw_ref, lanes):
    return [cw_ref[k : k + 1, lanes] for k in range(4)], cw_ref[4:5, lanes]


def prepare(b1, b2, bc_ref, dt_ref, cwb_ref, hp_ref, lk, score, bmat, cmat, btrans, ctrans,
            dts, sig, cum, cumt, ecol, tcol, transposed):
    rows = iota((TOK, LANES), 0)
    pos = rows - start_of(rows, b1, b2)
    for k in range(1, 4):
        lk[k - 1] = (pos >= k).astype(F32)
    links = [lk[0], lk[1], lk[2]]
    for half, keep in ((0, bmat), (1, cmat)):
        lanes = slice(half * LANES, (half + 1) * LANES)
        taps, bias = taps_of(cwb_ref, lanes)
        pre = conv_pre(bc_ref[:, lanes].astype(F32), taps, bias, links)
        act = pre * sigmoid(pre)
        keep[...] = act.astype(BF)
        if half == 0:
            btrans[...] = act[:Q].T.astype(BF)
        elif ctrans is not None:
            ctrans[...] = act[Q:].T.astype(BF)
    for c in range(2):
        part = slice(c * Q, (c + 1) * Q)
        if transposed:
            s = mm_nt(bmat[part, :], cmat[part, :])
        else:
            s = mm_nt(cmat[part, :], bmat[part, :])
        score[c] = jnp.where(allowed(c, b1, b2, transposed), s, 0.0)
    raw = jnp.where(iota((TOK, LANES), 1) < H // 4, dt_ref[...].astype(F32), 0.0) + hp_ref[0:1, :]
    step = jnp.maximum(raw, 0.0) + jnp.log1p(jnp.exp(-jnp.abs(raw)))
    dts[...] = step
    if sig is not None:
        sig[...] = sigmoid(raw)
    decay = step * (hp_ref[1:2, :] * LOG2E)
    lower = (iota((Q, Q), 0) >= iota((Q, Q), 1)).astype(F32)
    for c in range(2):
        part = slice(c * Q, (c + 1) * Q)
        total = jnp.dot(lower, decay[part], precision=HIGHEST, preferred_element_type=F32)
        cum[part, :] = total
        cumt[:, part] = total.T
        if c == 0:
            last = start_of(Q - 1, b1, b2)
            tcol[...] = jnp.where(rows[:Q] >= last, jnp.exp2(total[Q - 1 : Q, :] - total), 0.0)
        else:
            linked = start_of(rows[Q:], b1, b2) <= Q - 1
            ecol[...] = jnp.where(linked, jnp.exp2(total), 0.0)


def allowed(c, b1, b2, transposed):
    late = iota((Q, Q), 1 if transposed else 0) + c * Q
    early = iota((Q, Q), 0 if transposed else 1) + c * Q
    return (early <= late) & (early >= start_of(late, b1, b2))


def pair(ref_value, first):
    return jnp.where(first, ref_value[:, 0:1], ref_value[:, 1:2])


def fwd_kernel(bnd, xs_ref, bc_ref, dt_ref, cwx_ref, cwb_ref, hp_ref, out_ref,
               lk, score, bmat, cmat, btrans, dts, cum, cumt, ecol, tcol):
    b, t = pl.program_id(0), pl.program_id(1)

    @pl.when(t == 0)
    def _():
        prepare(bnd[b, 0], bnd[b, 1], bc_ref, dt_ref, cwb_ref, hp_ref, lk, score, bmat, cmat,
                btrans, None, dts, None, cum, cumt, ecol, tcol, False)

    turn = lax.rem(LANES - 2 * t, LANES)
    taps, bias = taps_of(cwx_ref, slice(None))
    pre = conv_pre(xs_ref[...].astype(F32), taps, bias, [lk[0], lk[1], lk[2]])
    x = pre * sigmoid(pre)
    first = iota((TOK, LANES), 1) < P_SIZE
    xt = x * pair(pltpu.roll(dts[...], turn, 1), first)
    xt16 = xt.astype(BF)
    mine = [jnp.where(first, xt16, jnp.zeros_like(xt16)), jnp.where(first, jnp.zeros_like(xt16), xt16)]
    cumr = pltpu.roll(cum[...], turn, 1)
    half = Q // 2
    outs = []
    for c in range(2):
        o = c * Q
        top = bottom = None
        for h in range(2):
            row = cumt[pl.ds(2 * t + h, 1), o : o + Q]
            col = cumr[o : o + Q, h : h + 1]
            w = jnp.exp2(jnp.minimum(col[:half] - row[:, :half], 0.0)) * score[c, :half, :half]
            y = mm(w.astype(BF), mine[h][o : o + half])
            top = y if top is None else top + y
            w = jnp.exp2(jnp.minimum(col[half:] - row, 0.0)) * score[c, half:, :]
            y = mm(w.astype(BF), mine[h][o : o + Q])
            bottom = y if bottom is None else bottom + y
        outs.append(jnp.concatenate([top, bottom], 0))
    tx = pair(pltpu.roll(tcol[...], turn, 1), first[:Q])
    ex = pair(pltpu.roll(ecol[...], turn, 1), first[:Q])
    state = mm(btrans[...], (tx * xt[:Q]).astype(BF))
    outs[1] = outs[1] + mm(cmat[Q:, :], state.astype(BF)) * ex
    skip = cwx_ref[5:6, :]
    out_ref[...] = jnp.concatenate(outs, 0) + skip * x


def bwd_kernel(bnd, xs_ref, bc_ref, dt_ref, cwx_ref, cwb_ref, hp_ref, scan_ref, dscan_ref,
               out_ref, dcw_ref, dhp_ref,
               lk, score, bmat, cmat, btrans, ctrans, dts, sig, cum, cumt, ecol, tcol, dscore, rsum, rsum3, dball, dcall):
    b, t = pl.program_id(0), pl.program_id(1)
    tiles = TILES
    b1, b2 = bnd[b, 0], bnd[b, 1]

    @pl.when(t == 0)
    def _():
        prepare(b1, b2, bc_ref, dt_ref, cwb_ref, hp_ref, lk, score, bmat, cmat,
                btrans, ctrans, dts, sig, cum, cumt, ecol, tcol, True)
        dscore[...] = jnp.zeros_like(dscore)
        rsum[...] = jnp.zeros_like(rsum)
        rsum3[...] = jnp.zeros_like(rsum3)
        dball[...] = jnp.zeros_like(dball)
        dcall[...] = jnp.zeros_like(dcall)

    @pl.when((t == 0) & (b == 0))
    def _():
        dcw_ref[...] = jnp.zeros_like(dcw_ref)
        dhp_ref[...] = jnp.zeros_like(dhp_ref)

    turn = lax.rem(LANES - 2 * t, LANES)
    taps, bias = taps_of(cwx_ref, slice(None))
    links = [lk[0], lk[1], lk[2]]
    xin = xs_ref[...].astype(F32)
    pre = conv_pre(xin, taps, bias, links)
    sg = sigmoid(pre)
    x = pre * sg
    first = iota((TOK, LANES), 1) < P_SIZE
    dtx = pair(pltpu.roll(dts[...], turn, 1), first)
    xt = x * dtx
    xt16 = xt.astype(BF)
    xtf = xt16.astype(F32)
    skip = cwx_ref[5:6, :]
    dy16 = dscan_ref[...]
    dy = dy16.astype(F32)
    dyf = dy
    mine = [jnp.where(first, dy16, jnp.zeros_like(dy16)), jnp.where(first, jnp.zeros_like(dy16), dy16)]
    cumr = pltpu.roll(cum[...], turn, 1)
    half = Q // 2
    parts = []
    for c in range(2):
        o = c * Q
        top = bottom = None
        for h in range(2):
            row = cumt[pl.ds(2 * t + h, 1), o : o + Q]
            col = cumr[o : o + Q, h : h + 1]
            w = jnp.exp2(jnp.minimum(row - col[:half], 0.0))
            dscore[c, :half, :] += w * mm_nt(xt16[o : o + half], mine[h][o : o + Q])
            y = mm((w * score[c, :half, :]).astype(BF), mine[h][o : o + Q])
            top = y if top is None else top + y
            w = jnp.exp2(jnp.minimum(row[:, half:] - col[half:], 0.0))
            dscore[c, half:, half:] += w * mm_nt(xt16[o + half : o + Q], mine[h][o + half : o + Q])
            y = mm((w * score[c, half:, half:]).astype(BF), mine[h][o + half : o + Q])
            bottom = y if bottom is None else bottom + y
        parts.append(jnp.concatenate([top, bottom], 0))
    tx = pair(pltpu.roll(tcol[...], turn, 1), first[:Q])
    ex = pair(pltpu.roll(ecol[...], turn, 1), first[:Q])
    txt16 = (tx * xt[:Q]).astype(BF)
    state = mm(btrans[...], txt16).astype(BF)
    dye = (ex * dy[Q:]).astype(BF)
    dstate = mm(ctrans[...], dye).astype(BF)
    dcall[...] += mm_nt(dye, state)
    dball[...] += mm_nt(txt16, dstate)
    across = tx * mm(bmat[:Q, :], dstate)
    within = jnp.concatenate(parts, 0)
    dxt = jnp.concatenate([parts[0] + across, parts[1]], 0)
    r1 = dyf * (scan_ref[...] - skip * x) - xtf * within
    r2 = x * dxt
    r3 = xtf[:Q] * across

    def split(v):
        hi = v.astype(BF)
        return [hi, (v - hi.astype(F32)).astype(BF)]

    def to_heads(width, offset):
        lane, head = iota((LANES, width), 0), iota((LANES, width), 1)
        return (head == offset + 2 * t + jnp.where(lane >= P_SIZE, 1, 0)).astype(BF)

    e1, e2 = to_heads(2 * LANES, 0), to_heads(2 * LANES, LANES)
    rsum[...] += mm(jnp.concatenate(split(r1), 1), jnp.concatenate([e1, e1], 0)) + mm(
        jnp.concatenate(split(r2), 1), jnp.concatenate([e2, e2], 0)
    )
    e3 = to_heads(LANES, 0)
    rsum3[...] += mm(jnp.concatenate(split(r3), 1), jnp.concatenate([e3, e3], 0))

    def conv_back(dact, pre, sg, xin, taps):
        dpre = dact * (sg * (1.0 + pre * (1.0 - sg)))
        g = taps[3] * dpre
        sums = [None] * 5
        sums[3] = jnp.sum(dpre * xin, axis=0, keepdims=True)
        sums[4] = jnp.sum(dpre, axis=0, keepdims=True)
        for k in range(1, 4):
            q = links[k - 1] * dpre
            g = g + taps[3 - k] * pltpu.roll(q, TOK - k, 0)
            sums[3 - k] = jnp.sum(q * pltpu.roll(xin, k, 0), axis=0, keepdims=True)
        return g, sums

    g, sums = conv_back(dxt * dtx + skip * dy, pre, sg, xin, taps)
    sums.append(jnp.sum(dy * x, axis=0, keepdims=True))
    sums.append(jnp.zeros((2, LANES), F32))
    here = pl.ds(pl.multiple_of(t * LANES, LANES), LANES)
    out_ref[:, here] = g.astype(BF)
    dcw_ref[:, here] += jnp.concatenate(sums, 0)

    @pl.when(t == tiles - 1)
    def _():
        db, dc = [], []
        for c in range(2):
            part = slice(c * Q, (c + 1) * Q)
            ds = jnp.where(allowed(c, b1, b2, True), dscore[c], 0.0)
            db.append(mm(ds.astype(BF), cmat[part, :]))
            dc.append(mm(ds.T.astype(BF), bmat[part, :]))
        db[0] = db[0] + dball[...]
        dc[1] = dc[1] + dcall[...]
        base = tiles * LANES
        for i, dact in enumerate((jnp.concatenate(db, 0), jnp.concatenate(dc, 0))):
            lanes = slice(i * LANES, (i + 1) * LANES)
            taps_b, bias_b = taps_of(cwb_ref, lanes)
            xin_b = bc_ref[:, lanes].astype(F32)
            pre_b = conv_pre(xin_b, taps_b, bias_b, links)
            g, sums = conv_back(dact, pre_b, sigmoid(pre_b), xin_b, taps_b)
            sums.append(jnp.zeros((3, LANES), F32))
            at = slice(base + i * LANES, base + (i + 1) * LANES)
            out_ref[:, at] = g.astype(BF)
            dcw_ref[:, at] += jnp.concatenate(sums, 0)
        upper = (iota((Q, Q), 0) <= iota((Q, Q), 1)).astype(F32)
        below = (iota((Q, Q), 0) > iota((Q, Q), 1)).astype(F32)
        high = functools.partial(jnp.dot, precision=HIGHEST, preferred_element_type=F32)
        rate = hp_ref[1:2, :]
        da = jnp.concatenate(
            [
                high(upper, rsum[:Q, :LANES]) + high(below, rsum3[...]),
                high(upper, rsum[Q:, :LANES]),
            ],
            0,
        )
        step = dts[...]
        draw = (rsum[:, LANES:] + da * rate) * sig[...]
        dhp_ref[0:1, :] += jnp.sum(draw, axis=0, keepdims=True)
        dhp_ref[1:2, :] += jnp.sum(da * (rate * step), axis=0, keepdims=True)
        out_ref[:, base + 2 * LANES :] = draw[:, : H // 4].astype(BF)


def params(*semantics):
    return pltpu.CompilerParams(dimension_semantics=semantics, vmem_limit_bytes=VMEM_LIMIT)


def cost(flops, moved):
    return pl.CostEstimate(flops=int(flops), bytes_accessed=int(moved), transcendentals=0)


def block_scratch(extra):
    column = pltpu.VMEM((TOK, LANES), F32)
    part = pltpu.VMEM((Q, LANES), F32)
    half = pltpu.VMEM((LANES, Q), BF)
    base = [
        pltpu.VMEM((3, TOK, LANES), F32),
        pltpu.VMEM((2, Q, Q), F32),
        pltpu.VMEM((TOK, LANES), BF),
        pltpu.VMEM((TOK, LANES), BF),
        half,
    ]
    rest = [column, pltpu.VMEM((LANES, TOK), F32), part, part]
    if not extra:
        return base + [column] + rest
    return base + [half, column, column] + rest + [
        pltpu.VMEM((2, Q, Q), F32),
        pltpu.VMEM((TOK, 2 * LANES), F32),
        part,
        part,
        part,
    ]


def mixer_specs(first):
    return [
        pl.BlockSpec((TOK, LANES), lambda b, t, *_: (b + first, t)),
        pl.BlockSpec((TOK, 2 * LANES), lambda b, t, *_: (b + first, TILES // 2)),
        pl.BlockSpec((TOK, LANES), lambda b, t, *_: (b + first, TILES + 2)),
        pl.BlockSpec((8, LANES), lambda b, t, *_: (0, t)),
        pl.BlockSpec((8, 2 * LANES), lambda b, t, *_: (0, TILES // 2)),
        pl.BlockSpec((8, LANES), lambda b, t, *_: (0, 0)),
    ]


ANY = pl.BlockSpec(memory_space=pl.ANY)


def fwd_into(bnd, *refs):
    fwd_kernel(bnd, *refs[:6], *refs[7:])


def scan_forward(bounds, proj, cw, hp, first, count, into=None):
    return pl.pallas_call(
        fwd_kernel if into is None else fwd_into,
        out_shape=jax.ShapeDtypeStruct((proj.shape[0], TILES * LANES), F32),
        grid_spec=pltpu.PrefetchScalarGridSpec(
            num_scalar_prefetch=1,
            grid=(count, TILES),
            in_specs=mixer_specs(first) + ([] if into is None else [ANY]),
            out_specs=pl.BlockSpec((TOK, LANES), lambda b, t, *_: (b + first, t)),
            scratch_shapes=block_scratch(False),
        ),
        input_output_aliases={} if into is None else {7: 0},
        compiler_params=params("arbitrary", "arbitrary"),
        cost_estimate=cost(count * 8e9, count * 4e6),
    )(bounds[first : first + count], proj, proj, proj, cw, cw, hp, *([] if into is None else [into]))


def bwd_into(bnd, *refs):
    bwd_kernel(bnd, *refs[:8], *refs[9:])


def scan_backward(bounds, proj, cw, hp, scan, dscan, first, count, into=None):
    tile = pl.BlockSpec((TOK, LANES), lambda b, t, *_: (b + first, t))
    return pl.pallas_call(
        bwd_kernel if into is None else bwd_into,
        out_shape=(
            jax.ShapeDtypeStruct((proj.shape[0], REST), BF),
            jax.ShapeDtypeStruct((8, (TILES + 2) * LANES), F32),
            jax.ShapeDtypeStruct((8, LANES), F32),
        ),
        grid_spec=pltpu.PrefetchScalarGridSpec(
            num_scalar_prefetch=1,
            grid=(count, TILES),
            in_specs=mixer_specs(first) + [tile, tile] + ([] if into is None else [ANY]),
            out_specs=(
                pl.BlockSpec((TOK, REST), lambda b, t, *_: (b + first, 0)),
                pl.BlockSpec((8, (TILES + 2) * LANES), lambda b, t, *_: (0, 0)),
                pl.BlockSpec((8, LANES), lambda b, t, *_: (0, 0)),
            ),
            scratch_shapes=block_scratch(True),
        ),
        input_output_aliases={} if into is None else {9: 0},
        compiler_params=params("arbitrary", "arbitrary"),
        cost_estimate=cost(count * 16e9, count * 6e6),
    )(bounds[first : first + count], proj, proj, proj, cw, cw, hp, scan, dscan, *([] if into is None else [into]))


def ginner_kernel(gout_ref, w_ref, out_ref, wide_ref):
    @pl.when(pl.program_id(0) == 0)
    def _():
        for k in range(8):
            for p in range(8):
                wide_ref[p * LANES : (p + 1) * LANES, k * 256 : (k + 1) * 256] = w_ref[
                    k * LANES : (k + 1) * LANES, p * 256 : (p + 1) * 256
                ]

    out_ref[...] = mm_nt(gout_ref[...], wide_ref[...]).astype(BF)


def inner_gradient(gout, w_two):
    rows, inner = gout.shape[0], TILES * LANES
    return pl.pallas_call(
        ginner_kernel,
        out_shape=(jax.ShapeDtypeStruct((rows, inner), BF), jax.ShapeDtypeStruct((inner, D), BF)),
        grid=(rows // TOK,),
        in_specs=[
            pl.BlockSpec((TOK, D), lambda i: (i, 0)),
            pl.BlockSpec((inner, D), lambda i: (1, 0)),
        ],
        out_specs=(pl.BlockSpec((TOK, inner), lambda i: (i, 0)), pl.BlockSpec((inner, D), lambda i: (0, 0))),
        compiler_params=params("arbitrary"),
        cost_estimate=cost(2 * rows * inner * D, 2 * (rows * D + rows * inner + 2 * inner * D)),
    )(gout, w_two)


def stat_kernel(place, norm_ref, w_ref, scan_ref, gin_ref, gain_ref, gate_ref, out_ref):
    gate_ref[...] = mm_nt(norm_ref[...], w_ref[...]).astype(BF)
    one = two = jnp.zeros((TOK, LANES), F32)
    for t in range(TILES):
        at = slice(t * LANES, (t + 1) * LANES)
        there = pl.ds(pl.multiple_of(place[t] * LANES, LANES), LANES)
        gate = gate_ref[:, at].astype(F32)
        gated = scan_ref[:, at] * (gate * sigmoid(gate))
        one = one + gated * gated
        two = two + gated * (gin_ref[:, there].astype(F32) * gain_ref[:, at])
    a = jnp.sum(one.T, axis=0, keepdims=True)
    c = jnp.sum(two.T, axis=0, keepdims=True)
    out_ref[0] = jnp.concatenate([a, c, jnp.zeros((6, TOK), F32)], 0)


def gate_stats(place, normed, w_two, scan, ginner, gain):
    rows, inner = scan.shape
    tile = pl.BlockSpec((TOK, inner), lambda b, *_: (b, 0))
    return pl.pallas_call(
        stat_kernel,
        out_shape=(jax.ShapeDtypeStruct((rows, inner), BF), jax.ShapeDtypeStruct((rows // TOK, 8, TOK), F32)),
        grid_spec=pltpu.PrefetchScalarGridSpec(
            num_scalar_prefetch=1,
            grid=(rows // TOK,),
            in_specs=[
                pl.BlockSpec((TOK, D), lambda b, *_: (b, 0)),
                pl.BlockSpec((inner, D), lambda b, *_: (0, 0)),
                tile,
                tile,
                pl.BlockSpec((1, inner), lambda b, *_: (0, 0)),
            ],
            out_specs=(tile, pl.BlockSpec((1, 8, TOK), lambda b, *_: (b, 0, 0))),
        ),
        compiler_params=params("arbitrary"),
        cost_estimate=cost(2 * rows * inner * D, rows * (D * 2 + inner * 8) + inner * D * 2),
    )(place, normed, w_two, scan, ginner, gain)


def gate_kernel(place, sum_ref, scan_ref, gate_ref, gin_ref, gain_ref, inner_ref, dgate_ref, dscan_ref, dgain_ref):
    rows = scan_ref.shape[0]

    @pl.when((pl.program_id(0) == 0) & (pl.program_id(1) == 0))
    def _():
        dgain_ref[...] = jnp.zeros_like(dgain_ref)

    r = lax.rsqrt(sum_ref[0, 0:1, :] * (1.0 / DIN) + EPSILON)
    c = r * r * sum_ref[0, 1:2, :] * (1.0 / DIN)
    rinv = jnp.broadcast_to(r, (LANES, rows)).T
    coef = jnp.broadcast_to(c, (LANES, rows)).T
    for t in range(TILES):
        at = slice(t * LANES, (t + 1) * LANES)
        there = pl.ds(pl.multiple_of(place[t] * LANES, LANES), LANES)
        gate = gate_ref[:, at].astype(F32)
        sg = sigmoid(gate)
        act = gate * sg
        scan = scan_ref[:, at]
        gain = gain_ref[:, at]
        gated = scan * act
        scaled = gated * rinv
        gin = gin_ref[:, there].astype(F32)
        inner_ref[:, there] = (scaled * gain).astype(BF)
        dgated = rinv * (gin * gain - gated * coef)
        dscan_ref[:, at] = (dgated * act).astype(BF)
        dgate_ref[:, at] = (dgated * scan * (sg + act * (1.0 - sg))).astype(BF)
        dgain_ref[0:1, at] += jnp.sum(gin * scaled, axis=0, keepdims=True)


def gate_both(place, sums, scan, gate, ginner, gain):
    rows, inner = scan.shape
    tile = pl.BlockSpec((Q, inner), lambda b, h, *_: (2 * b + h, 0))
    out = jax.ShapeDtypeStruct((rows, inner), BF)
    return pl.pallas_call(
        gate_kernel,
        out_shape=(out, out, out, jax.ShapeDtypeStruct((8, inner), F32)),
        grid_spec=pltpu.PrefetchScalarGridSpec(
            num_scalar_prefetch=1,
            grid=(rows // TOK, 2),
            in_specs=[
                pl.BlockSpec((1, 8, Q), lambda b, h, *_: (b, 0, h)),
                tile,
                tile,
                tile,
                pl.BlockSpec((1, inner), lambda b, h, *_: (0, 0)),
            ],
            out_specs=(tile, tile, tile, pl.BlockSpec((8, inner), lambda b, h, *_: (0, 0))),
        ),
        compiler_params=params("arbitrary", "arbitrary"),
        cost_estimate=cost(0, rows * inner * 14),
    )(place, sums, scan, gate, ginner, gain)


def back_kernel(a_ref, wa_ref, b_ref, wb_ref, norm_ref, out_ref, dgo_ref):
    @pl.when(pl.program_id(0) == 0)
    def _():
        dgo_ref[...] = jnp.zeros_like(dgo_ref)

    for c in range(4):
        at = slice(c * 512, (c + 1) * 512)
        res = mm(a_ref[...], wa_ref[:, at]) + mm(b_ref[...], wb_ref[:, at])
        out_ref[:, at] = res.astype(BF)
        dgo_ref[0:1, at] += jnp.sum(res * norm_ref[:, at].astype(F32), axis=0, keepdims=True)


def normed_gradient(gproj, w_rest, dgate, w_two, normed, first, count):
    rows, inner = dgate.shape
    row = lambda width: pl.BlockSpec((TOK, width), lambda b: (b + first, 0))
    return pl.pallas_call(
        back_kernel,
        out_shape=(jax.ShapeDtypeStruct((count * TOK, D), BF), jax.ShapeDtypeStruct((8, D), F32)),
        grid=(count,),
        in_specs=[
            row(REST),
            pl.BlockSpec((REST, D), lambda b: (0, 0)),
            row(inner),
            pl.BlockSpec((inner, D), lambda b: (0, 0)),
            row(D),
        ],
        out_specs=(pl.BlockSpec((TOK, D), lambda b: (b, 0)), pl.BlockSpec((8, D), lambda b: (0, 0))),
        compiler_params=params("arbitrary"),
        cost_estimate=cost(2 * count * TOK * D * (REST + inner), 2 * (REST + inner) * D),
    )(gproj, w_rest, dgate, w_two, normed)


def across_kernel(a_ref, b_ref, out_ref, turned):
    @pl.when(pl.program_id(0) == 0)
    def _():
        turned[...] = a_ref[...].T

    res = mm(turned[...], b_ref[...])
    if out_ref.shape[0] == res.shape[0]:
        out_ref[...] = res.astype(out_ref.dtype)
    else:
        for p in range(8):
            out_ref[:, p * 256 : (p + 1) * 256] = res[p * LANES : (p + 1) * LANES].astype(out_ref.dtype)


def across_rows(a, b, retile):
    rows, m = a.shape
    n = b.shape[1]
    if retile:
        spec = pl.BlockSpec((LANES, 8 * 256), lambda k: (k, 0))
    else:
        spec = pl.BlockSpec((m, 256), lambda k: (0, k))
    return pl.pallas_call(
        across_kernel,
        out_shape=jax.ShapeDtypeStruct((m, n), BF),
        grid=(n // 256,),
        in_specs=[pl.BlockSpec((rows, m), lambda k: (0, 0)), pl.BlockSpec((rows, 256), lambda k: (0, k))],
        out_specs=spec,
        scratch_shapes=[pltpu.VMEM((m, rows), BF)],
        compiler_params=params("arbitrary"),
        cost_estimate=cost(2 * rows * m * n, 2 * (rows * m + rows * n + m * n)),
    )(a, b)


STEP = 128


def norm_kernel(perm, tok_ref, gain_ref, out_ref):
    x = tok_ref[...].astype(F32)
    inv = lax.rsqrt(jnp.mean(x * x, axis=1, keepdims=True) + EPSILON)
    wide = D // 8
    for k in range(8):
        here = pl.ds(pl.multiple_of(perm[k] * wide, wide), wide)
        out_ref[:, k * wide : (k + 1) * wide] = (
            tok_ref[:, here].astype(F32) * inv * gain_ref[:, here]
        ).astype(BF)


def norm_rows(perm, tokens, gain):
    rows = tokens.shape[0]
    row = pl.BlockSpec((STEP, D), lambda i, *_: (i, 0))
    return pl.pallas_call(
        norm_kernel,
        out_shape=jax.ShapeDtypeStruct((rows, D), BF),
        grid_spec=pltpu.PrefetchScalarGridSpec(
            num_scalar_prefetch=1,
            grid=(rows // STEP,),
            in_specs=[row, pl.BlockSpec((1, D), lambda i, *_: (0, 0))],
            out_specs=row,
        ),
        compiler_params=params("arbitrary"),
        cost_estimate=pl.CostEstimate(flops=0, bytes_accessed=rows * D * 4, transcendentals=0),
    )(perm, tokens, gain)


def last_kernel(perm, tok_ref, cot_ref, keep_ref, gain_ref, one_ref, two_ref, three_ref, out_ref, grad):
    wide = D // 8
    for k in range(8):
        here = pl.ds(pl.multiple_of(perm[k] * wide, wide), wide)
        at = slice(k * wide, (k + 1) * wide)
        grad[:, here] = (
            one_ref[:, at].astype(F32) + two_ref[:, at].astype(F32) + three_ref[:, at].astype(F32)
        ) * gain_ref[:, here]
    x = tok_ref[...].astype(F32)
    inv = lax.rsqrt(jnp.mean(x * x, axis=1, keepdims=True) + EPSILON)
    g = grad[...]
    dot = jnp.mean(g * x, axis=1, keepdims=True)
    out_ref[...] = inv * (g - x * (inv * inv * dot)) + keep_ref[...] * cot_ref[...].astype(F32)


def last_rows(perm, tokens, cotangent, keep, gain, parts):
    rows = tokens.shape[0]
    row = pl.BlockSpec((STEP, D), lambda i, *_: (i, 0))
    return pl.pallas_call(
        last_kernel,
        out_shape=jax.ShapeDtypeStruct((rows, D), F32),
        grid_spec=pltpu.PrefetchScalarGridSpec(
            num_scalar_prefetch=1,
            grid=(rows // STEP,),
            in_specs=[
                row,
                row,
                pl.BlockSpec((STEP, 1), lambda i, *_: (i, 0)),
                pl.BlockSpec((1, D), lambda i, *_: (0, 0)),
                row,
                row,
                row,
            ],
            out_specs=row,
            scratch_shapes=[pltpu.VMEM((STEP, D), F32)],
        ),
        compiler_params=params("arbitrary"),
        cost_estimate=pl.CostEstimate(flops=0, bytes_accessed=rows * D * 14, transcendentals=0),
    )(perm, tokens, cotangent, keep, gain, *parts)


def first_join_kernel(me, one, two, three, four, out_ref, grad_ref, stage, sem):
    pieces = (one, two, three, four)
    inner = TILES * LANES
    copies = []
    for k in range(4):
        q = jnp.bitwise_xor(me[0], k)
        for t in range(TILES):
            rows = pl.ds(pl.multiple_of((4 * t + q) * LANES, LANES), LANES)
            stage[rows, :] = pieces[k][t * LANES : (t + 1) * LANES, :].astype(F32)
    copy = pltpu.make_async_copy(stage, out_ref.at[pl.ds(0, 4 * inner)], sem)
    copy.start()
    for k in range(4):
        q = jnp.bitwise_xor(me[0], k)
        rows = pl.ds(pl.multiple_of(q * LANES, LANES), LANES)
        for c in range(8 if one.shape[1] == 256 else 0):
            grad_ref[rows, c * 256 : (c + 1) * 256] = pieces[k][
                inner + c * LANES : inner + (c + 1) * LANES, :
            ].astype(F32)
    copy.wait()


def first_join(me, pieces, width):
    lanes = pieces[0].shape[1]
    whole = pl.BlockSpec(pieces[0].shape, lambda i, *_: (0, 0))
    return pl.pallas_call(
        first_join_kernel,
        out_shape=(
            jax.ShapeDtypeStruct((width, lanes), F32),
            jax.ShapeDtypeStruct((4 * LANES, D), F32),
        ),
        grid_spec=pltpu.PrefetchScalarGridSpec(
            num_scalar_prefetch=1,
            grid=(1,),
            in_specs=[whole] * 4,
            out_specs=(ANY, pl.BlockSpec((4 * LANES, D), lambda i, *_: (0, 0))),
            scratch_shapes=[pltpu.VMEM((4 * TILES * LANES, lanes), F32), pltpu.SemaphoreType.DMA],
        ),
        compiler_params=params("arbitrary"),
        cost_estimate=cost(0, 20e6),
    )(me, *pieces)


def last_join_kernel(me, one, two, three, four, into, out_ref, stage, sem):
    pieces = (one, two, three, four)
    inner = TILES * LANES
    few = H // 4
    for k in range(4):
        q = jnp.bitwise_xor(me[0], k)
        for t in range(TILES):
            rows = pl.ds(pl.multiple_of((4 * t + q) * LANES, LANES), LANES)
            stage[rows, :] = pieces[k][t * LANES : (t + 1) * LANES, :].astype(F32)
    stage[4 * inner : 4 * inner + 2 * N, :] = sum(p[inner : inner + 2 * N, :].astype(F32) for p in pieces)
    steps = None
    for k in range(4):
        q = jnp.bitwise_xor(me[0], k)
        head, mine = iota((H, few), 0), iota((H, few), 1)
        spread = (head == 8 * (mine // 2) + 2 * q + mine % 2).astype(BF)
        term = mm(spread, pieces[k][inner + 2 * N :, :])
        steps = term if steps is None else steps + term
    stage[4 * inner + 2 * N :, :] = steps
    copy = pltpu.make_async_copy(stage, out_ref.at[pl.ds(4 * inner, stage.shape[0])], sem)
    copy.start()
    copy.wait()


def last_join(me, pieces, into):
    lanes = pieces[0].shape[1]
    whole = pl.BlockSpec(pieces[0].shape, lambda i, *_: (0, 0))
    return pl.pallas_call(
        last_join_kernel,
        out_shape=jax.ShapeDtypeStruct(into.shape, F32),
        grid_spec=pltpu.PrefetchScalarGridSpec(
            num_scalar_prefetch=1,
            grid=(1,),
            in_specs=[whole] * 4 + [ANY],
            out_specs=ANY,
            scratch_shapes=[pltpu.VMEM((into.shape[0] - 4 * TILES * LANES, lanes), F32), pltpu.SemaphoreType.DMA],
        ),
        input_output_aliases={5: 0},
        compiler_params=params("arbitrary"),
        cost_estimate=cost(0, 8e6),
    )(me, *pieces, into)


def tie(*arrays):
    return lax.optimization_barrier(arrays)


def swap(x, d):
    return lax.ppermute(x, "rep", [(i, i ^ d) for i in range(4)])


def fw(x):
    return lax.ppermute(x, "shard", [(RING[i], RING[(i + 1) % 8]) for i in range(8)])


def bw(x):
    return lax.ppermute(x, "shard", [(RING[(i + 1) % 8], RING[i]) for i in range(8)])


def relative(s, n):
    if n != 8:
        return jnp.arange(8, dtype=jnp.int32), jnp.arange(8, dtype=jnp.int32)
    table, inverse = [], []
    for shard in range(8):
        p = RING.index(shard)
        row = [RING[(p + d) % 8] for d in (0, -1, 1, -2, 2, -3, 3, 4)]
        table.append(row)
        inverse.append([row.index(i) for i in range(8)])
    return jnp.asarray(table, jnp.int32)[s], jnp.asarray(inverse, jnp.int32)[s]


def cut(rows):
    return -(-rows // 32) * 16


def gather_ring(piece, work):
    half = cut(piece.shape[0])
    pieces, a, b = [piece], piece, piece
    done = []
    for k in range(4):
        if k < 3:
            a, b = fw(a), bw(b)
        else:
            a, b = fw(a[:half]), bw(b[half:])
        if k < len(work) and work[k] is not None:
            result = work[k](*done)
            a, b, *result = tie(a, b, *result)
            done = result
        else:
            a, b = tie(a, b)
        pieces += [a, b]
    far = jnp.concatenate(pieces[-2:], 0)
    return jnp.concatenate(pieces[:7] + [far], 1), done


def ring_sum(parts):
    own, f1, b1, f2, b2, f3, b3, far = parts
    half = cut(far.shape[0])
    add = lambda a, b: (a.astype(F32) + b.astype(F32)).astype(BF)
    rf, rb = yield fw(far[:half]), bw(far[half:])
    sf = jnp.concatenate([add(b3[:half], rf), b3[half:]], 0)
    sb = jnp.concatenate([f3[:half], add(f3[half:], rb)], 0)
    rf, rb = yield fw(sf), bw(sb)
    rf, rb = yield fw(add(b2, rf)), bw(add(f2, rb))
    rf, rb = yield fw(add(b1, rf)), bw(add(f1, rb))
    yield (own.astype(F32) + rf.astype(F32) + rb.astype(F32)).astype(BF)


def blocks_of(x):
    return [x[k * TOK : (k + 1) * TOK] for k in range(4)]


def sum_rep(parts):
    far = swap(parts[3], 1)
    chip = swap((parts[2].astype(F32) + far.astype(F32)).astype(BF), 2)
    return parts[0].astype(F32) + swap(parts[1], 1).astype(F32) + chip.astype(F32)


def shards(n, tokens, cotangent, lengths, order, mask, in_weight, out_weight, conv_weight, conv_bias, dt_bias,
           a_log, skip_gain, gain_outer, gain_inner):
    r, s = lax.axis_index("rep"), lax.axis_index("shard")
    ring = n == 8
    inner_width = TILES * LANES
    perm, place = relative(s, n)
    keep = mask.astype(F32)[:, None]
    catalog = jnp.arange(lengths.shape[0], dtype=jnp.int32)
    picked = jnp.sum(jnp.where(order[:, None] == catalog[None, :], lengths[None, :], 0), axis=1)
    bounds = jnp.stack([picked[0], picked[0] + picked[1]])[None, :]
    bounds = jnp.concatenate([bounds, swap(bounds, 1), swap(bounds, 2), swap(bounds, 3)], 0)

    turned = in_weight.T
    lanes = turned.shape[1]

    def own_rows(first, tile):
        part = turned[first : first + TILES * 4 * tile].reshape(TILES, 4, tile, lanes)
        return lax.dynamic_index_in_dim(part, r, 1, False).reshape(TILES * tile, lanes)

    rest = jnp.concatenate(
        [own_rows(DIN, LANES), turned[2 * DIN : 2 * DIN + 2 * N], own_rows(2 * DIN + 2 * N, 2)], 0
    ).astype(BF)
    gate_rows = own_rows(0, LANES).astype(BF)
    normed = norm_rows(perm, tokens, gain_outer[None, :])
    gout = (cotangent.astype(F32) * keep).astype(BF)

    def own_lanes(v, width):
        v = lax.dynamic_index_in_dim(v.reshape(v.shape[:-1] + (TILES, 4, width)), r, v.ndim, False)
        return v.reshape(v.shape[:-2] + (TILES * width,))

    heads = H // 4
    skip = jnp.broadcast_to(skip_gain[:, None], (H, P_SIZE)).reshape(1, DIN)
    rows8 = jnp.concatenate(
        [conv_weight, conv_bias[None], jnp.pad(skip, ((0, 0), (0, 2 * N))), jnp.zeros((2, CONVCH), F32)], 0
    )
    cw = jnp.concatenate([own_lanes(rows8[:, :DIN], LANES), rows8[:, DIN:]], 1)
    hp = jnp.stack([own_lanes(dt_bias, 2), own_lanes(-jnp.exp(a_log), 2)])
    hp = jnp.pad(hp, ((0, 6), (0, LANES - heads)))
    gain = own_lanes(gain_inner, LANES)[None, :]

    core, chip = swap(normed, 1), swap(normed, 2)
    if ring:
        w_rest, _ = gather_ring(rest, [])
    else:
        w_rest = lax.all_gather(rest, "shard", axis=1, tiled=True)
    w_rest, core, chip = tie(w_rest, core, chip)
    (all_normed,) = tie(jnp.concatenate([normed, core, chip, swap(chip, 1)], 0))

    if ring:
        out_rows = lax.dynamic_slice_in_dim(out_weight, r * LANES, LANES, 0).astype(BF)
        out_rows = out_rows.reshape(LANES, 8, 256).swapaxes(0, 1).reshape(inner_width, 256)
        two, _, gout = tie(jnp.concatenate([gate_rows, out_rows], 0), w_rest, gout)
        gcore, gchip = swap(gout, 1), swap(gout, 2)

        def project():
            return [mm_nt(all_normed, w_rest).astype(BF)]

        def scan_first(proj):
            return [proj, scan_forward(bounds, proj, cw, hp, 0, 2)]

        def scan_last(proj, scan):
            return [proj, scan_forward(bounds, proj, cw, hp, 2, 2, scan)]

        w_two, (proj, scan) = gather_ring(two, [project, scan_first, scan_last])
    else:
        gcore, gchip = swap(gout, 1), swap(gout, 2)
        proj = mm_nt(all_normed, w_rest).astype(BF)
        scan = scan_forward(bounds, proj, cw, hp, 0, 4)
        w_gate = lax.all_gather(gate_rows, "shard", axis=1, tiled=True)
        w_out = lax.all_gather(out_weight.astype(BF), "shard", axis=0, tiled=True)
        w_out = lax.dynamic_index_in_dim(w_out.reshape(TILES, 4, LANES, D), r, 1, False)
        w_out = w_out.reshape(8, LANES, 8, 256).transpose(2, 1, 0, 3).reshape(inner_width, D)
        w_two = jnp.concatenate([w_gate, w_out], 0)
    (all_gout,) = tie(jnp.concatenate([gout, gcore, gchip, swap(gchip, 1)], 0))

    ginner, w_out = inner_gradient(all_gout, w_two)
    gate, sums = gate_stats(place, all_normed, w_two, scan, ginner, gain)
    there = [swap(sums, d) for d in (1, 2, 3)]
    sums = jnp.stack([sums[k] + there[0][k ^ 1] + there[1][k ^ 2] + there[2][k ^ 3] for k in range(4)])
    inner, dgate, dscan, dgain = gate_both(place, sums, scan, gate, ginner, gain)
    grad_gate = across_rows(dgate, all_normed, False)
    grad_out = across_rows(inner, all_gout, True)

    def split(x):
        return [x[:, k * 256 : (k + 1) * 256] for k in range(8)]

    at_r = (jnp.arange(4) == r).astype(F32)
    sizes = [4 * CONVCH, CONVCH, H, H, H, D, DIN]

    def all_lanes(v, width):
        v = v.reshape(v.shape[:-1] + (TILES, 1, width)) * at_r[:, None]
        return v.reshape(v.shape[:-3] + (TILES * 4 * width,))

    def small_vector(dcw, dhp, dgo, dgain):
        wide = jnp.concatenate([all_lanes(dcw[:5, :inner_width], LANES), dcw[:5, inner_width:]], 1)
        dskip = jnp.sum(dcw[5, :inner_width].reshape(heads, P_SIZE), axis=1)
        dgo = dgo[0].reshape(8, D // 8)[place].reshape(D) / gain_outer
        parts = [
            wide.reshape(-1),
            all_lanes(dhp[0, :heads], 2),
            all_lanes(dhp[1, :heads], 2),
            all_lanes(dskip, 2),
            dgo,
            all_lanes(dgain[0], LANES),
        ]
        flat = jnp.concatenate(parts)
        return jnp.pad(flat, (0, -flat.shape[0] % 1024)).reshape(-1, LANES)

    width = in_weight.shape[1]
    back = functools.partial(scan_backward, bounds, proj, cw, hp, scan, dscan)
    final = functools.partial(normed_gradient, w_rest=w_rest, dgate=dgate, w_two=w_two, normed=all_normed)
    if ring:
        steps = ring_sum([jnp.concatenate(p, 0) for p in zip(split(grad_gate), split(grad_out))])
        sent = next(steps)
        branch = mm(inner, w_out).astype(BF)
        *sent, branch = tie(*sent, branch)
        b0, b1, b2, b3 = blocks_of(branch)
        sent = steps.send(sent)
        far = swap(b3, 1)
        gproj, dcw, dhp = back(0, 1)
        *sent, far, gproj = tie(*sent, far, gproj)
        sent = steps.send(sent)
        core, chip = swap(b1, 1), swap((b2.astype(F32) + far.astype(F32)).astype(BF), 2)
        gproj, d, e = back(1, 1, gproj)
        dcw, dhp = dcw + d, dhp + e
        gproj, d, e = back(2, 1, gproj)
        dcw, dhp = dcw + d, dhp + e
        *sent, gproj = tie(*sent, gproj)
        sent = steps.send(sent)
        gproj, d, e = back(3, 1, gproj)
        dcw, dhp = dcw + d, dhp + e
        *sent, gproj, core, chip = tie(*sent, gproj, core, chip)
        share = steps.send(sent)
        layer_out = (keep * (tokens.astype(F32) + b0.astype(F32) + core.astype(F32) + chip.astype(F32))).astype(BF)

        gates = [share, swap(share, 1), swap(share, 2)]
        grad_rest = lax.dot_general(gproj, all_normed, TN, preferred_element_type=F32).astype(BF)
        steps = ring_sum(split(grad_rest))
        sent = next(steps)
        grad3, dgo = final(gproj, first=3, count=1)
        *sent, grad3 = tie(*sent, grad3)
        sent = steps.send(sent)
        far = swap(grad3, 1)
        grad2, d = final(gproj, first=2, count=1)
        dgo = dgo + d
        far, grad2, gates[2], layer_out = tie(far, grad2, gates[2], layer_out)
        chip = swap((grad2.astype(F32) + far.astype(F32)).astype(BF), 2)
        grad1, d = final(gproj, first=1, count=1)
        dgo = dgo + d
        *sent, grad1 = tie(*sent, grad1)
        sent = steps.send(sent)
        core = swap(grad1, 1)
        gates.append(swap(gates[2], 1))
        grad0, d = final(gproj, first=0, count=1)
        dgo = dgo + d
        *sent, core, gates[3], grad0 = tie(*sent, core, gates[3], grad0)
        sent = steps.send(sent)
        grad_in, grad_out_weight = first_join(r[None], gates, width)
        small = small_vector(dcw, dhp, dgo, dgain)
        small = small + swap(small, 1)
        *sent, grad_in, small = tie(*sent, grad_in, small)
        share = steps.send(sent)
        rests = [share, swap(share, 1), swap(share, 2)]
        d = 1
        while d < n:
            small = small + lax.ppermute(small, "shard", [(i, i ^ d) for i in range(n)])
            d *= 2
        chip, small = tie(chip, small)
        small = small + swap(small, 2)
        rests.append(swap(rests[2], 1))
        parts = [grad0, core, chip]
        grad_tokens = last_rows(perm, tokens, cotangent, keep, gain_outer[None, :], parts)
    else:
        everyone = lambda x: [x, swap(x, 1), swap(x, 2), swap(x, 3)]
        rows_sum = lambda x: lax.psum_scatter(x.astype(F32), "shard", scatter_dimension=1, tiled=True).astype(BF)
        branch = mm(inner, w_out).astype(BF)
        gproj, dcw, dhp = back(0, 4)
        layer_out = (keep * (tokens.astype(F32) + sum_rep(blocks_of(branch)))).astype(BF)
        grad_rest = lax.dot_general(gproj, all_normed, TN, preferred_element_type=F32).astype(BF)
        gnormed, dgo = final(gproj, first=0, count=4)
        total = sum_rep(blocks_of(gnormed)).astype(BF)
        grad_tokens = last_rows(
            perm, tokens, cotangent, keep, gain_outer[None, :], [total, jnp.zeros_like(total), jnp.zeros_like(total)]
        )
        spread = grad_out.reshape(8, LANES, 8, 256).transpose(2, 1, 0, 3).reshape(TILES, 1, LANES, D).astype(F32)
        spread = spread * (jnp.arange(4)[None, :, None, None] == r)
        spread = lax.psum_scatter(spread.reshape(DIN, D), "shard", scatter_dimension=0, tiled=True)
        grad_out_weight = lax.psum(spread, "rep")
        gates = everyone(jnp.pad(rows_sum(grad_gate), ((0, inner_width), (0, 0))))
        rests = everyone(rows_sum(grad_rest))
        grad_in, _ = first_join(r[None], gates, width)
        small = lax.psum(small_vector(dcw, dhp, dgo, dgain), ("rep", "shard"))
    grad_in_weight = last_join(r[None], rests, grad_in).T

    small = small.reshape(-1)
    ends = [sum(sizes[: i + 1]) for i in range(len(sizes))]
    g_cw, g_cb, g_db, g_al, g_sk, g_go, g_gi = [small[e - z : e] for e, z in zip(ends, sizes)]
    return (
        layer_out,
        grad_tokens,
        grad_in_weight,
        grad_out_weight,
        g_cw.reshape(4, CONVCH),
        g_cb,
        g_db,
        g_al,
        g_sk,
        g_go,
        g_gi,
    )


def solution(mesh):
    rows = P(("rep", "shard"), None)
    vector = P(("rep", "shard"))
    owned = P("shard", None)
    return jax.shard_map(
        functools.partial(shards, mesh.shape["shard"]),
        mesh=mesh,
        in_specs=(rows, rows, P(), vector, vector, owned, owned) + (P(),) * 7,
        out_specs=(rows, rows, owned, owned) + (P(),) * 7,
        check_vma=False,
    )
```

time: 893 us -> 559 us (0.63)
  waiting for transfers between devices: 319 us -> 78.3 us
  matrix products: 153 us -> 40.1 us
  Pallas kernels: 191 us -> 267 us
  starting transfers between devices: 81 us -> 53.8 us
  local copies, waits for them, and re-layouts: 80.5 us -> 57.4 us
  between operations: 16.8 us -> 3.27 us
    psum x1 -> x0, waiting for transfers between devices: 119 us -> none  [shards(): small = lax.psum(jnp.concatenate(small), ('rep', 'shard'))]
    ppermute x48 -> x35, waiting for transfers between devices: 164 us -> 47.9 us  [the longest x16 30.1 us: fw(): lax.ppermute(x, 'shard', [(RING[i], RING[(i + 1) % 8]) for i in range(8)])]
    pallas_call x7 -> x17, Pallas kernels: 183 us -> 257 us  [the longest x4 85.4 us: scan_backward(): pl.pallas_call(bwd_kernel if into is None else bwd_into, out_shape=(jax.S...]
    dot_general x3 -> x1, matrix products: 59.2 us -> 13.5 us  [mm_nt(): return lax.dot_general(a, b, NT, preferred_element_type=F32)]
    dot_general x3 -> x1, matrix products: 44.7 us -> 10.8 us  [mm(): return jnp.dot(a, b, preferred_element_type=F32)]
    dot_general x3 -> x1, matrix products: 49.2 us -> 15.8 us  [shards(): lax.dot_general(gproj, all_normed, TN, preferred_element_type=F32)]
    ppermute x48 -> x35, starting transfers between devices: 61.7 us -> 40.9 us  [the longest x16 19.9 us: bw(): lax.ppermute(x, 'shard', [(RING[(i + 1) % 8], RING[i]) for i in range(8)])]
    unnamed x135 -> x108, local copies, waits for them, and re-layouts: 47.1 us -> 28.5 us
  transfers between devices with their start and end apart: 76 -> 61, of which waited for: 31 -> 21; matrix products, arithmetic and copies ran while one was open for 22% -> 19% of each run, Pallas kernels for 7% -> 34%
where the time goes in v2:
time: 559 us; the launch traced here: 550 us
  Pallas kernels  267 us (48%)
  waiting for transfers between devices  78.3 us (14%)
  local copies, waits for them, and re-layouts  57.4 us (10%)
  starting transfers between devices  53.8 us (10%)
  other arithmetic  51 us (9%)
  matrix products  40.1 us (7%)
    pallas_call x4, Pallas kernels, scan_backward(): pl.pallas_call(bwd_kernel if into is None else bwd_into, out_shape=(jax.S...  85.4 us
    pallas_call x2, Pallas kernels, scan_forward(): pl.pallas_call(fwd_kernel if into is None else fwd_into, out_shape=jax.Sh...  45.5 us
    pallas_call x4, Pallas kernels, normed_gradient(): pl.pallas_call(back_kernel, out_shape=(jax.ShapeDtypeStruct((count * TOK,...  43 us
    ppermute x26, waiting for transfers between devices, swap(): return lax.ppermute(x, 'rep', [(i, i ^ d) for i in range(4)])  30.4 us
    ppermute x16, waiting for transfers between devices, fw(): lax.ppermute(x, 'shard', [(RING[i], RING[(i + 1) % 8]) for i in range(8)])  30.1 us
    unnamed x108, local copies, waits for them, and re-layouts  28.5 us
    pallas_call x2, Pallas kernels, across_rows(): pl.pallas_call(across_kernel, out_shape=jax.ShapeDtypeStruct((m, n), BF),...  28.2 us
    ppermute x16, starting transfers between devices, bw(): lax.ppermute(x, 'shard', [(RING[(i + 1) % 8], RING[i]) for i in range(8)])  19.9 us
  transfers between devices with their start and end apart: 61, of which 21 were waited for; matrix products, arithmetic and copies ran while one was open for 19% of the time, Pallas kernels for 34%

profile of v2, /device:TPU:0, one launch (start us, length us, event | category | flops | bytes accessed | tf_op | source)
XLA Modules:
  0.0 550.5 jit_solution(1364415572407285732)
XLA Ops:
  35.4 10.7 %collective-permute-done.2 = bf16[1296,256]{1,0:T(8,128)(2,1)} collective-permute-done((bf16[1296,256]{1,0:T(8,128)(2,1)S(1)}, bf16[1296,256]{1,0:T(8,128)(2,1)}, u32[]{:S(2)}, u32[]{:S(2)}) %collective-permute-start.2) | collective-permute-done | bytes 663584 | tf_op jit(solution)/shard_map/ppermute | solution.py:747
  54.5 7.5 %collective-permute-done.4 = bf16[1296,256]{1,0:T(8,128)(2,1)S(1)} collective-permute-done((bf16[1296,256]{1,0:T(8,128)(2,1)}, bf16[1296,256]{1,0:T(8,128)(2,1)S(1)}, u32[]{:S(2)}, u32[]{:S(2)}) %collective-permute-start.4) | collective-permute-done | bytes 663584 | tf_op jit(solution)/shard_map/ppermute | solution.py:747
  89.6 13.5 %convolution_convert_fusion.1.xs_ref.bc_ref.dt_ref.refs_0_.refs_1_.refs_2_ = bf16[2048,1296]{1,0:T(8,128)(2,1)S(1)} fusion(bf16[2048,2048]{1,0:T(8,128)(2,1)S(1)} %pad_maximum_fusion.norm_ref.b_ref, bf16[1296,2048]{1,0:T(8,128)(2,1)S(1)} %bitcast.65), kind=kOutput, calls=%fused_computation.4 | convolution fusion | flops 10874290176 | bytes 19005440 | tf_op jit(solution)/shard_map/dot_general | solution.py:37
  108.0 22.7 %shard_map.240.refs_6_ = f32[2048,1024]{1,0:T(8,128)} custom-call(s32[2,2]{1,0:T(2,128)S(1)} %pad_add_fusion.bnd, bf16[2048,1296]{1,0:T(8,128)(2,1)S(1)} %convolution_convert_fusion.1.xs_ref.bc_ref.dt_ref.refs_0_.refs_1_.refs_2_, bf16[2048,1296]{1,0:T(8,128)(2,1)S(1)} %convolution_convert_fusion.1.xs_ref.bc_ref.dt_ref.refs_0_.refs_1_.refs_2_, ...), custom_call_target="tpu_custom_call" | custom-call | flops 16000000000 | bytes 8000000 | tf_op jit(solution)/shard_map/pallas_call | solution.py:353
  138.4 22.7 %shard_map.241.scan_ref.refs_6_ = f32[2048,1024]{1,0:T(8,128)} custom-call(s32[2,2]{1,0:T(2,128)S(1)} %pad_add_fusion.1.bnd, bf16[2048,1296]{1,0:T(8,128)(2,1)S(1)} %convolution_convert_fusion.1.xs_ref.bc_ref.dt_ref.refs_0_.refs_1_.refs_2_, ...), custom_call_target="tpu_custom_call", output_to_operand_aliasing={{}: (7, {})} | custom-call | flops 16000000000 | bytes 8000000 | tf_op jit(solution)/shard_map/pallas_call | solution.py:353
  163.4 6.6 %pad_maximum_fusion.1.gout_ref.b_ref = bf16[2048,2048]{1,0:T(8,128)(2,1)} fusion(bf16[512,2048]{1,0:T(8,128)(2,1)S(1)} %collective-permute-done.24, bf16[512,2048]{1,0:T(8,128)(2,1)} %collective-permute-done.23, bf16[512,2048]{1,0:T(8,128)(2,1)} %collective-permute-done.22, bf16[512,2048]{1,0:T(8,128)(2,1)} %multiply_convert_fusion.1), kind=kLoop, calls=%fused_computation.2 | loop fusion | flops 33554432 | bytes 16777216 | tf_op jit(solution)/shard_map/concatenate | solution.py:886
  176.5 12.9 %shard_map.242 = (bf16[2048,1024]{1,0:T(8,128)(2,1)S(1)}, bf16[1024,2048]{1,0:T(8,128)(2,1)}) custom-call(bf16[2048,2048]{1,0:T(8,128)(2,1)} %pad_maximum_fusion.1.gout_ref.b_ref, bf16[2048,2048]{1,0:T(8,128)(2,1)} %maximum_dynamic-update-slice_fusion.w_ref.wb_ref), custom_call_target="tpu_custom_call" | custom-call | flops 8589934592 | bytes 20971520 | tf_op jit(solution)/shard_map/pallas_call | solution.py:413
  191.5 17.3 %shard_map.243 = (bf16[2048,1024]{1,0:T(8,128)(2,1)S(1)}, f32[4,8,512]{2,1,0:T(8,128)S(1)}) custom-call(s32[8]{0:T(128)S(1)} %fusion.6.place, bf16[2048,2048]{1,0:T(8,128)(2,1)} %copy-done.20, bf16[2048,2048]{1,0:T(8,128)(2,1)} %maximum_dynamic-update-slice_fusion.w_ref.wb_ref, f32[2048,1024]{1,0:T(8,128)} %shard_map.241.scan_ref.refs_6_, ...), custom_call_target="tpu_custom_call" | custom-call | flops 8589934592 | bytes 29360128 | tf_op jit(solution)/shard_map/pallas_call | solution.py:445
  216.3 14.6 %shard_map.244 = (bf16[2048,1024]{1,0:T(8,128)(2,1)S(1)}, bf16[2048,1024]{1,0:T(8,128)(2,1)}, bf16[2048,1024]{1,0:T(8,128)(2,1)}, f32[8,1024]{1,0:T(8,128)S(1)}) custom-call(s32[8]{0:T(128)S(1)} %fusion.6.place, f32[4,8,512]{2,1,0:T(8,128)S(1)} %pad_maximum_fusion.9.sum_ref, f32[2048,1024]{1,0:T(8,128)} %shard_map.241.scan_ref.refs_6_, ...), custom_call_target="tpu_custom_call" | custom-call | bytes 29360128 | tf_op jit(solution)/shard_map/pallas_call | solution.py:498
  232.9 13.9 %shard_map.246 = bf16[1024,2048]{1,0:T(8,128)(2,1)S(1)} custom-call(bf16[2048,1024]{1,0:T(8,128)(2,1)} %copy-done.17, bf16[2048,2048]{1,0:T(8,128)(2,1)} %pad_maximum_fusion.1.gout_ref.b_ref), custom_call_target="tpu_custom_call" | custom-call | flops 8589934592 | bytes 16777216 | tf_op jit(solution)/shard_map/pallas_call | solution.py:570
  248.4 14.3 %shard_map.245 = bf16[1024,2048]{1,0:T(8,128)(2,1)S(1)} custom-call(bf16[2048,1024]{1,0:T(8,128)(2,1)} %get-tuple-element.131.a_ref.b_ref, bf16[2048,2048]{1,0:T(8,128)(2,1)} %copy-done.20), custom_call_target="tpu_custom_call" | custom-call | flops 8589934592 | bytes 16777216 | tf_op jit(solution)/shard_map/pallas_call | solution.py:570
  266.8 10.8 %convolution_convert_fusion = bf16[2048,2048]{1,0:T(8,128)(2,1)S(1)} fusion(bf16[2048,1024]{1,0:T(8,128)(2,1)S(1)} %copy-done.18, bf16[1024,2048]{1,0:T(8,128)(2,1)} %get-tuple-element.133), kind=kOutput, calls=%fused_computation.3 | convolution fusion | flops 8594128896 | bytes 16777216 | tf_op jit(solution)/shard_map/dot_general | solution.py:33
  285.6 21.4 %shard_map.247 = (bf16[2048,1296]{1,0:T(8,128)(2,1)}, f32[8,1280]{1,0:T(8,128)S(1)}, f32[8,128]{1,0:T(8,128)S(1)}) custom-call(s32[1,2]{1,0:T(1,128)S(1)} %add_bitcast_fusion.bnd, bf16[2048,1296]{1,0:T(8,128)(2,1)} %copy-done.19, bf16[2048,1296]{1,0:T(8,128)(2,1)} %copy-done.19, bf16[2048,1296]{1,0:T(8,128)(2,1)} %copy-done.19, ...), custom_call_target="tpu_custom_call" | custom-call | flops 16000000000 | bytes 6000000 | tf_op jit(solution)/shard_map/pallas_call | solution.py:375
  316.7 21.3 %shard_map.248 = (bf16[2048,1296]{1,0:T(8,128)(2,1)}, f32[8,1280]{1,0:T(8,128)S(1)}, f32[8,128]{1,0:T(8,128)S(1)}) custom-call(s32[1,2]{1,0:T(1,128)S(1)} %collective-permute-done.15.bnd, bf16[2048,1296]{1,0:T(8,128)(2,1)} %copy-done.19, bf16[2048,1296]{1,0:T(8,128)(2,1)} %copy-done.19, ...), custom_call_target="tpu_custom_call", output_to_operand_aliasing={{0}: (9, {})} | custom-call | flops 16000000000 | bytes 6000000 | tf_op jit(solution)/shard_map/pallas_call | solution.py:375
  338.1 21.3 %shard_map.249 = (bf16[2048,1296]{1,0:T(8,128)(2,1)}, f32[8,1280]{1,0:T(8,128)S(1)}, f32[8,128]{1,0:T(8,128)S(1)}) custom-call(s32[1,2]{1,0:T(1,128)S(1)} %collective-permute-done.18.bnd, bf16[2048,1296]{1,0:T(8,128)(2,1)} %copy-done.19, bf16[2048,1296]{1,0:T(8,128)(2,1)} %copy-done.19, ...), custom_call_target="tpu_custom_call", output_to_operand_aliasing={{0}: (9, {})} | custom-call | flops 16000000000 | bytes 6000000 | tf_op jit(solution)/shard_map/pallas_call | solution.py:375
  364.4 21.4 %shard_map.250 = (bf16[2048,1296]{1,0:T(8,128)(2,1)}, f32[8,1280]{1,0:T(8,128)S(1)}, f32[8,128]{1,0:T(8,128)S(1)}) custom-call(s32[1,2]{1,0:T(1,128)S(1)} %collective-permute-done.19.bnd, bf16[2048,1296]{1,0:T(8,128)(2,1)} %copy-done.19, bf16[2048,1296]{1,0:T(8,128)(2,1)} %copy-done.19, ...), custom_call_target="tpu_custom_call", output_to_operand_aliasing={{0}: (9, {})} | custom-call | flops 16000000000 | bytes 6000000 | tf_op jit(solution)/shard_map/pallas_call | solution.py:375
  387.1 15.8 %convolution_convert_fusion.2 = bf16[1296,2048]{1,0:T(8,128)(2,1)S(1)} fusion(bf16[2048,1296]{1,0:T(8,128)(2,1)} %get-tuple-element.150.a_ref, bf16[2048,2048]{1,0:T(8,128)(2,1)} %copy-done.20), kind=kOutput, calls=%fused_computation.5 | convolution fusion | flops 10874290176 | bytes 19005440 | tf_op jit(solution)/shard_map/dot_general | solution.py:949
  408.7 10.7 %shard_map.251 = (bf16[512,2048]{1,0:T(8,128)(2,1)S(1)}, f32[8,2048]{1,0:T(8,128)S(1)}) custom-call(bf16[2048,1296]{1,0:T(8,128)(2,1)} %get-tuple-element.150.a_ref, bf16[1296,2048]{1,0:T(8,128)(2,1)} %maximum_dynamic-update-slice_fusion.1.wa_ref, bf16[2048,1024]{1,0:T(8,128)(2,1)} %get-tuple-element.131.a_ref.b_ref, ...), custom_call_target="tpu_custom_call" | custom-call | flops 4865392640 | bytes 9502720 | tf_op jit(solution)/shard_map/pallas_call | solution.py:533
  422.0 6.3 %multiply_convert_fusion = bf16[512,2048]{1,0:T(8,128)(2,1)} fusion(bf16[512,2048]{1,0:T(8,128)(2,1)} %collective-permute-done.38, bf16[512,2048]{1,0:T(8,128)(2,1)} %collective-permute-done.37, bf16[512,2048]{1,0:T(8,128)(2,1)S(1)} %copy-done.2, bf16[2048,2048]{1,0:T(8,128)(2,1)} %copy-done.21, f32[512]{0:T(512)S(1)} %copy-done.36), kind=kLoop, calls=%fused_computation.7 | loop fusion | flops 9437184 | bytes 10487808 | tf_op jit(solution)/shard_map/convert_element_type | solution.py:946
  428.2 10.7 %shard_map.253 = (bf16[512,2048]{1,0:T(8,128)(2,1)S(1)}, f32[8,2048]{1,0:T(8,128)S(1)}) custom-call(bf16[2048,1296]{1,0:T(8,128)(2,1)} %get-tuple-element.150.a_ref, bf16[1296,2048]{1,0:T(8,128)(2,1)} %maximum_dynamic-update-slice_fusion.1.wa_ref, bf16[2048,1024]{1,0:T(8,128)(2,1)} %get-tuple-element.131.a_ref.b_ref, ...), custom_call_target="tpu_custom_call" | custom-call | flops 4865392640 | bytes 9502720 | tf_op jit(solution)/shard_map/pallas_call | solution.py:533
  439.8 10.7 %shard_map.252 = (bf16[512,2048]{1,0:T(8,128)(2,1)S(1)}, f32[8,2048]{1,0:T(8,128)S(1)}) custom-call(bf16[2048,1296]{1,0:T(8,128)(2,1)} %get-tuple-element.150.a_ref, bf16[1296,2048]{1,0:T(8,128)(2,1)} %maximum_dynamic-update-slice_fusion.1.wa_ref, bf16[2048,1024]{1,0:T(8,128)(2,1)} %get-tuple-element.131.a_ref.b_ref, ...), custom_call_target="tpu_custom_call" | custom-call | flops 4865392640 | bytes 9502720 | tf_op jit(solution)/shard_map/pallas_call | solution.py:533
  455.5 11.0 %shard_map.254 = (bf16[512,2048]{1,0:T(8,128)(2,1)S(1)}, f32[8,2048]{1,0:T(8,128)S(1)}) custom-call(bf16[2048,1296]{1,0:T(8,128)(2,1)} %get-tuple-element.150.a_ref, bf16[1296,2048]{1,0:T(8,128)(2,1)} %maximum_dynamic-update-slice_fusion.1.wa_ref, bf16[2048,1024]{1,0:T(8,128)(2,1)} %get-tuple-element.131.a_ref.b_ref, ...), custom_call_target="tpu_custom_call" | custom-call | flops 4865392640 | bytes 9502720 | tf_op jit(solution)/shard_map/pallas_call | solution.py:533
  507.9 25.4 %collective-permute-done.58.three = bf16[1296,256]{1,0:T(8,128)(2,1)} collective-permute-done((bf16[1296,256]{1,0:T(8,128)(2,1)S(1)}, bf16[1296,256]{1,0:T(8,128)(2,1)}, u32[]{:S(2)}, u32[]{:S(2)}) %collective-permute-start.58) | collective-permute-done | bytes 663584 | tf_op jit(solution)/shard_map/ppermute | solution.py:743
  535.9 7.1 %shard_map.256 = f32[512,2048]{1,0:T(8,128)} custom-call(s32[8]{0:T(128)S(1)} %copy-done.15, bf16[512,2048]{1,0:T(8,128)(2,1)S(1)} %copy-done.2, bf16[512,2048]{1,0:T(8,128)(2,1)S(1)} %copy-done.4, f32[512,1]{1,0:T(8,128)S(1)} %copy.45.keep_ref, f32[1,2048]{1,0:T(1,128)S(1)} %bitcast.63, bf16[512,2048]{1,0:T(8,128)(2,1)} %copy-done.7, ...), custom_call_target="tpu_custom_call" | custom-call | bytes 14680064 | tf_op jit(solution)/shard_map/pallas_call | solution.py:631
  (348 shorter events, 196.7 us)
Async XLA Ops:
  17.5 57.1 %collective-permute-start.8 = (bf16[512,2048]{1,0:T(8,128)(2,1)}, bf16[512,2048]{1,0:T(8,128)(2,1)}, u32[]{:S(2)}, u32[]{:S(2)}) collective-permute-start(bf16[512,2048]{1,0:T(8,128)(2,1)} %shard_map.239), channel_id=1, source_target_pairs={{0,8},{8,0},{16,24},{24,16},{1,9},{9,1},{17,25},{25,17},{2,10},{10... | collective-permute-start | bytes 6291464 | tf_op jit(solution)/shard_map/ppermute | solution.py:743
  17.5 57.1 %collective-permute-start.9 = (bf16[512,2048]{1,0:T(8,128)(2,1)}, bf16[512,2048]{1,0:T(8,128)(2,1)}, u32[]{:S(2)}, u32[]{:S(2)}) collective-permute-start(bf16[512,2048]{1,0:T(8,128)(2,1)} %shard_map.239), channel_id=1, source_target_pairs={{0,16},{8,24},{16,0},{24,8},{1,17},{9,25},{17,1},{25,9},{2,18},{10... | collective-permute-start | bytes 6291464 | tf_op jit(solution)/shard_map/ppermute | solution.py:743
  22.3 57.5 %collective-permute-start.15 = (s32[1,2]{1,0:T(1,128)S(1)}, s32[1,2]{1,0:T(1,128)S(1)}, u32[]{:S(2)}, u32[]{:S(2)}) collective-permute-start(s32[1,2]{1,0:T(1,128)S(1)} %add_bitcast_fusion.bnd), channel_id=1, source_target_pairs={{0,8},{8,0},{16,24},{24,16},{1,9},{9,1},{17,25},{25,17},{2,10},{10... | collective-permute-start | bytes 32 | tf_op jit(solution)/shard_map/ppermute | solution.py:743
  81.9 48.8 %collective-permute-start.23 = (bf16[512,2048]{1,0:T(8,128)(2,1)}, bf16[512,2048]{1,0:T(8,128)(2,1)}, u32[]{:S(2)}, u32[]{:S(2)}) collective-permute-start(bf16[512,2048]{1,0:T(8,128)(2,1)} %multiply_convert_fusion.1), channel_id=1, source_target_pairs={{0,16},{8,24},{16,0},{24,8},{1,17},{9,25},{17,1},{25,9},{2,18},{10... | collective-permute-start | bytes 6291464 | tf_op jit(solution)/shard_map/ppermute | solution.py:743
  83.4 80.0 %collective-permute-start.22 = (bf16[512,2048]{1,0:T(8,128)(2,1)}, bf16[512,2048]{1,0:T(8,128)(2,1)}, u32[]{:S(2)}, u32[]{:S(2)}) collective-permute-start(bf16[512,2048]{1,0:T(8,128)(2,1)} %multiply_convert_fusion.1), channel_id=1, source_target_pairs={{0,8},{8,0},{16,24},{24,16},{1,9},{9,1},{17,25},{25,17},{2,10},{10... | collective-permute-start | bytes 6291464 | tf_op jit(solution)/shard_map/ppermute | solution.py:743
  105.8 28.4 %collective-permute-start.13 = (bf16[2048,256]{1,0:T(8,128)(2,1)S(1)}, bf16[2048,256]{1,0:T(8,128)(2,1)S(1)}, u32[]{:S(2)}, u32[]{:S(2)}) collective-permute-start(bf16[2048,256]{1,0:T(8,128)(2,1)S(1)} %collective-permute-done.11), channel_id=1, source_target_pairs={{0,2},{2,4},{4,6},{6,7},{7,5},{5,3},{3,1},{1,0},{8,10},{10,12},{12... | collective-permute-start | bytes 3145736 | tf_op jit(solution)/shard_map/ppermute | solution.py:747
  106.3 27.8 %collective-permute-start.14 = (bf16[2048,256]{1,0:T(8,128)(2,1)}, bf16[2048,256]{1,0:T(8,128)(2,1)S(1)}, u32[]{:S(2)}, u32[]{:S(2)}) collective-permute-start(bf16[2048,256]{1,0:T(8,128)(2,1)} %collective-permute-done.12), channel_id=1, source_target_pairs={{2,0},{4,2},{6,4},{7,6},{5,7},{3,5},{1,3},{0,1},{10,8},{12,10},{14... | collective-permute-start | bytes 3145736 | tf_op jit(solution)/shard_map/ppermute | solution.py:751
  130.7 32.7 %collective-permute-start.24 = (bf16[512,2048]{1,0:T(8,128)(2,1)}, bf16[512,2048]{1,0:T(8,128)(2,1)S(1)}, u32[]{:S(2)}, u32[]{:S(2)}) collective-permute-start(bf16[512,2048]{1,0:T(8,128)(2,1)} %collective-permute-done.23), channel_id=1, source_target_pairs={{0,8},{8,0},{16,24},{24,16},{1,9},{9,1},{17,25},{25,17},{2,10},{10... | collective-permute-start | bytes 6291464 | tf_op jit(solution)/shard_map/ppermute | solution.py:743
  134.1 27.0 %collective-permute-start.16 = (bf16[2048,256]{1,0:T(8,128)(2,1)S(1)}, bf16[2048,256]{1,0:T(8,128)(2,1)S(1)}, u32[]{:S(2)}, u32[]{:S(2)}) collective-permute-start(bf16[2048,256]{1,0:T(8,128)(2,1)S(1)} %collective-permute-done.13), channel_id=1, source_target_pairs={{0,2},{2,4},{4,6},{6,7},{7,5},{5,3},{3,1},{1,0},{8,10},{10,12},{12... | collective-permute-start | bytes 3145736 | tf_op jit(solution)/shard_map/ppermute | solution.py:747
  134.7 26.4 %collective-permute-start.17 = (bf16[2048,256]{1,0:T(8,128)(2,1)S(1)}, bf16[2048,256]{1,0:T(8,128)(2,1)S(1)}, u32[]{:S(2)}, u32[]{:S(2)}) collective-permute-start(bf16[2048,256]{1,0:T(8,128)(2,1)S(1)} %collective-permute-done.14), channel_id=1, source_target_pairs={{2,0},{4,2},{6,4},{7,6},{5,7},{3,5},{1,3},{0,1},{10,8},{12,10},{14... | collective-permute-start | bytes 3145736 | tf_op jit(solution)/shard_map/ppermute | solution.py:751
  282.2 27.2 %collective-permute-start.32 = (bf16[512,2048]{1,0:T(8,128)(2,1)}, bf16[512,2048]{1,0:T(8,128)(2,1)S(1)}, u32[]{:S(2)}, u32[]{:S(2)}) collective-permute-start(bf16[512,2048]{1,0:T(8,128)(2,1)} %get-tuple-element.200), channel_id=1, source_target_pairs={{0,8},{8,0},{16,24},{24,16},{1,9},{9,1},{17,25},{25,17},{2,10},{10... | collective-permute-start | bytes 6291464 | tf_op jit(solution)/shard_map/ppermute | solution.py:743
  283.2 25.8 %collective-permute-start.30 = (bf16[2048,256]{1,0:T(8,128)(2,1)}, bf16[2048,256]{1,0:T(8,128)(2,1)S(1)}, u32[]{:S(2)}, u32[]{:S(2)}) collective-permute-start(bf16[2048,256]{1,0:T(8,128)(2,1)} %pad_maximum_fusion.3), channel_id=1, source_target_pairs={{0,2},{2,4},{4,6},{6,7},{7,5},{5,3},{3,1},{1,0},{8,10},{10,12},{12... | collective-permute-start | bytes 3145736 | tf_op jit(solution)/shard_map/ppermute | solution.py:747
  307.0 80.1 %collective-permute-start.37 = (bf16[512,2048]{1,0:T(8,128)(2,1)}, bf16[512,2048]{1,0:T(8,128)(2,1)}, u32[]{:S(2)}, u32[]{:S(2)}) collective-permute-start(bf16[512,2048]{1,0:T(8,128)(2,1)} %get-tuple-element.199), channel_id=1, source_target_pairs={{0,8},{8,0},{16,24},{24,16},{1,9},{9,1},{17,25},{25,17},{2,10},{10... | collective-permute-start | bytes 6291464 | tf_op jit(solution)/shard_map/ppermute | solution.py:743
  309.7 49.7 %collective-permute-start.33 = (bf16[2048,256]{1,0:T(8,128)(2,1)S(1)}, bf16[2048,256]{1,0:T(8,128)(2,1)S(1)}, u32[]{:S(2)}, u32[]{:S(2)}) collective-permute-start(bf16[2048,256]{1,0:T(8,128)(2,1)S(1)} %add_convert_fusion.6), channel_id=1, source_target_pairs={{0,2},{2,4},{4,6},{6,7},{7,5},{5,3},{3,1},{1,0},{8,10},{10,12},{12... | collective-permute-start | bytes 3145736 | tf_op jit(solution)/shard_map/ppermute | solution.py:747
  310.4 49.0 %collective-permute-start.34 = (bf16[2048,256]{1,0:T(8,128)(2,1)S(1)}, bf16[2048,256]{1,0:T(8,128)(2,1)S(1)}, u32[]{:S(2)}, u32[]{:S(2)}) collective-permute-start(bf16[2048,256]{1,0:T(8,128)(2,1)S(1)} %add_convert_fusion.5), channel_id=1, source_target_pairs={{2,0},{4,2},{6,4},{7,6},{5,7},{3,5},{1,3},{0,1},{10,8},{12,10},{14... | collective-permute-start | bytes 3145736 | tf_op jit(solution)/shard_map/ppermute | solution.py:751
  316.0 71.1 %collective-permute-start.38 = (bf16[512,2048]{1,0:T(8,128)(2,1)}, bf16[512,2048]{1,0:T(8,128)(2,1)}, u32[]{:S(2)}, u32[]{:S(2)}) collective-permute-start(bf16[512,2048]{1,0:T(8,128)(2,1)} %add_convert_fusion.1), channel_id=1, source_target_pairs={{0,16},{8,24},{16,0},{24,8},{1,17},{9,25},{17,1},{25,9},{2,18},{10... | collective-permute-start | bytes 6291464 | tf_op jit(solution)/shard_map/ppermute | solution.py:743
  360.7 26.4 %collective-permute-start.35 = (bf16[2048,256]{1,0:T(8,128)(2,1)}, bf16[2048,256]{1,0:T(8,128)(2,1)}, u32[]{:S(2)}, u32[]{:S(2)}) collective-permute-start(bf16[2048,256]{1,0:T(8,128)(2,1)} %add_convert_fusion.4), channel_id=1, source_target_pairs={{0,2},{2,4},{4,6},{6,7},{7,5},{5,3},{3,1},{1,0},{8,10},{10,12},{12... | collective-permute-start | bytes 3145736 | tf_op jit(solution)/shard_map/ppermute | solution.py:747
  407.3 48.1 %collective-permute-start.42 = (bf16[2048,256]{1,0:T(8,128)(2,1)S(1)}, bf16[2048,256]{1,0:T(8,128)(2,1)S(1)}, u32[]{:S(2)}, u32[]{:S(2)}) collective-permute-start(bf16[2048,256]{1,0:T(8,128)(2,1)S(1)} %add_convert_fusion.2.one), channel_id=1, source_target_pairs={{0,16},{8,24},{16,0},{24,8},{1,17},{9,25},{17,1},{25,9},{2,18},{10... | collective-permute-start | bytes 3145736 | tf_op jit(solution)/shard_map/ppermute | solution.py:743
  419.4 36.0 %collective-permute-start.41 = (bf16[512,2048]{1,0:T(8,128)(2,1)S(1)}, bf16[512,2048]{1,0:T(8,128)(2,1)}, u32[]{:S(2)}, u32[]{:S(2)}) collective-permute-start(bf16[512,2048]{1,0:T(8,128)(2,1)S(1)} %get-tuple-element.152), channel_id=1, source_target_pairs={{0,8},{8,0},{16,24},{24,16},{1,9},{9,1},{17,25},{25,17},{2,10},{10... | collective-permute-start | bytes 6291464 | tf_op jit(solution)/shard_map/ppermute | solution.py:743
  439.8 32.0 %collective-permute-start.47 = (bf16[512,2048]{1,0:T(8,128)(2,1)S(1)}, bf16[512,2048]{1,0:T(8,128)(2,1)}, u32[]{:S(2)}, u32[]{:S(2)}) collective-permute-start(bf16[512,2048]{1,0:T(8,128)(2,1)S(1)} %get-tuple-element.164), channel_id=1, source_target_pairs={{0,8},{8,0},{16,24},{24,16},{1,9},{9,1},{17,25},{25,17},{2,10},{10... | collective-permute-start | bytes 6291464 | tf_op jit(solution)/shard_map/ppermute | solution.py:743
  471.0 62.3 %collective-permute-start.49 = (bf16[512,2048]{1,0:T(8,128)(2,1)}, bf16[512,2048]{1,0:T(8,128)(2,1)}, u32[]{:S(2)}, u32[]{:S(2)}) collective-permute-start(bf16[512,2048]{1,0:T(8,128)(2,1)} %add_convert_fusion), channel_id=1, source_target_pairs={{0,16},{8,24},{16,0},{24,8},{1,17},{9,25},{17,1},{25,9},{2,18},{10... | collective-permute-start | bytes 6291464 | tf_op jit(solution)/shard_map/ppermute | solution.py:743
  494.2 39.1 %collective-permute-start.58 = (bf16[1296,256]{1,0:T(8,128)(2,1)S(1)}, bf16[1296,256]{1,0:T(8,128)(2,1)}, u32[]{:S(2)}, u32[]{:S(2)}) collective-permute-start(bf16[1296,256]{1,0:T(8,128)(2,1)S(1)} %add_convert_fusion.7.one), channel_id=1, source_target_pairs={{0,16},{8,24},{16,0},{24,8},{1,17},{9,25},{17,1},{25,9},{2,18},{10... | collective-permute-start | bytes 1990664 | tf_op jit(solution)/shard_map/ppermute | solution.py:743
  505.4 27.9 %collective-permute-start.56 = (f32[224,128]{1,0:T(8,128)S(1)}, f32[224,128]{1,0:T(8,128)S(1)}, u32[]{:S(2)}, u32[]{:S(2)}) collective-permute-start(f32[224,128]{1,0:T(8,128)S(1)} %add.241), channel_id=1, source_target_pairs={{0,4},{1,5},{2,6},{3,7},{4,0},{5,1},{6,2},{7,3},{8,12},{9,13},{10,... | collective-permute-start | bytes 344072 | tf_op jit(solution)/shard_map/ppermute | solution.py:978
  507.9 38.3 %collective-permute-start.57 = (bf16[1296,256]{1,0:T(8,128)(2,1)S(1)}, bf16[1296,256]{1,0:T(8,128)(2,1)}, u32[]{:S(2)}, u32[]{:S(2)}) collective-permute-start(bf16[1296,256]{1,0:T(8,128)(2,1)S(1)} %add_convert_fusion.7.one), channel_id=1, source_target_pairs={{0,8},{8,0},{16,24},{24,16},{1,9},{9,1},{17,25},{25,17},{2,10},{10... | collective-permute-start | bytes 1990664 | tf_op jit(solution)/shard_map/ppermute | solution.py:743
  (85 other events, 1214.8 us)

commit v3 on v2

v3 whole, which is shorter than its diff:
```python
import functools

import jax
import jax.numpy as jnp
from jax import lax
from jax.experimental import pallas as pl
from jax.experimental.pallas import tpu as pltpu
from jax.sharding import PartitionSpec as P

D = 2048
DIN = 4096
P_SIZE = 64
N = 128
Q = 256
H = 64
CONVCH = DIN + 2 * N
EPSILON = 1e-05
LOG2E = 1.4426950408889634
LANES = 128
TOK = 512
TILES = DIN // 128 // 4
HEADS = H // 4
REST = TILES * 128 + 2 * N + H // 4
HIGHEST = lax.Precision.HIGHEST
BF = jnp.bfloat16
F32 = jnp.float32
NT = (((1,), (1,)), ((), ()))
TN = (((0,), (0,)), ((), ()))
RING = (0, 2, 4, 6, 7, 5, 3, 1)


def mm(a, b):
    return jnp.dot(a, b, preferred_element_type=F32)


def mm_nt(a, b):
    return lax.dot_general(a, b, NT, preferred_element_type=F32)


def iota(shape, dim):
    return lax.broadcasted_iota(jnp.int32, shape, dim)


def start_of(rows, b1, b2):
    return jnp.where(rows >= b2, b2, jnp.where(rows >= b1, b1, 0))


def sigmoid(v):
    return 0.5 * jnp.tanh(0.5 * v) + 0.5


def conv_pre(x, taps, bias, lk):
    pre = bias + taps[3] * x
    for k in range(1, 4):
        pre = pre + taps[3 - k] * (pltpu.roll(x, k, 0) * lk[k - 1])
    return pre


def taps_of(cw_ref, lanes):
    return [cw_ref[k : k + 1, lanes] for k in range(4)], cw_ref[4:5, lanes]


def terms(v, count):
    out = []
    for _ in range(count):
        out.append(v.astype(BF).astype(F32))
        v = v - out[-1]
    return out


def side_by_side(parts):
    return sum(pltpu.roll(p, HEADS * i, 1) if i else p for i, p in enumerate(parts))


def prepare(b1, b2, bc_ref, dt_ref, cwb_ref, hp_ref, lk, score, bmat, cmat, btrans, ctrans,
            dts, sig, late, early, expand, transposed):
    rows = iota((TOK, LANES), 0)
    lane = iota((TOK, LANES), 1)
    pos = rows - start_of(rows, b1, b2)
    for k in range(1, 4):
        lk[k - 1] = (pos >= k).astype(F32)
    links = [lk[0], lk[1], lk[2]]
    for half, keep in ((0, bmat), (1, cmat)):
        lanes = slice(half * LANES, (half + 1) * LANES)
        taps, bias = taps_of(cwb_ref, lanes)
        pre = conv_pre(bc_ref[:, lanes].astype(F32), taps, bias, links)
        act = pre * sigmoid(pre)
        keep[...] = act.astype(BF)
        if half == 0:
            btrans[...] = act[:Q].T.astype(BF)
        elif ctrans is not None:
            ctrans[...] = act[Q:].T.astype(BF)
    for c in range(2):
        part = slice(c * Q, (c + 1) * Q)
        if transposed:
            s = mm_nt(bmat[part, :], cmat[part, :])
        else:
            s = mm_nt(cmat[part, :], bmat[part, :])
        score[c] = jnp.where(allowed(c, b1, b2, transposed), s, 0.0)
    real = lane < HEADS
    raw = jnp.where(real, dt_ref[...].astype(F32), 0.0) + hp_ref[0:1, :]
    step = jnp.where(real, jnp.maximum(raw, 0.0) + jnp.log1p(jnp.exp(-jnp.abs(raw))), 0.0)
    if dts is not None:
        dts[...] = step
        sig[...] = sigmoid(raw)
    decay = step * (hp_ref[1:2, :] * LOG2E)
    lower = (iota((Q, Q), 0) >= iota((Q, Q), 1)).astype(F32)
    sums = [
        jnp.dot(lower, decay[c * Q : (c + 1) * Q], precision=HIGHEST, preferred_element_type=F32) for c in range(2)
    ]
    last = start_of(Q - 1, b1, b2)
    out = jnp.where(rows[:Q] >= last, jnp.exp2(sums[0][Q - 1 : Q, :] - sums[0]), 0.0)
    into = jnp.where(start_of(rows[Q:], b1, b2) <= Q - 1, jnp.exp2(sums[1]), 0.0)
    middle = jnp.where(real, jnp.concatenate([out, into], 0), 0.0)
    expand[...] = side_by_side(terms(step, 2) + terms(middle, 2)).astype(BF)
    split = side_by_side(terms(jnp.concatenate(sums, 0), 3))
    used = lane % 64 < 3 * HEADS
    late[...] = jnp.where(used & (lane >= 64), 1.0, split).astype(BF)
    early[...] = jnp.where(used & (lane < 64), 1.0, pltpu.roll(-split, 64, 1)).astype(BF)


def both_heads(v, t):
    lane = iota(v.shape, 1) % HEADS
    zero = jnp.zeros_like(v)
    return jnp.concatenate([jnp.where(lane == 2 * t, v, zero), jnp.where(lane == 2 * t + 1, v, zero)], 0)


def spread_over(expand, t):
    row, col = iota((LANES, 2 * LANES), 0), iota((LANES, 2 * LANES), 1)
    head = 2 * t + (col % LANES) // P_SIZE
    pick = (row % HEADS == head) & (row // (2 * HEADS) == col // LANES)
    both = mm(expand[...], pick.astype(BF))
    return both[:, :LANES], both[:, LANES:]


def allowed(c, b1, b2, transposed):
    late = iota((Q, Q), 1 if transposed else 0) + c * Q
    early = iota((Q, Q), 0 if transposed else 1) + c * Q
    return (early <= late) & (early >= start_of(late, b1, b2))


def fwd_kernel(bnd, xs_ref, bc_ref, dt_ref, cwx_ref, cwb_ref, hp_ref, out_ref,
               lk, score, bmat, cmat, btrans, late, early, expand):
    b = pl.program_id(0)
    prepare(bnd[b, 0], bnd[b, 1], bc_ref, dt_ref, cwb_ref, hp_ref, lk, score, bmat, cmat,
            btrans, None, None, None, late, early, expand, False)
    for t in range(TILES):
        fwd_tile(t, slice(t * LANES, (t + 1) * LANES), xs_ref, cwx_ref, out_ref,
                 lk, score, cmat, btrans, late, early, expand)


def fwd_tile(t, at, xs_ref, cwx_ref, out_ref, lk, score, cmat, btrans, late, early, expand):
    taps, bias = taps_of(cwx_ref, at)
    pre = conv_pre(xs_ref[:, at].astype(F32), taps, bias, [lk[0], lk[1], lk[2]])
    x = pre * sigmoid(pre)
    first = iota((TOK, LANES), 1) < P_SIZE
    dtx, middle = spread_over(expand, t)
    xt = x * dtx
    xt16 = xt.astype(BF)
    half = Q // 2
    outs = []
    for c in range(2):
        o = c * Q
        for rows, width in ((slice(o, o + half), half), (slice(o + half, o + Q), Q)):
            last = rows.stop - o
            w = mm_nt(both_heads(late[rows, :], t), early[o : o + width, :])
            s = score[c, last - half : last, :width]
            w = jnp.exp2(jnp.minimum(w, 0.0)) * jnp.concatenate([s, s], 0)
            y = mm(w.astype(BF), xt16[o : o + width])
            outs.append(jnp.where(first[:half], y[:half], y[half:]))
    outs = [jnp.concatenate(outs[:2], 0), jnp.concatenate(outs[2:], 0)]
    state = mm(btrans[...], (middle[:Q] * xt[:Q]).astype(BF))
    outs[1] = outs[1] + mm(cmat[Q:, :], state.astype(BF)) * middle[Q:]
    skip = cwx_ref[5:6, at]
    out_ref[:, at] = jnp.concatenate(outs, 0) + skip * x


def conv_back(dact, pre, sg, xin, taps, links):
    dpre = dact * (sg * (1.0 + pre * (1.0 - sg)))
    g = taps[3] * dpre
    sums = [None] * 5
    sums[3] = jnp.sum(dpre * xin, axis=0, keepdims=True)
    sums[4] = jnp.sum(dpre, axis=0, keepdims=True)
    for k in range(1, 4):
        q = links[k - 1] * dpre
        g = g + taps[3 - k] * pltpu.roll(q, TOK - k, 0)
        sums[3 - k] = jnp.sum(q * pltpu.roll(xin, k, 0), axis=0, keepdims=True)
    return g, sums


def bwd_tile(t, at, xs_ref, cwx_ref, scan_ref, dscan_ref, out_ref, dcw_ref,
             lk, score, bmat, btrans, ctrans, late, early, expand, dscore, rsum, rsum3, dball, dcall):
    taps, bias = taps_of(cwx_ref, at)
    links = [lk[0], lk[1], lk[2]]
    xin = xs_ref[:, at].astype(F32)
    pre = conv_pre(xin, taps, bias, links)
    sg = sigmoid(pre)
    x = pre * sg
    first = iota((TOK, LANES), 1) < P_SIZE
    dtx, middle = spread_over(expand, t)
    xt = x * dtx
    xt16 = xt.astype(BF)
    xtf = xt16.astype(F32)
    skip = cwx_ref[5:6, at]
    dy16 = dscan_ref[:, at]
    dy = dy16.astype(F32)
    dyf = dy
    zero = jnp.zeros((Q // 2, LANES), BF)
    half = Q // 2
    parts = []
    for c in range(2):
        o = c * Q
        for rows, begin in ((slice(o, o + half), 0), (slice(o + half, o + Q), half)):
            at_row = slice(begin, begin + half)
            later = slice(o + begin, o + Q)
            w = jnp.exp2(jnp.minimum(mm_nt(both_heads(early[rows, :], t), late[later, :]), 0.0))
            xr = xt16[rows]
            xr = jnp.concatenate([jnp.where(first[:half], xr, zero), jnp.where(first[:half], zero, xr)], 0)
            wp = w * mm_nt(xr, dy16[later])
            dscore[c, at_row, begin:] += wp[:half] + wp[half:]
            s = score[c, at_row, begin:]
            y = mm((w * jnp.concatenate([s, s], 0)).astype(BF), dy16[later])
            parts.append(jnp.where(first[:half], y[:half], y[half:]))
    parts = [jnp.concatenate(parts[:2], 0), jnp.concatenate(parts[2:], 0)]
    tx, ex = middle[:Q], middle[Q:]
    txt16 = (tx * xt[:Q]).astype(BF)
    state = mm(btrans[...], txt16).astype(BF)
    dye = (ex * dy[Q:]).astype(BF)
    dstate = mm(ctrans[...], dye).astype(BF)
    dcall[...] += mm_nt(dye, state)
    dball[...] += mm_nt(txt16, dstate)
    across = tx * mm(bmat[:Q, :], dstate)
    within = jnp.concatenate(parts, 0)
    dxt = jnp.concatenate([parts[0] + across, parts[1]], 0)
    r1 = dyf * (scan_ref[:, at] - skip * x) - xtf * within
    r2 = x * dxt
    r3 = xtf[:Q] * across

    hi = r1.astype(BF)
    row, col = iota((2 * LANES, LANES), 0), iota((2 * LANES, LANES), 1)
    pick = (col == 2 * t + (row % LANES) // P_SIZE).astype(BF)
    rsum[...] += mm(jnp.concatenate([hi, (r1 - hi.astype(F32)).astype(BF)], 1), pick)
    row, col = iota((2 * LANES, 2 * LANES), 0), iota((2 * LANES, 2 * LANES), 1)
    pick = ((col % LANES == 2 * t + (row % LANES) // P_SIZE) & (row // LANES == col // LANES)).astype(BF)
    r3 = jnp.concatenate([r3, jnp.zeros_like(r3)], 0)
    rsum3[...] += mm(jnp.concatenate([r2.astype(BF), r3.astype(BF)], 1), pick)
    g, sums = conv_back(dxt * dtx + skip * dy, pre, sg, xin, taps, links)
    sums.append(jnp.sum(dy * x, axis=0, keepdims=True))
    sums.append(jnp.zeros((2, LANES), F32))
    out_ref[:, at] = g.astype(BF)
    dcw_ref[:, at] += jnp.concatenate(sums, 0)


def bwd_kernel(bnd, xs_ref, bc_ref, dt_ref, cwx_ref, cwb_ref, hp_ref, scan_ref, dscan_ref,
               out_ref, dcw_ref, dhp_ref,
               lk, score, bmat, cmat, btrans, late, early, expand, ctrans, dts, sig, dscore, rsum, rsum3, dball, dcall):
    b = pl.program_id(0)
    b1, b2 = bnd[b, 0], bnd[b, 1]

    @pl.when(b == 0)
    def _():
        dcw_ref[...] = jnp.zeros_like(dcw_ref)
        dhp_ref[...] = jnp.zeros_like(dhp_ref)

    prepare(b1, b2, bc_ref, dt_ref, cwb_ref, hp_ref, lk, score, bmat, cmat,
            btrans, ctrans, dts, sig, late, early, expand, True)
    for v in (dscore, rsum, rsum3, dball, dcall):
        v[...] = jnp.zeros_like(v)
    for t in range(TILES):
        bwd_tile(t, slice(t * LANES, (t + 1) * LANES), xs_ref, cwx_ref, scan_ref, dscan_ref, out_ref, dcw_ref,
                 lk, score, bmat, btrans, ctrans, late, early, expand, dscore, rsum, rsum3, dball, dcall)
    links = [lk[0], lk[1], lk[2]]

    db, dc = [], []
    for c in range(2):
        part = slice(c * Q, (c + 1) * Q)
        ds = jnp.where(allowed(c, b1, b2, True), dscore[c], 0.0)
        db.append(mm(ds.astype(BF), cmat[part, :]))
        dc.append(mm(ds.T.astype(BF), bmat[part, :]))
    db[0] = db[0] + dball[...]
    dc[1] = dc[1] + dcall[...]
    base = TILES * LANES
    for i, dact in enumerate((jnp.concatenate(db, 0), jnp.concatenate(dc, 0))):
        lanes = slice(i * LANES, (i + 1) * LANES)
        taps_b, bias_b = taps_of(cwb_ref, lanes)
        xin_b = bc_ref[:, lanes].astype(F32)
        pre_b = conv_pre(xin_b, taps_b, bias_b, links)
        g, sums = conv_back(dact, pre_b, sigmoid(pre_b), xin_b, taps_b, links)
        sums.append(jnp.zeros((3, LANES), F32))
        at = slice(base + i * LANES, base + (i + 1) * LANES)
        out_ref[:, at] = g.astype(BF)
        dcw_ref[:, at] += jnp.concatenate(sums, 0)
    upper = (iota((Q, Q), 0) <= iota((Q, Q), 1)).astype(F32)
    below = (iota((Q, Q), 0) > iota((Q, Q), 1)).astype(F32)
    high = functools.partial(jnp.dot, precision=HIGHEST, preferred_element_type=F32)
    rate = hp_ref[1:2, :]
    da = jnp.concatenate(
        [
            high(upper, rsum[:Q, :]) + high(below, rsum3[:Q, LANES:]),
            high(upper, rsum[Q:, :]),
        ],
        0,
    )
    step = dts[...]
    draw = (rsum3[:, :LANES] + da * rate) * sig[...]
    dhp_ref[0:1, :] += jnp.sum(draw, axis=0, keepdims=True)
    dhp_ref[1:2, :] += jnp.sum(da * (rate * step), axis=0, keepdims=True)
    out_ref[:, base + 2 * LANES :] = draw[:, :HEADS].astype(BF)


def params(*semantics, mib=48):
    return pltpu.CompilerParams(dimension_semantics=semantics, vmem_limit_bytes=mib * 1024 * 1024)


def cost(flops, moved):
    return pl.CostEstimate(flops=int(flops / 16), bytes_accessed=int(moved / 16), transcendentals=0)


def block_scratch(extra):
    column = pltpu.VMEM((TOK, LANES), F32)
    packed = pltpu.VMEM((TOK, LANES), BF)
    part = pltpu.VMEM((Q, LANES), F32)
    half = pltpu.VMEM((LANES, Q), BF)
    square = pltpu.VMEM((2, Q, Q), F32)
    base = [pltpu.VMEM((3, TOK, LANES), F32), square, packed, packed, half, packed, packed, packed]
    if not extra:
        return base
    return base + [half, column, column, square, column, pltpu.VMEM((TOK, 2 * LANES), F32), part, part]


def mixer_specs(first):
    return [
        pl.BlockSpec((TOK, TILES * LANES), lambda b, *_: (b + first, 0)),
        pl.BlockSpec((TOK, 2 * LANES), lambda b, *_: (b + first, TILES // 2)),
        pl.BlockSpec((TOK, LANES), lambda b, *_: (b + first, TILES + 2)),
        pl.BlockSpec((8, TILES * LANES), lambda b, *_: (0, 0)),
        pl.BlockSpec((8, 2 * LANES), lambda b, *_: (0, TILES // 2)),
        pl.BlockSpec((8, LANES), lambda b, *_: (0, 0)),
    ]


ANY = pl.BlockSpec(memory_space=pl.ANY)


def fwd_into(bnd, *refs):
    fwd_kernel(bnd, *refs[:6], *refs[7:])


def scan_forward(bounds, proj, cw, hp, first, count, into=None):
    return pl.pallas_call(
        fwd_kernel if into is None else fwd_into,
        out_shape=jax.ShapeDtypeStruct((proj.shape[0], TILES * LANES), F32),
        grid_spec=pltpu.PrefetchScalarGridSpec(
            num_scalar_prefetch=1,
            grid=(count,),
            in_specs=mixer_specs(first) + ([] if into is None else [ANY]),
            out_specs=pl.BlockSpec((TOK, TILES * LANES), lambda b, *_: (b + first, 0)),
            scratch_shapes=block_scratch(False),
        ),
        input_output_aliases={} if into is None else {7: 0},
        compiler_params=params("arbitrary"),
        cost_estimate=cost(count * 8e9, count * 4e6),
    )(bounds[first : first + count], proj, proj, proj, cw, cw, hp, *([] if into is None else [into]))


def bwd_into(bnd, *refs):
    bwd_kernel(bnd, *refs[:8], *refs[9:])


def scan_backward(bounds, proj, cw, hp, scan, dscan, first, count, into=None):
    tile = pl.BlockSpec((TOK, TILES * LANES), lambda b, *_: (b + first, 0))
    return pl.pallas_call(
        bwd_kernel if into is None else bwd_into,
        out_shape=(
            jax.ShapeDtypeStruct((proj.shape[0], REST), BF),
            jax.ShapeDtypeStruct((8, (TILES + 2) * LANES), F32),
            jax.ShapeDtypeStruct((8, LANES), F32),
        ),
        grid_spec=pltpu.PrefetchScalarGridSpec(
            num_scalar_prefetch=1,
            grid=(count,),
            in_specs=mixer_specs(first) + [tile, tile] + ([] if into is None else [ANY]),
            out_specs=(
                pl.BlockSpec((TOK, REST), lambda b, *_: (b + first, 0)),
                pl.BlockSpec((8, (TILES + 2) * LANES), lambda b, *_: (0, 0)),
                pl.BlockSpec((8, LANES), lambda b, *_: (0, 0)),
            ),
            scratch_shapes=block_scratch(True),
        ),
        input_output_aliases={} if into is None else {9: 0},
        compiler_params=params("arbitrary"),
        cost_estimate=cost(count * 16e9, count * 6e6),
    )(
        bounds[first : first + count],
        proj, proj, proj,
        cw,
        cw,
        hp,
        scan, dscan,
        *([] if into is None else [into]),
    )


def whole_once(a):
    return pl.BlockSpec(a.shape, lambda i, *_: (0, 0), pipeline_mode=pl.Buffered(1))


def ginner_kernel(perm, gout_ref, *refs):
    pieces, (out_ref, wide_ref, gate_ref) = refs[:-3], refs[-3:]
    inner = TILES * LANES

    @pl.when(pl.program_id(0) == 0)
    def _():
        for p, piece in enumerate(pieces):
            rows = pl.ds(pl.multiple_of(perm[p] * LANES, LANES), LANES)
            for k in range(8):
                wide_ref[rows, k * 256 : (k + 1) * 256] = piece[inner + k * LANES : inner + (k + 1) * LANES, :]
            gate_ref[:, p * 256 : (p + 1) * 256] = piece[:inner, :]

    out_ref[...] = mm_nt(gout_ref[...], wide_ref[...]).astype(BF)


def inner_gradient(perm, gout, pieces):
    rows, inner = gout.shape[0], TILES * LANES
    whole = pl.BlockSpec((inner, D), lambda i, *_: (0, 0))
    return pl.pallas_call(
        ginner_kernel,
        out_shape=(jax.ShapeDtypeStruct((rows, inner), BF), jax.ShapeDtypeStruct((inner, D), BF), jax.ShapeDtypeStruct((inner, D), BF)),
        grid_spec=pltpu.PrefetchScalarGridSpec(
            num_scalar_prefetch=1,
            grid=(rows // TOK,),
            in_specs=[pl.BlockSpec((TOK, D), lambda i, *_: (i, 0))] + [whole_once(a) for a in pieces],
            out_specs=(pl.BlockSpec((TOK, inner), lambda i, *_: (i, 0)), whole, whole),
        ),
        compiler_params=params("arbitrary"),
        cost_estimate=cost(2 * rows * inner * D, 2 * (rows * D + rows * inner + 4 * inner * D)),
    )(perm, gout, *pieces)


def out_kernel(perm, inner_ref, gout_ref, out_ref, turned, result):
    @pl.when(pl.program_id(0) == 0)
    def _():
        turned[...] = inner_ref[...].T

    result[...] = mm(turned[...], gout_ref[...])
    for p in range(8):
        rows = pl.ds(pl.multiple_of(perm[p] * LANES, LANES), LANES)
        out_ref[:, p * 256 : (p + 1) * 256] = result[rows, :].astype(BF)


def out_terms(perm, inner, gout):
    rows, wide = inner.shape
    return pl.pallas_call(
        out_kernel,
        out_shape=jax.ShapeDtypeStruct((wide, D), BF),
        grid_spec=pltpu.PrefetchScalarGridSpec(
            num_scalar_prefetch=1,
            grid=(8,),
            in_specs=[
                pl.BlockSpec((rows, wide), lambda k, *_: (0, 0)),
                pl.BlockSpec((rows, 256), lambda k, *_: (0, k)),
            ],
            out_specs=pl.BlockSpec((LANES, D), lambda k, *_: (k, 0)),
            scratch_shapes=[pltpu.VMEM((wide, rows), BF), pltpu.VMEM((wide, 256), F32)],
        ),
        compiler_params=params("arbitrary", mib=48),
        cost_estimate=cost(2 * rows * wide * D, 2 * (rows * wide + rows * D + wide * D)),
    )(perm, inner, gout)


def stat_kernel(norm_ref, w_ref, scan_ref, gin_ref, gain_ref, gate_ref, out_ref):
    gate_ref[...] = mm_nt(norm_ref[...], w_ref[...]).astype(BF)
    one = two = jnp.zeros((TOK, LANES), F32)
    for t in range(TILES):
        at = slice(t * LANES, (t + 1) * LANES)
        gate = gate_ref[:, at].astype(F32)
        gated = scan_ref[:, at] * (gate * sigmoid(gate))
        one = one + gated * gated
        two = two + gated * (gin_ref[:, at].astype(F32) * gain_ref[:, at])
    a = jnp.sum(one.T, axis=0, keepdims=True)
    c = jnp.sum(two.T, axis=0, keepdims=True)
    out_ref[0] = jnp.concatenate([a, c, jnp.zeros((6, TOK), F32)], 0)


def gate_stats(normed, w_gate, scan, ginner, gain):
    rows, inner = scan.shape
    tile = pl.BlockSpec((TOK, inner), lambda b: (b, 0))
    return pl.pallas_call(
        stat_kernel,
        out_shape=(jax.ShapeDtypeStruct((rows, inner), BF), jax.ShapeDtypeStruct((rows // TOK, 8, TOK), F32)),
        grid=(rows // TOK,),
        in_specs=[
            pl.BlockSpec((TOK, D), lambda b: (b, 0)),
            pl.BlockSpec((inner, D), lambda b: (0, 0)),
            tile,
            tile,
            pl.BlockSpec((1, inner), lambda b: (0, 0)),
        ],
        out_specs=(tile, pl.BlockSpec((1, 8, TOK), lambda b: (b, 0, 0))),
        compiler_params=params("arbitrary", mib=48),
        cost_estimate=cost(2 * rows * inner * D, rows * (D * 2 + inner * 8) + inner * D * 2),
    )(normed, w_gate, scan, ginner, gain)


def gate_kernel(sum_ref, scan_ref, gate_ref, gin_ref, gain_ref, inner_ref, dgate_ref, dscan_ref, dgain_ref):
    rows = scan_ref.shape[0]

    @pl.when((pl.program_id(0) == 0) & (pl.program_id(1) == 0))
    def _():
        dgain_ref[...] = jnp.zeros_like(dgain_ref)

    r = lax.rsqrt(sum_ref[0, 0:1, :] * (1.0 / DIN) + EPSILON)
    c = r * r * sum_ref[0, 1:2, :] * (1.0 / DIN)
    rinv = jnp.broadcast_to(r, (LANES, rows)).T
    coef = jnp.broadcast_to(c, (LANES, rows)).T
    for t in range(TILES):
        at = slice(t * LANES, (t + 1) * LANES)
        gate = gate_ref[:, at].astype(F32)
        sg = sigmoid(gate)
        act = gate * sg
        scan = scan_ref[:, at]
        gain = gain_ref[:, at]
        gated = scan * act
        scaled = gated * rinv
        gin = gin_ref[:, at].astype(F32)
        inner_ref[:, at] = (scaled * gain).astype(BF)
        dgated = rinv * (gin * gain - gated * coef)
        dscan_ref[:, at] = (dgated * act).astype(BF)
        dgate_ref[:, at] = (dgated * scan * (sg + act * (1.0 - sg))).astype(BF)
        dgain_ref[0:1, at] += jnp.sum(gin * scaled, axis=0, keepdims=True)


def gate_both(sums, scan, gate, ginner, gain):
    rows, inner = scan.shape
    tile = pl.BlockSpec((Q, inner), lambda b, h: (2 * b + h, 0))
    whole = jax.ShapeDtypeStruct((rows, inner), BF)
    return pl.pallas_call(
        gate_kernel,
        out_shape=(whole, whole, whole, jax.ShapeDtypeStruct((8, inner), F32)),
        grid=(rows // TOK, 2),
        in_specs=[
            pl.BlockSpec((1, 8, Q), lambda b, h: (b, 0, h)),
            tile,
            tile,
            tile,
            pl.BlockSpec((1, inner), lambda b, h: (0, 0)),
        ],
        out_specs=(tile, tile, tile, pl.BlockSpec((8, inner), lambda b, h: (0, 0))),
        compiler_params=params("arbitrary", "arbitrary", mib=48),
        cost_estimate=cost(0, rows * inner * 14),
    )(sums, scan, gate, ginner, gain)


def back_kernel(a_ref, wa_ref, b_ref, wb_ref, norm_ref, out_ref, dgo_ref):
    @pl.when(pl.program_id(0) == 0)
    def _():
        dgo_ref[...] = jnp.zeros_like(dgo_ref)

    for c in range(4):
        at = slice(c * 512, (c + 1) * 512)
        res = mm(a_ref[...], wa_ref[:, at]) + mm(b_ref[...], wb_ref[:, at])
        out_ref[:, at] = res.astype(BF)
        dgo_ref[0:1, at] += jnp.sum(res * norm_ref[:, at].astype(F32), axis=0, keepdims=True)


def normed_gradient(gproj, w_rest, dgate, w_two, normed, first, count):
    rows, inner = dgate.shape
    row = lambda width: pl.BlockSpec((TOK, width), lambda b: (b + first, 0))
    return pl.pallas_call(
        back_kernel,
        out_shape=(jax.ShapeDtypeStruct((count * TOK, D), BF), jax.ShapeDtypeStruct((8, D), F32)),
        grid=(count,),
        in_specs=[
            row(REST),
            pl.BlockSpec((REST, D), lambda b: (0, 0)),
            row(inner),
            pl.BlockSpec((inner, D), lambda b: (0, 0)),
            row(D),
        ],
        out_specs=(pl.BlockSpec((TOK, D), lambda b: (b, 0)), pl.BlockSpec((8, D), lambda b: (0, 0))),
        compiler_params=params("arbitrary", mib=48),
        cost_estimate=cost(2 * count * TOK * D * (REST + inner), 2 * (REST + inner) * D),
    )(gproj, w_rest, dgate, w_two, normed)


def across_kernel(a_ref, b_ref, out_ref, *turned):
    if len(turned) == 2:
        (kept, turned) = turned

        @pl.when(pl.program_id(0) == 0)
        def _():
            turned[...] = a_ref[...].T
            kept[...] = turned[...]
    else:
        turned = a_ref
    out_ref[...] = mm(turned[...], b_ref[...]).astype(out_ref.dtype)


def across_rows(a, b, first, count, turn):
    rows, n = b.shape
    m = a.shape[1] if turn else a.shape[0]
    whole = pl.BlockSpec(a.shape, lambda k: (0, 0))
    part = jax.ShapeDtypeStruct((m, count * 256), BF)
    spec = pl.BlockSpec((m, 256), lambda k: (0, k))
    return pl.pallas_call(
        across_kernel,
        out_shape=(part, jax.ShapeDtypeStruct((m, rows), BF)) if turn else part,
        grid=(count,),
        in_specs=[whole, pl.BlockSpec((rows, 256), lambda k: (0, k + first))],
        out_specs=(spec, pl.BlockSpec((m, rows), lambda k: (0, 0))) if turn else spec,
        scratch_shapes=[pltpu.VMEM((m, rows), BF)] if turn else [],
        compiler_params=params("arbitrary", mib=48),
        cost_estimate=cost(2 * rows * m * 256 * count, 2 * (rows * m + rows * 256 * count + m * 256 * count)),
    )(a, b)


def pick_rest_kernel(me, *refs):
    tiles, (shared, steps, out_ref) = refs[:TILES], refs[TILES:]
    for t, ref in enumerate(tiles):
        out_ref[t * LANES : (t + 1) * LANES, :] = ref[...].astype(BF)
    wide = TILES * LANES
    out_ref[wide : wide + 2 * N, :] = shared[...].astype(BF)
    mine, head = iota((HEADS, H), 0), iota((HEADS, H), 1)
    pick = (head == 8 * (mine // 2) + 2 * me[0] + mine % 2).astype(BF)
    out_ref[wide + 2 * N :, :] = mm(pick, steps[...].astype(BF)).astype(BF)


def tile_spec(lanes, t):
    return pl.BlockSpec((LANES, lanes), lambda i, me: (4 * t + me[0], 0))


def pick_rest(me, turned):
    lanes = turned.shape[1]
    fixed = lambda rows, at: pl.BlockSpec((rows, lanes), lambda i, me: (at // rows, 0))
    return pl.pallas_call(
        pick_rest_kernel,
        out_shape=jax.ShapeDtypeStruct((REST, lanes), BF),
        grid_spec=pltpu.PrefetchScalarGridSpec(
            num_scalar_prefetch=1,
            grid=(1,),
            in_specs=[tile_spec(lanes, TILES + t) for t in range(TILES)] + [fixed(2 * N, 2 * DIN), fixed(H, 2 * DIN + 2 * N)],
            out_specs=pl.BlockSpec((REST, lanes), lambda i, me: (0, 0)),
        ),
        compiler_params=params("arbitrary"),
        cost_estimate=cost(0, 6 * REST * lanes),
    )(me, *[turned] * (TILES + 2))


def pick_two_kernel(me, *refs):
    tiles, (rows, out_ref) = refs[:TILES], refs[TILES:]
    for t, ref in enumerate(tiles):
        out_ref[t * LANES : (t + 1) * LANES, :] = ref[...].astype(BF)
    wide = TILES * LANES
    for k in range(8):
        out_ref[wide + k * LANES : wide + (k + 1) * LANES, :] = rows[:, k * 256 : (k + 1) * 256].astype(BF)


def pick_two(me, turned, out_weight):
    lanes = turned.shape[1]
    return pl.pallas_call(
        pick_two_kernel,
        out_shape=jax.ShapeDtypeStruct((2 * TILES * LANES, lanes), BF),
        grid_spec=pltpu.PrefetchScalarGridSpec(
            num_scalar_prefetch=1,
            grid=(1,),
            in_specs=[tile_spec(lanes, t) for t in range(TILES)] + [pl.BlockSpec((LANES, D), lambda i, me: (me[0], 0))],
            out_specs=pl.BlockSpec((2 * TILES * LANES, lanes), lambda i, me: (0, 0)),
        ),
        compiler_params=params("arbitrary"),
        cost_estimate=cost(0, 12 * TILES * LANES * lanes),
    )(me, *[turned] * TILES, out_weight)


def pick_gate_kernel(me, *refs):
    for t, ref in enumerate(refs[:-1]):
        refs[-1][t * LANES : (t + 1) * LANES, :] = ref[...].astype(BF)


def pick_gate(me, turned):
    lanes = turned.shape[1]
    return pl.pallas_call(
        pick_gate_kernel,
        out_shape=jax.ShapeDtypeStruct((TILES * LANES, lanes), BF),
        grid_spec=pltpu.PrefetchScalarGridSpec(
            num_scalar_prefetch=1,
            grid=(1,),
            in_specs=[tile_spec(lanes, t) for t in range(TILES)],
            out_specs=pl.BlockSpec((TILES * LANES, lanes), lambda i, me: (0, 0)),
        ),
        compiler_params=params("arbitrary"),
        cost_estimate=cost(0, 6 * TILES * LANES * lanes),
    )(me, *[turned] * TILES)


STEP = 128


def norm_kernel(perm, tok_ref, gain_ref, out_ref):
    x = tok_ref[...].astype(F32)
    inv = lax.rsqrt(jnp.mean(x * x, axis=1, keepdims=True) + EPSILON)
    wide = D // 8
    for k in range(8):
        here = pl.ds(pl.multiple_of(perm[k] * wide, wide), wide)
        out_ref[:, k * wide : (k + 1) * wide] = (
            tok_ref[:, here].astype(F32) * inv * gain_ref[:, here]
        ).astype(BF)


def norm_rows(perm, tokens, gain):
    rows = tokens.shape[0]
    row = pl.BlockSpec((STEP, D), lambda i, *_: (i, 0))
    return pl.pallas_call(
        norm_kernel,
        out_shape=jax.ShapeDtypeStruct((rows, D), BF),
        grid_spec=pltpu.PrefetchScalarGridSpec(
            num_scalar_prefetch=1,
            grid=(rows // STEP,),
            in_specs=[row, pl.BlockSpec((1, D), lambda i, *_: (0, 0))],
            out_specs=row,
        ),
        compiler_params=params("arbitrary"),
        cost_estimate=pl.CostEstimate(flops=0, bytes_accessed=rows * D * 4, transcendentals=0),
    )(perm, tokens, gain)


def last_kernel(perm, tok_ref, cot_ref, keep_ref, gain_ref, one_ref, two_ref, three_ref, out_ref, grad):
    wide = D // 8
    for k in range(8):
        here = pl.ds(pl.multiple_of(perm[k] * wide, wide), wide)
        at = slice(k * wide, (k + 1) * wide)
        grad[:, here] = (
            one_ref[:, at].astype(F32) + two_ref[:, at].astype(F32) + three_ref[:, at].astype(F32)
        ) * gain_ref[:, here]
    x = tok_ref[...].astype(F32)
    inv = lax.rsqrt(jnp.mean(x * x, axis=1, keepdims=True) + EPSILON)
    g = grad[...]
    dot = jnp.mean(g * x, axis=1, keepdims=True)
    out_ref[...] = inv * (g - x * (inv * inv * dot)) + keep_ref[...] * cot_ref[...].astype(F32)


def last_rows(perm, tokens, cotangent, keep, gain, parts):
    rows = tokens.shape[0]
    row = pl.BlockSpec((STEP, D), lambda i, *_: (i, 0))
    return pl.pallas_call(
        last_kernel,
        out_shape=jax.ShapeDtypeStruct((rows, D), F32),
        grid_spec=pltpu.PrefetchScalarGridSpec(
            num_scalar_prefetch=1,
            grid=(rows // STEP,),
            in_specs=[
                row,
                row,
                pl.BlockSpec((STEP, 1), lambda i, *_: (i, 0)),
                pl.BlockSpec((1, D), lambda i, *_: (0, 0)),
                row,
                row,
                row,
            ],
            out_specs=row,
            scratch_shapes=[pltpu.VMEM((STEP, D), F32)],
        ),
        compiler_params=params("arbitrary"),
        cost_estimate=pl.CostEstimate(flops=0, bytes_accessed=rows * D * 14, transcendentals=0),
    )(perm, tokens, cotangent, keep, gain, *parts)


def first_join_kernel(me, *refs):
    pieces, (out_ref, grad_ref, stage, sem) = refs[:4], refs[4:]
    inner = TILES * LANES
    for k in range(4):
        q = jnp.bitwise_xor(me[0], k)
        for t in range(TILES):
            rows = pl.ds(pl.multiple_of((4 * t + q) * LANES, LANES), LANES)
            stage[rows, :] = pieces[k][t * LANES : (t + 1) * LANES, :].astype(F32)
    copy = pltpu.make_async_copy(stage, out_ref.at[pl.ds(0, 4 * inner)], sem)
    copy.start()
    for k in range(4):
        q = jnp.bitwise_xor(me[0], k)
        rows = pl.ds(pl.multiple_of(q * LANES, LANES), LANES)
        for c in range((pieces[k].shape[0] - inner) // LANES):
            grad_ref[rows, c * 256 : (c + 1) * 256] = pieces[k][
                inner + c * LANES : inner + (c + 1) * LANES, :
            ].astype(F32)
    copy.wait()


def first_join(me, pieces, width):
    lanes = pieces[0].shape[1]
    whole = pl.BlockSpec(pieces[0].shape, lambda i, *_: (0, 0))
    return pl.pallas_call(
        first_join_kernel,
        out_shape=(
            jax.ShapeDtypeStruct((width, lanes), F32),
            jax.ShapeDtypeStruct((4 * LANES, D), F32),
        ),
        grid_spec=pltpu.PrefetchScalarGridSpec(
            num_scalar_prefetch=1,
            grid=(1,),
            in_specs=[whole] * 4,
            out_specs=(ANY, pl.BlockSpec((4 * LANES, D), lambda i, *_: (0, 0))),
            scratch_shapes=[pltpu.VMEM((4 * TILES * LANES, lanes), F32), pltpu.SemaphoreType.DMA],
        ),
        compiler_params=params("arbitrary", mib=48),
        cost_estimate=cost(0, 20e6),
    )(me, *pieces)


def last_join_kernel(me, one, two, three, four, into, out_ref, stage, sem):
    pieces = (one, two, three, four)
    inner = TILES * LANES
    few = H // 4
    for k in range(4):
        q = jnp.bitwise_xor(me[0], k)
        for t in range(TILES):
            rows = pl.ds(pl.multiple_of((4 * t + q) * LANES, LANES), LANES)
            stage[rows, :] = pieces[k][t * LANES : (t + 1) * LANES, :].astype(F32)
    stage[4 * inner : 4 * inner + 2 * N, :] = sum(p[inner : inner + 2 * N, :].astype(F32) for p in pieces)
    steps = None
    for k in range(4):
        q = jnp.bitwise_xor(me[0], k)
        head, mine = iota((H, few), 0), iota((H, few), 1)
        spread = (head == 8 * (mine // 2) + 2 * q + mine % 2).astype(BF)
        term = mm(spread, pieces[k][inner + 2 * N :, :])
        steps = term if steps is None else steps + term
    stage[4 * inner + 2 * N :, :] = steps
    copy = pltpu.make_async_copy(stage, out_ref.at[pl.ds(4 * inner, stage.shape[0])], sem)
    copy.start()
    copy.wait()


def last_join(me, pieces, into):
    lanes = pieces[0].shape[1]
    whole = pl.BlockSpec(pieces[0].shape, lambda i, *_: (0, 0))
    return pl.pallas_call(
        last_join_kernel,
        out_shape=jax.ShapeDtypeStruct(into.shape, F32),
        grid_spec=pltpu.PrefetchScalarGridSpec(
            num_scalar_prefetch=1,
            grid=(1,),
            in_specs=[whole] * 4 + [ANY],
            out_specs=ANY,
            scratch_shapes=[pltpu.VMEM((into.shape[0] - 4 * TILES * LANES, lanes), F32), pltpu.SemaphoreType.DMA],
        ),
        input_output_aliases={5: 0},
        compiler_params=params("arbitrary"),
        cost_estimate=cost(0, 8e6),
    )(me, *pieces, into)


def tie(*arrays):
    return lax.optimization_barrier(arrays)


def swap(x, d):
    return lax.ppermute(x, "rep", [(i, i ^ d) for i in range(4)])


def fw(x):
    return lax.ppermute(x, "shard", [(RING[i], RING[(i + 1) % 8]) for i in range(8)])


def bw(x):
    return lax.ppermute(x, "shard", [(RING[(i + 1) % 8], RING[i]) for i in range(8)])


def relative(s, n):
    if n != 8:
        return jnp.arange(8, dtype=jnp.int32), jnp.arange(8, dtype=jnp.int32)
    table, inverse = [], []
    for shard in range(8):
        p = RING.index(shard)
        row = [RING[(p + d) % 8] for d in (0, -1, 1, -2, 2, -3, 3, 4)]
        table.append(row)
        inverse.append([row.index(i) for i in range(8)])
    return jnp.asarray(table, jnp.int32)[s], jnp.asarray(inverse, jnp.int32)[s]


def cut(rows):
    return -(-rows // 32) * 16


def ring_pieces(piece, pieces):
    half = cut(piece.shape[0])
    a = b = piece
    pieces.append(piece)
    for _ in range(3):
        a, b = yield fw(a), bw(b)
        pieces += [a, b]
    a, b = yield fw(a[:half]), bw(b[half:])
    pieces.append(jnp.concatenate([a, b], 0))
    yield


def add16(a, b):
    return (a.astype(F32) + b.astype(F32)).astype(BF)


def ring_sum():
    far = yield
    half = cut(far.shape[0])
    rf, rb, (own, f1, b1, f2, b2, f3, b3) = yield far[:half], far[half:]
    sf = jnp.concatenate([add16(b3[:half], rf), b3[half:]], 0)
    sb = jnp.concatenate([f3[:half], add16(f3[half:], rb)], 0)
    rf, rb = yield sf, sb
    rf, rb = yield add16(b2, rf), add16(f2, rb)
    rf, rb = yield add16(b1, rf), add16(f1, rb)
    yield (own.astype(F32) + rf.astype(F32) + rb.astype(F32)).astype(BF)


def launch(steps, arrived, *others):
    forward, backward, *others = tie(*steps.send(arrived), *others)
    return [fw(forward), bw(backward)], *others


def blocks_of(x):
    return [x[k * TOK : (k + 1) * TOK] for k in range(4)]


def sum_rep(parts):
    far = swap(parts[3], 1)
    chip = swap((parts[2].astype(F32) + far.astype(F32)).astype(BF), 2)
    return parts[0].astype(F32) + swap(parts[1], 1).astype(F32) + chip.astype(F32)


def shards(n, tokens, cotangent, lengths, order, mask, in_weight, out_weight, conv_weight, conv_bias, dt_bias,
           a_log, skip_gain, gain_outer, gain_inner):
    r, s = lax.axis_index("rep"), lax.axis_index("shard")
    ring = n == 8
    inner_width = TILES * LANES
    perm, place = relative(s, n)
    keep = mask.astype(F32)[:, None]
    catalog = jnp.arange(lengths.shape[0], dtype=jnp.int32)
    picked = jnp.sum(jnp.where(order[:, None] == catalog[None, :], lengths[None, :], 0), axis=1)
    bounds = jnp.stack([picked[0], picked[0] + picked[1]])[None, :]
    bounds = jnp.concatenate([bounds, swap(bounds, 1), swap(bounds, 2), swap(bounds, 3)], 0)

    turned = in_weight.T
    me = r[None]
    rest = pick_rest(me, turned)
    normed = norm_rows(perm, tokens, gain_outer[None, :])
    gout = (cotangent.astype(F32) * keep).astype(BF)

    def own_lanes(v, width):
        v = lax.dynamic_index_in_dim(v.reshape(v.shape[:-1] + (TILES, 4, width)), r, v.ndim, False)
        return v.reshape(v.shape[:-2] + (TILES * width,))

    heads = H // 4
    skip = jnp.broadcast_to(skip_gain[:, None], (H, P_SIZE)).reshape(1, DIN)
    rows8 = jnp.concatenate(
        [conv_weight, conv_bias[None], jnp.pad(skip, ((0, 0), (0, 2 * N))), jnp.zeros((2, CONVCH), F32)], 0
    )
    cw = jnp.concatenate([own_lanes(rows8[:, :DIN], LANES), rows8[:, DIN:]], 1)
    hp = jnp.stack([own_lanes(dt_bias, 2), own_lanes(-jnp.exp(a_log), 2)])
    hp = jnp.pad(hp, ((0, 6), (0, LANES - heads)))
    gain = own_lanes(gain_inner, LANES)[None, :]

    if ring:
        pieces = []
        steps = ring_pieces(rest, pieces)
        sent = next(steps)
        core, chip = swap(normed, 1), swap(normed, 2)
        two = pick_two(me, turned, out_weight)
        *sent, core, two = tie(*sent, core, two)
        sent = steps.send(sent)
        *sent, gout = tie(*sent, gout)
        sent = steps.send(sent)
        sent = steps.send(tie(*sent))
        *sent, chip, two = tie(*sent, chip, two)
        steps.send(sent)
        rest_pieces = pieces

        pieces = []
        steps = ring_pieces(two, pieces)
        sent = next(steps)
        far, gchip, gcore = swap(chip, 1), swap(gout, 2), swap(gout, 1)
        w_rest = jnp.concatenate(rest_pieces, 1)
        all_normed = jnp.concatenate([normed, core, chip, far], 0)
        all_normed, w_rest = tie(all_normed, w_rest)
        proj = mm_nt(all_normed, w_rest).astype(BF)
        *sent, proj = tie(*sent, proj)
        sent = steps.send(sent)
        scan = scan_forward(bounds, proj, cw, hp, 0, 2)
        *sent, scan, gchip, gcore = tie(*sent, scan, gchip, gcore)
        sent = steps.send(sent)
        gfar = swap(gchip, 1)
        scan = scan_forward(bounds, proj, cw, hp, 2, 2, scan)
        *sent, scan, gfar = tie(*sent, scan, gfar)
        sent = steps.send(sent)
        all_gout = jnp.concatenate([gout, gcore, gchip, gfar], 0)
        *sent, all_gout = tie(*sent, all_gout)
        steps.send(sent)
        ginner, w_out, w_two = inner_gradient(perm, all_gout, pieces)
    else:
        everyone = lambda x: [x, swap(x, 1), swap(x, 2), swap(x, 3)]
        w_rest = lax.all_gather(rest, "shard", axis=1, tiled=True)
        w_two = lax.all_gather(pick_gate(me, turned), "shard", axis=1, tiled=True)
        w_out = lax.all_gather(out_weight.astype(BF), "shard", axis=0, tiled=True)
        w_out = lax.dynamic_index_in_dim(w_out.reshape(TILES, 4, LANES, D), r, 1, False).reshape(inner_width, D)
        all_normed = jnp.concatenate(everyone(normed), 0)
        all_gout = jnp.concatenate(everyone(gout), 0)
        proj = mm_nt(all_normed, w_rest).astype(BF)
        scan = scan_forward(bounds, proj, cw, hp, 0, 4)
        ginner = mm_nt(all_gout, w_out).astype(BF)

    gate, sums = gate_stats(all_normed, w_two, scan, ginner, gain)
    there = [swap(sums, d) for d in (1, 2, 3)]
    sums = jnp.stack([sums[k] + there[0][k ^ 1] + there[1][k ^ 2] + there[2][k ^ 3] for k in range(4)])
    inner, dgate, dscan, dgain = gate_both(sums, scan, gate, ginner, gain)

    def columns_of(x):
        return [x[:, k * 256 : (k + 1) * 256] for k in range(x.shape[1] // 256)]

    at_r = (jnp.arange(4) == r).astype(F32)
    sizes = [4 * CONVCH, CONVCH, H, H, H, D, DIN]

    def all_lanes(v, width):
        v = v.reshape(v.shape[:-1] + (TILES, 1, width)) * at_r[:, None]
        return v.reshape(v.shape[:-3] + (TILES * 4 * width,))

    def small_vector(dcw, dhp, dgo, dgain):
        wide = jnp.concatenate([all_lanes(dcw[:5, :inner_width], LANES), dcw[:5, inner_width:]], 1)
        dskip = jnp.sum(dcw[5, :inner_width].reshape(heads, P_SIZE), axis=1)
        dgo = dgo[0].reshape(8, D // 8)[place].reshape(D) / gain_outer
        parts = [
            wide.reshape(-1),
            all_lanes(dhp[0, :heads], 2),
            all_lanes(dhp[1, :heads], 2),
            all_lanes(dskip, 2),
            dgo,
            all_lanes(dgain[0], LANES),
        ]
        flat = jnp.concatenate(parts)
        return jnp.pad(flat, (0, -flat.shape[0] % 1024)).reshape(-1, LANES)

    width = in_weight.shape[1]
    final = functools.partial(normed_gradient, w_rest=w_rest, dgate=dgate, w_two=w_two, normed=all_normed)
    if ring:
        outs = columns_of(out_terms(perm, inner, all_gout))
        (dgate, _) = tie(dgate, outs[7])
        terms8 = columns_of(across_rows(dgate, all_normed, 0, 8, True)[0])
        terms8 = [jnp.concatenate(p, 0) for p in zip(terms8, outs)]
        steps = ring_sum()
        next(steps)
        sent, inner, dscan = launch(steps, terms8[7], inner, dscan)
        back = functools.partial(scan_backward, bounds, proj, cw, hp, scan)
        branch = mm(inner, w_out).astype(BF)
        *sent, branch = tie(*sent, branch)
        b0, b1, b2, b3 = blocks_of(branch)
        sent, dscan, b3 = launch(steps, (*sent, terms8[:7]), dscan, b3)
        far = swap(b3, 1)
        gproj, dcw, dhp = back(dscan, 2, 2)
        *sent, gproj, far = tie(*sent, gproj, far)
        sent, gproj, chip = launch(steps, sent, gproj, add16(b2, far))
        core, chip = swap(b1, 1), swap(chip, 2)
        grad3, dgo = final(gproj, first=3, count=1)
        (gproj, grad3) = tie(gproj, grad3)
        far = swap(grad3, 1)
        gproj, d, e = back(dscan, 0, 1, gproj)
        dcw, dhp = dcw + d, dhp + e
        *sent, gproj, core, far = tie(*sent, gproj, core, far)
        sent, gproj = launch(steps, sent, gproj)
        grad2, d = final(gproj, first=2, count=1)
        dgo = dgo + d
        (gproj, total) = tie(gproj, add16(grad2, far))
        gproj, d, e = back(dscan, 1, 1, gproj)
        dcw, dhp = dcw + d, dhp + e
        *sent, gproj, chip = tie(*sent, gproj, chip)
        share, gproj = tie(steps.send(sent), gproj)
        branch = (b0, core, chip)
        upper = swap(total[: TOK // 2], 2)

        far, turned_proj = across_rows(gproj, all_normed, 7, 1, True)
        steps = ring_sum()
        next(steps)
        sent, turned_proj = launch(steps, far, turned_proj)
        gates = [share, swap(share, 1)]
        seven = across_rows(turned_proj, all_normed, 0, 7, False)
        *sent, seven, gproj, upper, lower, share = tie(*sent, seven, gproj, upper, total[TOK // 2 :], share)
        sent, gproj, lower = launch(steps, (*sent, columns_of(seven)), gproj, lower)
        lower = swap(lower, 2)
        early, d = final(gproj, first=0, count=2)
        dgo = dgo + d
        *sent, early, lower, share = tie(*sent, early, lower, share)
        sent, early, share, dgo = launch(steps, sent, early, share, dgo)
        gates.append(swap(share, 2))
        core = swap(early[TOK:], 1)
        small = small_vector(dcw, dhp, dgo, dgain)
        bits = [1 << k for k in range(n.bit_length() - 1)]
        flip = lambda v, d: v + lax.ppermute(v, "shard", [(i, i ^ d) for i in range(n)])
        small = small + swap(small, 1)
        small = flip(small, bits[0])
        layer_out = (keep * (tokens.astype(F32) + sum(b.astype(F32) for b in branch))).astype(BF)
        *sent, core, layer_out, small = tie(*sent, core, layer_out, small)
        sent, core, small = launch(steps, sent, core, small)
        small = flip(small, bits[1])
        parts = [early[:TOK], core, jnp.concatenate([upper, lower], 0)]
        grad_tokens = last_rows(perm, tokens, cotangent, keep, gain_outer[None, :], parts)
        *sent, gates[2], grad_tokens, small = tie(*sent, gates[2], grad_tokens, small)
        share, small, gates[2] = tie(steps.send(sent), small, gates[2])
        rests = [share, swap(share, 1), swap(share, 2)]
        gates.append(swap(gates[2], 1))
        grad_in, grad_out_weight = first_join(me, gates, width)
        for d in bits[2:]:
            small = flip(small, d)
        small = small + swap(small, 2)
        rests.append(swap(rests[2], 1))
    else:
        rows_sum = lambda x, axis: lax.psum_scatter(
            x.astype(F32), "shard", scatter_dimension=axis, tiled=True
        ).astype(BF)
        branch = sum_rep(blocks_of(mm(inner, w_out).astype(BF)))
        gproj, dcw, dhp = scan_backward(bounds, proj, cw, hp, scan, dscan, 0, 4)
        layer_out = (keep * (tokens.astype(F32) + branch.astype(F32))).astype(BF)
        gnormed, dgo = final(gproj, first=0, count=4)
        total = sum_rep(blocks_of(gnormed)).astype(BF)
        grad_tokens = last_rows(
            perm, tokens, cotangent, keep, gain_outer[None, :], [total, jnp.zeros_like(total), jnp.zeros_like(total)]
        )
        grad_out = lax.dot_general(inner, all_gout, TN, preferred_element_type=F32)
        spread = grad_out.reshape(TILES, 1, LANES, D).astype(F32) * (jnp.arange(4)[None, :, None, None] == r)
        spread = lax.psum_scatter(spread.reshape(DIN, D), "shard", scatter_dimension=0, tiled=True)
        grad_out_weight = lax.psum(spread, "rep")
        gates = everyone(rows_sum(across_rows(dgate, all_normed, 0, 8, True)[0], 1))
        rests = everyone(rows_sum(across_rows(gproj, all_normed, 0, 8, True)[0], 1))
        grad_in, _ = first_join(me, gates, width)
        small = lax.psum(small_vector(dcw, dhp, dgo, dgain), ("rep", "shard"))
    grad_in_weight = last_join(me, rests, grad_in).T

    small = small.reshape(-1)
    ends = [sum(sizes[: i + 1]) for i in range(len(sizes))]
    g_cw, g_cb, g_db, g_al, g_sk, g_go, g_gi = [small[e - z : e] for e, z in zip(ends, sizes)]
    return (
        layer_out,
        grad_tokens,
        grad_in_weight,
        grad_out_weight,
        g_cw.reshape(4, CONVCH),
        g_cb,
        g_db,
        g_al,
        g_sk,
        g_go,
        g_gi,
    )


def solution(mesh):
    rows = P(("rep", "shard"), None)
    vector = P(("rep", "shard"))
    owned = P("shard", None)
    return jax.shard_map(
        functools.partial(shards, mesh.shape["shard"]),
        mesh=mesh,
        in_specs=(rows, rows, P(), vector, vector, owned, owned) + (P(),) * 7,
        out_specs=(rows, rows, owned, owned) + (P(),) * 7,
        check_vma=False,
    )
```

time: 559 us -> 543 us (0.971)
  waiting for transfers between devices: 78.3 us -> 106 us
  local copies, waits for them, and re-layouts: 57.4 us -> 38.2 us
  matrix products: 40.1 us -> 25.7 us
  Pallas kernels: 267 us -> 256 us
    ppermute x16, waiting for transfers between devices: 30.1 us -> 56.9 us  [fw(): lax.ppermute(x, 'shard', [(RING[i], RING[(i + 1) % 8]) for i in range(8)])]
    pallas_call x3 -> x7, Pallas kernels: 42.8 us -> 66.9 us  [the longest x3 35.4 us: across_rows(): pl.pallas_call(across_kernel, out_shape=(part, jax.ShapeDtypeStruct((m, r...]
    pallas_call x4 -> x3, Pallas kernels: 85.4 us -> 67.9 us  [scan_backward(): pl.pallas_call(bwd_kernel if into is None else bwd_into, out_shape=(jax.S...]
    dot_general x1 -> x0, matrix products: 15.8 us -> none  [shards(): lax.dot_general(gproj, all_normed, TN, preferred_element_type=F32)]
    pallas_call x2, Pallas kernels: 45.5 us -> 32.7 us  [scan_forward(): pl.pallas_call(fwd_kernel if into is None else fwd_into, out_shape=jax.Sh...]
    unnamed x108 -> x128, local copies, waits for them, and re-layouts: 28.5 us -> 17.4 us
    ppermute x26 -> x27, waiting for transfers between devices: 30.4 us -> 20.9 us  [swap(): return lax.ppermute(x, 'rep', [(i, i ^ d) for i in range(4)])]
    ppermute x3, waiting for transfers between devices: 6.81 us -> 15 us  [shards(): lax.ppermute(v, 'shard', [(i, i ^ d) for i in range(n)])]
  transfers between devices with their start and end apart: 61 -> 62, of which waited for: 21 -> 27; matrix products, arithmetic and copies ran while one was open for 19% -> 15% of each run, Pallas kernels for 34% -> 32%
where the time goes in v3:
time: 543 us; the launch traced here: 536 us
  Pallas kernels  256 us (47%)
  waiting for transfers between devices  106 us (20%)
  starting transfers between devices  56.3 us (10%)
  other arithmetic  50.5 us (9%)
  local copies, waits for them, and re-layouts  38.2 us (7%)
  matrix products  25.7 us (5%)
    pallas_call x3, Pallas kernels, scan_backward(): pl.pallas_call(bwd_kernel if into is None else bwd_into, out_shape=(jax.S...  67.9 us
    ppermute x16, waiting for transfers between devices, fw(): lax.ppermute(x, 'shard', [(RING[i], RING[(i + 1) % 8]) for i in range(8)])  56.9 us
    pallas_call x3, Pallas kernels, normed_gradient(): pl.pallas_call(back_kernel, out_shape=(jax.ShapeDtypeStruct((count * TOK,...  38 us
    pallas_call x3, Pallas kernels, across_rows(): pl.pallas_call(across_kernel, out_shape=(part, jax.ShapeDtypeStruct((m, r...  35.4 us
    pallas_call x2, Pallas kernels, scan_forward(): pl.pallas_call(fwd_kernel if into is None else fwd_into, out_shape=jax.Sh...  32.7 us
    ppermute x27, waiting for transfers between devices, swap(): return lax.ppermute(x, 'rep', [(i, i ^ d) for i in range(4)])  20.9 us
    ppermute x16, starting transfers between devices, fw(): lax.ppermute(x, 'shard', [(RING[i], RING[(i + 1) % 8]) for i in range(8)])  20.4 us
    convert_element_type x12, other arithmetic, add16(): return (a.astype(F32) + b.astype(F32)).astype(BF)  18.3 us
  transfers between devices with their start and end apart: 62, of which 27 were waited for; matrix products, arithmetic and copies ran while one was open for 15% of the time, Pallas kernels for 32%

profile of v3, /device:TPU:0, one launch (start us, length us, event | category | flops | bytes accessed | tf_op | source)
XLA Modules:
  0.0 536.4 jit_solution(3456756430489296909)
XLA Ops:
  13.6 12.1 %collective-permute-done = bf16[1296,256]{1,0:T(8,128)(2,1)S(1)} collective-permute-done((bf16[1296,256]{1,0:T(8,128)(2,1)S(1)}, bf16[1296,256]{1,0:T(8,128)(2,1)S(1)}, u32[]{:S(2)}, u32[]{:S(2)}) %collective-permute-start) | collective-permute-done | bytes 663584 | tf_op jit(solution)/shard_map/ppermute | solution.py:859
  30.9 12.5 %collective-permute-done.3 = bf16[1296,256]{1,0:T(8,128)(2,1)S(1)} collective-permute-done((bf16[1296,256]{1,0:T(8,128)(2,1)S(1)}, bf16[1296,256]{1,0:T(8,128)(2,1)S(1)}, u32[]{:S(2)}, u32[]{:S(2)}) %collective-permute-start.3) | collective-permute-done | bytes 663584 | tf_op jit(solution)/shard_map/ppermute | solution.py:859
  46.8 13.2 %collective-permute-done.5 = bf16[1296,256]{1,0:T(8,128)(2,1)S(1)} collective-permute-done((bf16[1296,256]{1,0:T(8,128)(2,1)S(1)}, bf16[1296,256]{1,0:T(8,128)(2,1)S(1)}, u32[]{:S(2)}, u32[]{:S(2)}) %collective-permute-start.5) | collective-permute-done | bytes 663584 | tf_op jit(solution)/shard_map/ppermute | solution.py:859
  85.5 15.0 %convolution_convert_fusion.1.xs_ref.bc_ref.dt_ref.refs_0_.refs_1_.refs_2_ = bf16[2048,1296]{1,0:T(8,128)(2,1)} fusion(bf16[2048,2048]{1,0:T(8,128)(2,1)S(1)} %pad_maximum_fusion.norm_ref.b_ref, bf16[1296,2048]{1,0:T(8,128)(2,1)S(1)} %maximum_dynamic-update-slice_fusion.wa_ref), kind=kOutput, calls=%fused_computation.4 | convolution fusion | flops 10874290176 | bytes 19005440 | tf_op jit(solution)/shard_map/dot_general | solution.py:37
  110.6 16.4 %shard_map.242.refs_6_ = f32[2048,1024]{1,0:T(8,128)} custom-call(s32[2,2]{1,0:T(2,128)S(1)} %pad_add_fusion.bnd, bf16[2048,1296]{1,0:T(8,128)(2,1)S(1)} %copy-done.2, bf16[2048,1296]{1,0:T(8,128)(2,1)S(1)} %copy-done.2, bf16[2048,1296]{1,0:T(8,128)(2,1)S(1)} %copy-done.2, f32[8,1280]{1,0:T(8,128)S(1)} %pad_maximum_fusion.10.cwx_ref.cwb_ref.refs_3_.refs_4_, ...), custom_call_target="tpu_custom_call" | custom-call | flops 1000000000 | bytes 500000 | tf_op jit(solution)/shard_map/pallas_call | solution.py:350
  136.1 16.3 %shard_map.243.scan_ref.refs_6_ = f32[2048,1024]{1,0:T(8,128)} custom-call(s32[2,2]{1,0:T(2,128)S(1)} %pad_add_fusion.1.bnd, bf16[2048,1296]{1,0:T(8,128)(2,1)S(1)} %copy-done.3, bf16[2048,1296]{1,0:T(8,128)(2,1)S(1)} %copy-done.3, bf16[2048,1296]{1,0:T(8,128)(2,1)S(1)} %copy-done.3, ...), custom_call_target="tpu_custom_call", output_to_operand_aliasing={{}: (7, {})} | custom-call | flops 1000000000 | bytes 500000 | tf_op jit(solution)/shard_map/pallas_call | solution.py:350
  159.1 6.1 %pad_maximum_fusion.1.gout_ref = bf16[2048,2048]{1,0:T(8,128)(2,1)} fusion(bf16[512,2048]{1,0:T(8,128)(2,1)S(1)} %collective-permute-done.22, bf16[512,2048]{1,0:T(8,128)(2,1)} %collective-permute-done.16, bf16[512,2048]{1,0:T(8,128)(2,1)} %collective-permute-done.17, bf16[512,2048]{1,0:T(8,128)(2,1)S(1)} %copy-done.21), kind=kLoop, calls=%fused_computation.2 | loop fusion | flops 33554432 | bytes 16777216 | tf_op jit(solution)/shard_map/concatenate | solution.py:989
  171.5 15.8 %shard_map.244 = (bf16[2048,1024]{1,0:T(8,128)(2,1)}, bf16[1024,2048]{1,0:T(8,128)(2,1)}, bf16[1024,2048]{1,0:T(8,128)(2,1)}) custom-call(s32[8]{0:T(128)S(1)} %fusion.3.perm, bf16[2048,2048]{1,0:T(8,128)(2,1)} %pad_maximum_fusion.1.gout_ref, bf16[2048,256]{1,0:T(8,128)(2,1)S(1)} %shard_map.241.refs_0_, bf16[2048,256]{1,0:T(8,128)(2,1)} %collective-permute-done.11.refs_1_, ...), custom_call_target="tpu_custom_call" | custom-call | flops 536870912 | bytes 1835008 | tf_op jit(solution)/shard_map/pallas_call | solution.py:426
  187.3 16.5 %shard_map.245 = (bf16[2048,1024]{1,0:T(8,128)(2,1)S(1)}, f32[4,8,512]{2,1,0:T(8,128)S(1)}) custom-call(bf16[2048,2048]{1,0:T(8,128)(2,1)} %copy-done.18, bf16[1024,2048]{1,0:T(8,128)(2,1)} %get-tuple-element.178.w_ref.wb_ref, f32[2048,1024]{1,0:T(8,128)} %shard_map.243.scan_ref.refs_6_, bf16[2048,1024]{1,0:T(8,128)(2,1)} %get-tuple-element.180.gin_ref, ...), custom_call_target="tpu_custom_call" | custom-call | flops 536870912 | bytes 1835008 | tf_op jit(solution)/shard_map/pallas_call | solution.py:488
  211.5 13.4 %shard_map.246 = (bf16[2048,1024]{1,0:T(8,128)(2,1)S(1)}, bf16[2048,1024]{1,0:T(8,128)(2,1)}, bf16[2048,1024]{1,0:T(8,128)(2,1)}, f32[8,1024]{1,0:T(8,128)S(1)}) custom-call(f32[4,8,512]{2,1,0:T(8,128)S(1)} %pad_maximum_fusion.9.sum_ref, f32[2048,1024]{1,0:T(8,128)} %shard_map.243.scan_ref.refs_6_, bf16[2048,1024]{1,0:T(8,128)(2,1)} %copy-done.12, ...), custom_call_target="tpu_custom_call" | custom-call | bytes 1835008 | tf_op jit(solution)/shard_map/pallas_call | solution.py:537
  226.9 15.0 %shard_map.247 = bf16[1024,2048]{1,0:T(8,128)(2,1)S(1)} custom-call(s32[8]{0:T(128)S(1)} %fusion.3.perm, bf16[2048,1024]{1,0:T(8,128)(2,1)} %copy-done.13, bf16[2048,2048]{1,0:T(8,128)(2,1)} %pad_maximum_fusion.1.gout_ref), custom_call_target="tpu_custom_call" | custom-call | flops 536870912 | bytes 1048576 | tf_op jit(solution)/shard_map/pallas_call | solution.py:453
  243.1 16.8 %shard_map.248 = (bf16[1024,2048]{1,0:T(8,128)(2,1)S(1)}, bf16[1024,2048]{1,0:T(8,128)(2,1)}) custom-call(bf16[2048,1024]{1,0:T(8,128)(2,1)} %get-tuple-element.185.a_ref.b_ref, bf16[2048,2048]{1,0:T(8,128)(2,1)} %copy-done.18), custom_call_target="tpu_custom_call" | custom-call | flops 536870912 | bytes 1048576 | tf_op jit(solution)/shard_map/pallas_call | solution.py:605
  263.4 10.7 %convolution_convert_fusion = bf16[2048,2048]{1,0:T(8,128)(2,1)S(1)} fusion(bf16[2048,1024]{1,0:T(8,128)(2,1)S(1)} %copy-done.14, bf16[1024,2048]{1,0:T(8,128)(2,1)} %get-tuple-element.191), kind=kOutput, calls=%fused_computation.3 | convolution fusion | flops 8594128896 | bytes 16777216 | tf_op jit(solution)/shard_map/dot_general | solution.py:33
  282.9 32.1 %shard_map.249 = (bf16[2048,1296]{1,0:T(8,128)(2,1)}, f32[8,1280]{1,0:T(8,128)S(1)}, f32[8,128]{1,0:T(8,128)S(1)}) custom-call(s32[2,2]{1,0:T(2,128)S(1)} %pad_add_fusion.1.bnd, bf16[2048,1296]{1,0:T(8,128)(2,1)} %convolution_convert_fusion.1.xs_ref.bc_ref.dt_ref.refs_0_.refs_1_.refs_2_, ...), custom_call_target="tpu_custom_call" | custom-call | flops 2000000000 | bytes 750000 | tf_op jit(solution)/shard_map/pallas_call | solution.py:372
  321.0 10.7 %shard_map.250 = (bf16[512,2048]{1,0:T(8,128)(2,1)S(1)}, f32[8,2048]{1,0:T(8,128)S(1)}) custom-call(bf16[2048,1296]{1,0:T(8,128)(2,1)} %get-tuple-element.209.a_ref.refs_8_, bf16[1296,2048]{1,0:T(8,128)(2,1)} %copy-done.19, bf16[2048,1024]{1,0:T(8,128)(2,1)} %get-tuple-element.185.a_ref.b_ref, bf16[1024,2048]{1,0:T(8,128)(2,1)} %get-tuple-element.178.w_ref.wb_ref, ...), custom_call_target="tpu_custom_call" | custom-call | flops 304087040 | bytes 593920 | tf_op jit(solution)/shard_map/pallas_call | solution.py:569
  336.3 17.9 %shard_map.251 = (bf16[2048,1296]{1,0:T(8,128)(2,1)}, f32[8,1280]{1,0:T(8,128)S(1)}, f32[8,128]{1,0:T(8,128)S(1)}) custom-call(s32[1,2]{1,0:T(1,128)S(1)} %add_bitcast_fusion.bnd, bf16[2048,1296]{1,0:T(8,128)(2,1)} %convolution_convert_fusion.1.xs_ref.bc_ref.dt_ref.refs_0_.refs_1_.refs_2_, ...), custom_call_target="tpu_custom_call", output_to_operand_aliasing={{0}: (9, {})} | custom-call | flops 1000000000 | bytes 375000 | tf_op jit(solution)/shard_map/pallas_call | solution.py:372
  364.8 10.7 %shard_map.252 = (bf16[512,2048]{1,0:T(8,128)(2,1)S(1)}, f32[8,2048]{1,0:T(8,128)S(1)}) custom-call(bf16[2048,1296]{1,0:T(8,128)(2,1)} %get-tuple-element.220.a_ref.refs_8_, bf16[1296,2048]{1,0:T(8,128)(2,1)} %copy-done.19, bf16[2048,1024]{1,0:T(8,128)(2,1)} %get-tuple-element.185.a_ref.b_ref, bf16[1024,2048]{1,0:T(8,128)(2,1)} %get-tuple-element.178.w_ref.wb_ref, ...), custom_call_target="tpu_custom_call" | custom-call | flops 304087040 | bytes 593920 | tf_op jit(solution)/shard_map/pallas_call | solution.py:569
  378.5 17.9 %shard_map.253 = (bf16[2048,1296]{1,0:T(8,128)(2,1)}, f32[8,1280]{1,0:T(8,128)S(1)}, f32[8,128]{1,0:T(8,128)S(1)}) custom-call(s32[1,2]{1,0:T(1,128)S(1)} %collective-permute-done.15.bnd, bf16[2048,1296]{1,0:T(8,128)(2,1)} %convolution_convert_fusion.1.xs_ref.bc_ref.dt_ref.refs_0_.refs_1_.refs_2_, ...), custom_call_target="tpu_custom_call", output_to_operand_aliasing={{0}: (9, {})} | custom-call | flops 1000000000 | bytes 375000 | tf_op jit(solution)/shard_map/pallas_call | solution.py:372
  408.2 14.0 %shard_map.255 = bf16[1296,1792]{1,0:T(8,128)(2,1)S(1)} custom-call(bf16[1296,2048]{1,0:T(8,128)(2,1)} %copy-done.10, bf16[2048,2048]{1,0:T(8,128)(2,1)} %copy-done.18), custom_call_target="tpu_custom_call" | custom-call | flops 594542592 | bytes 1080832 | tf_op jit(solution)/shard_map/pallas_call | solution.py:605
  430.7 16.7 %shard_map.256 = (bf16[1024,2048]{1,0:T(8,128)(2,1)S(1)}, f32[8,2048]{1,0:T(8,128)S(1)}) custom-call(bf16[2048,1296]{1,0:T(8,128)(2,1)} %get-tuple-element.241.a_ref, bf16[1296,2048]{1,0:T(8,128)(2,1)} %copy-done.19, bf16[2048,1024]{1,0:T(8,128)(2,1)} %get-tuple-element.185.a_ref.b_ref, bf16[1024,2048]{1,0:T(8,128)(2,1)} %get-tuple-element.178.w_ref.wb_ref, ...), custom_call_target="tpu_custom_call" | custom-call | flops 608174080 | bytes 593920 | tf_op jit(solution)/shard_map/pallas_call | solution.py:569
  460.5 6.1 %multiply_convert_fusion = bf16[512,2048]{1,0:T(8,128)(2,1)} fusion(bf16[512,2048]{1,0:T(8,128)(2,1)} %collective-permute-done.39, bf16[512,2048]{1,0:T(8,128)(2,1)} %copy-done.29, bf16[512,2048]{1,0:T(8,128)(2,1)S(1)} %copy-done.6, bf16[2048,2048]{1,0:T(8,128)(2,1)} %copy-done.20, f32[512]{0:T(512)S(1)} %copy-done.52), kind=kLoop, calls=%fused_computation.5 | loop fusion | flops 9437184 | bytes 10487808 | tf_op jit(solution)/shard_map/convert_element_type | solution.py:1092
  468.0 9.1 %collective-permute-done.50 = f32[224,128]{1,0:T(8,128)S(1)} collective-permute-done((f32[224,128]{1,0:T(8,128)S(1)}, f32[224,128]{1,0:T(8,128)S(1)}, u32[]{:S(2)}, u32[]{:S(2)}) %collective-permute-start.50) | collective-permute-done | bytes 114720 | tf_op jit(solution)/shard_map/ppermute | solution.py:1089
  485.8 7.1 %shard_map.257 = f32[512,2048]{1,0:T(8,128)} custom-call(s32[8]{0:T(128)S(1)} %fusion.3.perm, bf16[512,2048]{1,0:T(8,128)(2,1)S(1)} %copy-done.6, bf16[512,2048]{1,0:T(8,128)(2,1)S(1)} %copy-done.9, f32[512,1]{1,0:T(8,128)S(1)} %copy.35.keep_ref, f32[1,2048]{1,0:T(1,128)S(1)} %bitcast.48, bf16[512,2048]{1,0:T(8,128)(2,1)} %get-tuple-element.295.one_ref, ...), custom_call_target="tpu_custom_call" | custom-call | bytes 14680064 | tf_op jit(solution)/shard_map/pallas_call | solution.py:744
  506.3 9.3 %collective-permute-done.56.three = bf16[1296,256]{1,0:T(8,128)(2,1)S(1)} collective-permute-done((bf16[1296,256]{1,0:T(8,128)(2,1)S(1)}, bf16[1296,256]{1,0:T(8,128)(2,1)S(1)}, u32[]{:S(2)}, u32[]{:S(2)}) %collective-permute-start.56) | collective-permute-done | bytes 663584 | tf_op jit(solution)/shard_map/ppermute | solution.py:855
  (361 shorter events, 201.5 us)
Async XLA Ops:
  10.2 55.3 %collective-permute-start.9 = (bf16[512,2048]{1,0:T(8,128)(2,1)S(1)}, bf16[512,2048]{1,0:T(8,128)(2,1)}, u32[]{:S(2)}, u32[]{:S(2)}) collective-permute-start(bf16[512,2048]{1,0:T(8,128)(2,1)S(1)} %shard_map.239), channel_id=1, source_target_pairs={{0,16},{8,24},{16,0},{24,8},{1,17},{9,25},{17,1},{25,9},{2,18},{10... | collective-permute-start | bytes 6291464 | tf_op jit(solution)/shard_map/ppermute | solution.py:855
  70.8 37.1 %collective-permute-start.15 = (s32[1,2]{1,0:T(1,128)S(1)}, s32[1,2]{1,0:T(1,128)S(1)}, u32[]{:S(2)}, u32[]{:S(2)}) collective-permute-start(s32[1,2]{1,0:T(1,128)S(1)} %add_bitcast_fusion.bnd), channel_id=1, source_target_pairs={{0,8},{8,0},{16,24},{24,16},{1,9},{9,1},{17,25},{25,17},{2,10},{10... | collective-permute-start | bytes 32 | tf_op jit(solution)/shard_map/ppermute | solution.py:855
  76.6 50.3 %collective-permute-start.16 = (bf16[512,2048]{1,0:T(8,128)(2,1)}, bf16[512,2048]{1,0:T(8,128)(2,1)}, u32[]{:S(2)}, u32[]{:S(2)}) collective-permute-start(bf16[512,2048]{1,0:T(8,128)(2,1)} %multiply_convert_fusion.1), channel_id=1, source_target_pairs={{0,16},{8,24},{16,0},{24,8},{1,17},{9,25},{17,1},{25,9},{2,18},{10... | collective-permute-start | bytes 6291464 | tf_op jit(solution)/shard_map/ppermute | solution.py:855
  78.2 48.7 %collective-permute-start.17 = (bf16[512,2048]{1,0:T(8,128)(2,1)}, bf16[512,2048]{1,0:T(8,128)(2,1)}, u32[]{:S(2)}, u32[]{:S(2)}) collective-permute-start(bf16[512,2048]{1,0:T(8,128)(2,1)} %multiply_convert_fusion.1), channel_id=1, source_target_pairs={{0,8},{8,0},{16,24},{24,16},{1,9},{9,1},{17,25},{25,17},{2,10},{10... | collective-permute-start | bytes 6291464 | tf_op jit(solution)/shard_map/ppermute | solution.py:855
  78.6 25.7 %collective-permute-start.11 = (bf16[2048,256]{1,0:T(8,128)(2,1)S(1)}, bf16[2048,256]{1,0:T(8,128)(2,1)}, u32[]{:S(2)}, u32[]{:S(2)}) collective-permute-start(bf16[2048,256]{1,0:T(8,128)(2,1)S(1)} %shard_map.241.refs_0_), channel_id=1, source_target_pairs={{0,2},{2,4},{4,6},{6,7},{7,5},{5,3},{3,1},{1,0},{8,10},{10,12},{12... | collective-permute-start | bytes 3145736 | tf_op jit(solution)/shard_map/ppermute | solution.py:859
  79.6 25.4 %collective-permute-start.12 = (bf16[2048,256]{1,0:T(8,128)(2,1)S(1)}, bf16[2048,256]{1,0:T(8,128)(2,1)}, u32[]{:S(2)}, u32[]{:S(2)}) collective-permute-start(bf16[2048,256]{1,0:T(8,128)(2,1)S(1)} %shard_map.241.refs_0_), channel_id=1, source_target_pairs={{2,0},{4,2},{6,4},{7,6},{5,7},{3,5},{1,3},{0,1},{10,8},{12,10},{14... | collective-permute-start | bytes 3145736 | tf_op jit(solution)/shard_map/ppermute | solution.py:863
  105.1 24.7 %collective-permute-start.13 = (bf16[2048,256]{1,0:T(8,128)(2,1)}, bf16[2048,256]{1,0:T(8,128)(2,1)S(1)}, u32[]{:S(2)}, u32[]{:S(2)}) collective-permute-start(bf16[2048,256]{1,0:T(8,128)(2,1)} %collective-permute-done.11.refs_1_), channel_id=1, source_target_pairs={{0,2},{2,4},{4,6},{6,7},{7,5},{5,3},{3,1},{1,0},{8,10},{10,12},{12... | collective-permute-start | bytes 3145736 | tf_op jit(solution)/shard_map/ppermute | solution.py:859
  105.7 24.6 %collective-permute-start.14 = (bf16[2048,256]{1,0:T(8,128)(2,1)}, bf16[2048,256]{1,0:T(8,128)(2,1)S(1)}, u32[]{:S(2)}, u32[]{:S(2)}) collective-permute-start(bf16[2048,256]{1,0:T(8,128)(2,1)} %collective-permute-done.12.refs_2_), channel_id=1, source_target_pairs={{2,0},{4,2},{6,4},{7,6},{5,7},{3,5},{1,3},{0,1},{10,8},{12,10},{14... | collective-permute-start | bytes 3145736 | tf_op jit(solution)/shard_map/ppermute | solution.py:863
  130.3 26.1 %collective-permute-start.22 = (bf16[512,2048]{1,0:T(8,128)(2,1)}, bf16[512,2048]{1,0:T(8,128)(2,1)S(1)}, u32[]{:S(2)}, u32[]{:S(2)}) collective-permute-start(bf16[512,2048]{1,0:T(8,128)(2,1)} %collective-permute-done.16), channel_id=1, source_target_pairs={{0,8},{8,0},{16,24},{24,16},{1,9},{9,1},{17,25},{25,17},{2,10},{10... | collective-permute-start | bytes 6291464 | tf_op jit(solution)/shard_map/ppermute | solution.py:855
  130.3 25.6 %collective-permute-start.18 = (bf16[2048,256]{1,0:T(8,128)(2,1)S(1)}, bf16[2048,256]{1,0:T(8,128)(2,1)S(1)}, u32[]{:S(2)}, u32[]{:S(2)}) collective-permute-start(bf16[2048,256]{1,0:T(8,128)(2,1)S(1)} %collective-permute-done.13.refs_3_), channel_id=1, source_target_pairs={{0,2},{2,4},{4,6},{6,7},{7,5},{5,3},{3,1},{1,0},{8,10},{10,12},{12... | collective-permute-start | bytes 3145736 | tf_op jit(solution)/shard_map/ppermute | solution.py:859
  130.8 25.5 %collective-permute-start.19 = (bf16[2048,256]{1,0:T(8,128)(2,1)S(1)}, bf16[2048,256]{1,0:T(8,128)(2,1)S(1)}, u32[]{:S(2)}, u32[]{:S(2)}) collective-permute-start(bf16[2048,256]{1,0:T(8,128)(2,1)S(1)} %collective-permute-done.14.refs_4_), channel_id=1, source_target_pairs={{2,0},{4,2},{6,4},{7,6},{5,7},{3,5},{1,3},{0,1},{10,8},{12,10},{14... | collective-permute-start | bytes 3145736 | tf_op jit(solution)/shard_map/ppermute | solution.py:863
  280.8 34.2 %collective-permute-start.32 = (bf16[512,2048]{1,0:T(8,128)(2,1)}, bf16[512,2048]{1,0:T(8,128)(2,1)S(1)}, u32[]{:S(2)}, u32[]{:S(2)}) collective-permute-start(bf16[512,2048]{1,0:T(8,128)(2,1)} %get-tuple-element.200), channel_id=1, source_target_pairs={{0,8},{8,0},{16,24},{24,16},{1,9},{9,1},{17,25},{25,17},{2,10},{10... | collective-permute-start | bytes 6291464 | tf_op jit(solution)/shard_map/ppermute | solution.py:855
  280.9 34.2 %collective-permute-start.30 = (bf16[2048,256]{1,0:T(8,128)(2,1)}, bf16[2048,256]{1,0:T(8,128)(2,1)S(1)}, u32[]{:S(2)}, u32[]{:S(2)}) collective-permute-start(bf16[2048,256]{1,0:T(8,128)(2,1)} %pad_maximum_fusion.4), channel_id=1, source_target_pairs={{0,2},{2,4},{4,6},{6,7},{7,5},{5,3},{3,1},{1,0},{8,10},{10,12},{12... | collective-permute-start | bytes 3145736 | tf_op jit(solution)/shard_map/ppermute | solution.py:859
  282.2 32.8 %collective-permute-start.31 = (bf16[2048,256]{1,0:T(8,128)(2,1)S(1)}, bf16[2048,256]{1,0:T(8,128)(2,1)S(1)}, u32[]{:S(2)}, u32[]{:S(2)}) collective-permute-start(bf16[2048,256]{1,0:T(8,128)(2,1)S(1)} %pad_maximum_fusion.5), channel_id=1, source_target_pairs={{2,0},{4,2},{6,4},{7,6},{5,7},{3,5},{1,3},{0,1},{10,8},{12,10},{14... | collective-permute-start | bytes 3145736 | tf_op jit(solution)/shard_map/ppermute | solution.py:863
  282.9 71.3 %collective-permute-start.35 = (bf16[512,2048]{1,0:T(8,128)(2,1)}, bf16[512,2048]{1,0:T(8,128)(2,1)S(1)}, u32[]{:S(2)}, u32[]{:S(2)}) collective-permute-start(bf16[512,2048]{1,0:T(8,128)(2,1)} %get-tuple-element.289), channel_id=1, source_target_pairs={{0,8},{8,0},{16,24},{24,16},{1,9},{9,1},{17,25},{25,17},{2,10},{10... | collective-permute-start | bytes 6291464 | tf_op jit(solution)/shard_map/ppermute | solution.py:855
  331.6 27.1 %collective-permute-start.36 = (bf16[512,2048]{1,0:T(8,128)(2,1)S(1)}, bf16[512,2048]{1,0:T(8,128)(2,1)S(1)}, u32[]{:S(2)}, u32[]{:S(2)}) collective-permute-start(bf16[512,2048]{1,0:T(8,128)(2,1)S(1)} %get-tuple-element.211), channel_id=1, source_target_pairs={{0,8},{8,0},{16,24},{24,16},{1,9},{9,1},{17,25},{25,17},{2,10},{10... | collective-permute-start | bytes 6291464 | tf_op jit(solution)/shard_map/ppermute | solution.py:855
  332.2 25.4 %collective-permute-start.33 = (bf16[2048,256]{1,0:T(8,128)(2,1)}, bf16[2048,256]{1,0:T(8,128)(2,1)}, u32[]{:S(2)}, u32[]{:S(2)}) collective-permute-start(bf16[2048,256]{1,0:T(8,128)(2,1)} %add_convert_fusion.6), channel_id=1, source_target_pairs={{0,2},{2,4},{4,6},{6,7},{7,5},{5,3},{3,1},{1,0},{8,10},{10,12},{12... | collective-permute-start | bytes 3145736 | tf_op jit(solution)/shard_map/ppermute | solution.py:859
  333.6 25.2 %collective-permute-start.34 = (bf16[2048,256]{1,0:T(8,128)(2,1)}, bf16[2048,256]{1,0:T(8,128)(2,1)}, u32[]{:S(2)}, u32[]{:S(2)}) collective-permute-start(bf16[2048,256]{1,0:T(8,128)(2,1)} %add_convert_fusion.5), channel_id=1, source_target_pairs={{2,0},{4,2},{6,4},{7,6},{5,7},{3,5},{1,3},{0,1},{10,8},{12,10},{14... | collective-permute-start | bytes 3145736 | tf_op jit(solution)/shard_map/ppermute | solution.py:863
  335.6 60.7 %collective-permute-start.39 = (bf16[512,2048]{1,0:T(8,128)(2,1)S(1)}, bf16[512,2048]{1,0:T(8,128)(2,1)}, u32[]{:S(2)}, u32[]{:S(2)}) collective-permute-start(bf16[512,2048]{1,0:T(8,128)(2,1)S(1)} %add_convert_fusion.1), channel_id=1, source_target_pairs={{0,16},{8,24},{16,0},{24,8},{1,17},{9,25},{17,1},{25,9},{2,18},{10... | collective-permute-start | bytes 6291464 | tf_op jit(solution)/shard_map/ppermute | solution.py:855
  362.7 33.6 %collective-permute-start.37 = (bf16[2048,256]{1,0:T(8,128)(2,1)S(1)}, bf16[2048,256]{1,0:T(8,128)(2,1)}, u32[]{:S(2)}, u32[]{:S(2)}) collective-permute-start(bf16[2048,256]{1,0:T(8,128)(2,1)S(1)} %add_convert_fusion.4), channel_id=1, source_target_pairs={{0,2},{2,4},{4,6},{6,7},{7,5},{5,3},{3,1},{1,0},{8,10},{10,12},{12... | collective-permute-start | bytes 3145736 | tf_op jit(solution)/shard_map/ppermute | solution.py:859
  364.3 32.0 %collective-permute-start.38 = (bf16[2048,256]{1,0:T(8,128)(2,1)}, bf16[2048,256]{1,0:T(8,128)(2,1)}, u32[]{:S(2)}, u32[]{:S(2)}) collective-permute-start(bf16[2048,256]{1,0:T(8,128)(2,1)} %add_convert_fusion.3), channel_id=1, source_target_pairs={{2,0},{4,2},{6,4},{7,6},{5,7},{3,5},{1,3},{0,1},{10,8},{12,10},{14... | collective-permute-start | bytes 3145736 | tf_op jit(solution)/shard_map/ppermute | solution.py:863
  378.0 44.3 %collective-permute-start.42 = (bf16[256,2048]{1,0:T(8,128)(2,1)}, bf16[256,2048]{1,0:T(8,128)(2,1)}, u32[]{:S(2)}, u32[]{:S(2)}) collective-permute-start(bf16[256,2048]{1,0:T(8,128)(2,1)} %get-tuple-element.312), channel_id=1, source_target_pairs={{0,16},{8,24},{16,0},{24,8},{1,17},{9,25},{17,1},{25,9},{2,18},{10... | collective-permute-start | bytes 3145736 | tf_op jit(solution)/shard_map/ppermute | solution.py:855
  466.6 32.2 %collective-permute-start.53 = (bf16[2048,256]{1,0:T(8,128)(2,1)S(1)}, bf16[2048,256]{1,0:T(8,128)(2,1)}, u32[]{:S(2)}, u32[]{:S(2)}) collective-permute-start(bf16[2048,256]{1,0:T(8,128)(2,1)S(1)} %add_convert_fusion.2.refs_0_), channel_id=1, source_target_pairs={{0,16},{8,24},{16,0},{24,8},{1,17},{9,25},{17,1},{25,9},{2,18},{10... | collective-permute-start | bytes 3145736 | tf_op jit(solution)/shard_map/ppermute | solution.py:855
  506.3 25.7 %collective-permute-start.55 = (bf16[1296,256]{1,0:T(8,128)(2,1)S(1)}, bf16[1296,256]{1,0:T(8,128)(2,1)}, u32[]{:S(2)}, u32[]{:S(2)}) collective-permute-start(bf16[1296,256]{1,0:T(8,128)(2,1)S(1)} %add_convert_fusion.7.one), channel_id=1, source_target_pairs={{0,8},{8,0},{16,24},{24,16},{1,9},{9,1},{17,25},{25,17},{2,10},{10... | collective-permute-start | bytes 1990664 | tf_op jit(solution)/shard_map/ppermute | solution.py:855
  (97 other events, 1428.8 us)

commit v4 on v3

--- a/solution.py
+++ b/solution.py
@@ -593,15 +593,15 @@
             kept[...] = turned[...]
     else:
         turned = a_ref
-    out_ref[...] = mm(turned[...], b_ref[...]).astype(out_ref.dtype)
+    out_ref[0] = mm(turned[...], b_ref[...]).astype(out_ref.dtype)
 
 
 def across_rows(a, b, first, count, turn):
     rows, n = b.shape
     m = a.shape[1] if turn else a.shape[0]
     whole = pl.BlockSpec(a.shape, lambda k: (0, 0))
-    part = jax.ShapeDtypeStruct((m, count * 256), BF)
-    spec = pl.BlockSpec((m, 256), lambda k: (0, k))
+    part = jax.ShapeDtypeStruct((count, m, 256), BF)
+    spec = pl.BlockSpec((1, m, 256), lambda k: (k, 0, 0))
     return pl.pallas_call(
         across_kernel,
         out_shape=(part, jax.ShapeDtypeStruct((m, rows), BF)) if turn else part,
@@ -801,7 +801,7 @@
             scratch_shapes=[pltpu.VMEM((4 * TILES * LANES, lanes), F32), pltpu.SemaphoreType.DMA],
         ),
         compiler_params=params("arbitrary", mib=48),
-        cost_estimate=cost(0, 20e6),
+        cost_estimate=cost(0, 320e6),
     )(me, *pieces)
 
 
@@ -965,15 +965,16 @@
         *sent, gout = tie(*sent, gout)
         sent = steps.send(sent)
         sent = steps.send(tie(*sent))
-        *sent, chip, two = tie(*sent, chip, two)
+        near = jnp.concatenate(pieces[:7] + [jnp.zeros_like(rest)], 1)
+        *sent, chip, two, near = tie(*sent, chip, two, near)
         steps.send(sent)
-        rest_pieces = pieces
+        rest_far = pieces[7]
 
         pieces = []
         steps = ring_pieces(two, pieces)
         sent = next(steps)
         far, gchip, gcore = swap(chip, 1), swap(gout, 2), swap(gout, 1)
-        w_rest = jnp.concatenate(rest_pieces, 1)
+        w_rest = lax.dynamic_update_slice(near, rest_far, (0, 7 * rest.shape[1]))
         all_normed = jnp.concatenate([normed, core, chip, far], 0)
         all_normed, w_rest = tie(all_normed, w_rest)
         proj = mm_nt(all_normed, w_rest).astype(BF)
@@ -1037,7 +1038,7 @@
     if ring:
         outs = columns_of(out_terms(perm, inner, all_gout))
         (dgate, _) = tie(dgate, outs[7])
-        terms8 = columns_of(across_rows(dgate, all_normed, 0, 8, True)[0])
+        terms8 = columns_of(lax.dot_general(dgate, all_normed, TN, preferred_element_type=F32).astype(BF))
         terms8 = [jnp.concatenate(p, 0) for p in zip(terms8, outs)]
         steps = ring_sum()
         next(steps)
@@ -1052,31 +1053,31 @@
         *sent, gproj, far = tie(*sent, gproj, far)
         sent, gproj, chip = launch(steps, sent, gproj, add16(b2, far))
         core, chip = swap(b1, 1), swap(chip, 2)
-        grad3, dgo = final(gproj, first=3, count=1)
-        (gproj, grad3) = tie(gproj, grad3)
-        far = swap(grad3, 1)
+        late, dgo = final(gproj, first=2, count=2)
+        *sent, gproj, core, late = tie(*sent, gproj, core, late)
+        sent, gproj, late = launch(steps, sent, gproj, late)
+        far = swap(late[TOK:], 1)
         gproj, d, e = back(dscan, 0, 1, gproj)
         dcw, dhp = dcw + d, dhp + e
-        *sent, gproj, core, far = tie(*sent, gproj, core, far)
-        sent, gproj = launch(steps, sent, gproj)
-        grad2, d = final(gproj, first=2, count=1)
-        dgo = dgo + d
-        (gproj, total) = tie(gproj, add16(grad2, far))
+        gproj, far = tie(gproj, far)
+        gproj, total = tie(gproj, add16(late[:TOK], far))
         gproj, d, e = back(dscan, 1, 1, gproj)
         dcw, dhp = dcw + d, dhp + e
-        *sent, gproj, chip = tie(*sent, gproj, chip)
+        *sent, gproj = tie(*sent, gproj)
         share, gproj = tie(steps.send(sent), gproj)
-        branch = (b0, core, chip)
         upper = swap(total[: TOK // 2], 2)
 
         far, turned_proj = across_rows(gproj, all_normed, 7, 1, True)
         steps = ring_sum()
         next(steps)
-        sent, turned_proj = launch(steps, far, turned_proj)
+        sent, turned_proj = launch(steps, far[0], turned_proj)
         gates = [share, swap(share, 1)]
         seven = across_rows(turned_proj, all_normed, 0, 7, False)
-        *sent, seven, gproj, upper, lower, share = tie(*sent, seven, gproj, upper, total[TOK // 2 :], share)
-        sent, gproj, lower = launch(steps, (*sent, columns_of(seven)), gproj, lower)
+        *sent, seven, gproj, upper, lower, share, chip = tie(
+            *sent, seven, gproj, upper, total[TOK // 2 :], share, chip
+        )
+        branch = (b0, core, chip)
+        sent, gproj, lower = launch(steps, (*sent, list(seven)), gproj, lower)
         lower = swap(lower, 2)
         early, d = final(gproj, first=0, count=2)
         dgo = dgo + d
@@ -1084,27 +1085,27 @@
         sent, early, share, dgo = launch(steps, sent, early, share, dgo)
         gates.append(swap(share, 2))
         core = swap(early[TOK:], 1)
-        small = small_vector(dcw, dhp, dgo, dgain)
         bits = [1 << k for k in range(n.bit_length() - 1)]
         flip = lambda v, d: v + lax.ppermute(v, "shard", [(i, i ^ d) for i in range(n)])
+        layer_out = (keep * (tokens.astype(F32) + sum(b.astype(F32) for b in branch))).astype(BF)
+        *sent, core, layer_out, dgo = tie(*sent, core, layer_out, dgo)
+        sent, core, dgo = launch(steps, sent, core, dgo)
+        small = small_vector(dcw, dhp, dgo, dgain)
         small = small + swap(small, 1)
-        small = flip(small, bits[0])
-        layer_out = (keep * (tokens.astype(F32) + sum(b.astype(F32) for b in branch))).astype(BF)
-        *sent, core, layer_out, small = tie(*sent, core, layer_out, small)
-        sent, core, small = launch(steps, sent, core, small)
-        small = flip(small, bits[1])
         parts = [early[:TOK], core, jnp.concatenate([upper, lower], 0)]
         grad_tokens = last_rows(perm, tokens, cotangent, keep, gain_outer[None, :], parts)
         *sent, gates[2], grad_tokens, small = tie(*sent, gates[2], grad_tokens, small)
         share, small, gates[2] = tie(steps.send(sent), small, gates[2])
         rests = [share, swap(share, 1), swap(share, 2)]
         gates.append(swap(gates[2], 1))
+        for d in bits:
+            small = flip(small, d)
         grad_in, grad_out_weight = first_join(me, gates, width)
-        for d in bits[2:]:
-            small = flip(small, d)
+        rests[2], grad_in = tie(rests[2], grad_in)
         small = small + swap(small, 2)
         rests.append(swap(rests[2], 1))
     else:
+        side = lambda x: jnp.concatenate(list(x), 1)
         rows_sum = lambda x, axis: lax.psum_scatter(
             x.astype(F32), "shard", scatter_dimension=axis, tiled=True
         ).astype(BF)
@@ -1120,8 +1121,8 @@
         spread = grad_out.reshape(TILES, 1, LANES, D).astype(F32) * (jnp.arange(4)[None, :, None, None] == r)
         spread = lax.psum_scatter(spread.reshape(DIN, D), "shard", scatter_dimension=0, tiled=True)
         grad_out_weight = lax.psum(spread, "rep")
-        gates = everyone(rows_sum(across_rows(dgate, all_normed, 0, 8, True)[0], 1))
-        rests = everyone(rows_sum(across_rows(gproj, all_normed, 0, 8, True)[0], 1))
+        gates = everyone(rows_sum(side(across_rows(dgate, all_normed, 0, 8, True)[0]), 1))
+        rests = everyone(rows_sum(side(across_rows(gproj, all_normed, 0, 8, True)[0]), 1))
         grad_in, _ = first_join(me, gates, width)
         small = lax.psum(small_vector(dcw, dhp, dgo, dgain), ("rep", "shard"))
     grad_in_weight = last_join(me, rests, grad_in).T

time: 543 us -> 531 us (0.978)
  Pallas kernels: 256 us -> 233 us
  matrix products: 25.7 us -> 37.2 us
    pallas_call x3 -> x2, Pallas kernels: 35.4 us -> 18.4 us  [across_rows(): pl.pallas_call(across_kernel, out_shape=(part, jax.ShapeDtypeStruct((m, r...]
    dot_general x0 -> x1, matrix products: none -> 11.5 us  [shards(): lax.dot_general(dgate, all_normed, TN, preferred_element_type=F32)]
    ppermute x16, waiting for transfers between devices: 56.9 us -> 67.8 us  [fw(): lax.ppermute(x, 'shard', [(RING[i], RING[(i + 1) % 8]) for i in range(8)])]
    ppermute x3, waiting for transfers between devices: 15 us -> 8.2 us  [shards(): lax.ppermute(v, 'shard', [(i, i ^ d) for i in range(n)])]
    ppermute x27, waiting for transfers between devices: 20.9 us -> 14.7 us  [swap(): return lax.ppermute(x, 'rep', [(i, i ^ d) for i in range(4)])]
    ppermute x16, waiting for transfers between devices: 13.1 us -> 19 us  [bw(): lax.ppermute(x, 'shard', [(RING[(i + 1) % 8], RING[i]) for i in range(8)])]
    pallas_call x3 -> x2, Pallas kernels: 38 us -> 33.4 us  [normed_gradient(): pl.pallas_call(back_kernel, out_shape=(jax.ShapeDtypeStruct((count * TOK,...]
    unnamed x128 -> x106, local copies, waits for them, and re-layouts: 17.4 us -> 14.5 us
  transfers between devices with their start and end apart: 62 -> 62, of which waited for: 27 -> 31; matrix products, arithmetic and copies ran while one was open for 15% -> 17% of each run, Pallas kernels for 32% -> 32%
where the time goes in v4:
time: 531 us; the launch traced here: 524 us
  Pallas kernels  233 us (44%)
  waiting for transfers between devices  110 us (21%)
  starting transfers between devices  51.5 us (10%)
  other arithmetic  50.2 us (9%)
  local copies, waits for them, and re-layouts  38.5 us (7%)
  matrix products  37.2 us (7%)
    pallas_call x3, Pallas kernels, scan_backward(): pl.pallas_call(bwd_kernel if into is None else bwd_into, out_shape=(jax.S...  68 us
    ppermute x16, waiting for transfers between devices, fw(): lax.ppermute(x, 'shard', [(RING[i], RING[(i + 1) % 8]) for i in range(8)])  67.8 us
    pallas_call x2, Pallas kernels, normed_gradient(): pl.pallas_call(back_kernel, out_shape=(jax.ShapeDtypeStruct((count * TOK,...  33.4 us
    pallas_call x2, Pallas kernels, scan_forward(): pl.pallas_call(fwd_kernel if into is None else fwd_into, out_shape=jax.Sh...  32.7 us
    ppermute x16, starting transfers between devices, fw(): lax.ppermute(x, 'shard', [(RING[i], RING[(i + 1) % 8]) for i in range(8)])  22 us
    ppermute x16, waiting for transfers between devices, bw(): lax.ppermute(x, 'shard', [(RING[(i + 1) % 8], RING[i]) for i in range(8)])  19 us
    pallas_call x2, Pallas kernels, across_rows(): pl.pallas_call(across_kernel, out_shape=(part, jax.ShapeDtypeStruct((m, r...  18.4 us
    pallas_call x1, Pallas kernels, gate_stats(): pl.pallas_call(stat_kernel, out_shape=(jax.ShapeDtypeStruct((rows, inner)...  16.5 us
  transfers between devices with their start and end apart: 62, of which 31 were waited for; matrix products, arithmetic and copies ran while one was open for 17% of the time, Pallas kernels for 32%

profile of v4, /device:TPU:0, one launch (start us, length us, event | category | flops | bytes accessed | tf_op | source)
XLA Modules:
  0.0 523.7 jit_solution(14623437724747380613)
XLA Ops:
  13.5 12.1 %collective-permute-done = bf16[1296,256]{1,0:T(8,128)(2,1)S(1)} collective-permute-done((bf16[1296,256]{1,0:T(8,128)(2,1)S(1)}, bf16[1296,256]{1,0:T(8,128)(2,1)S(1)}, u32[]{:S(2)}, u32[]{:S(2)}) %collective-permute-start) | collective-permute-done | bytes 663584 | tf_op jit(solution)/shard_map/ppermute | solution.py:859
  31.1 12.3 %collective-permute-done.3 = bf16[1296,256]{1,0:T(8,128)(2,1)S(1)} collective-permute-done((bf16[1296,256]{1,0:T(8,128)(2,1)S(1)}, bf16[1296,256]{1,0:T(8,128)(2,1)S(1)}, u32[]{:S(2)}, u32[]{:S(2)}) %collective-permute-start.3) | collective-permute-done | bytes 663584 | tf_op jit(solution)/shard_map/ppermute | solution.py:859
  47.0 12.9 %collective-permute-done.5 = bf16[1296,256]{1,0:T(8,128)(2,1)S(1)} collective-permute-done((bf16[1296,256]{1,0:T(8,128)(2,1)S(1)}, bf16[1296,256]{1,0:T(8,128)(2,1)S(1)}, u32[]{:S(2)}, u32[]{:S(2)}) %collective-permute-start.5) | collective-permute-done | bytes 663584 | tf_op jit(solution)/shard_map/ppermute | solution.py:859
  63.7 6.3 %collective-permute-done.8 = bf16[640,256]{1,0:T(8,128)(2,1)S(1)} collective-permute-done((bf16[640,256]{1,0:T(8,128)(2,1)S(1)}, bf16[640,256]{1,0:T(8,128)(2,1)S(1)}, u32[]{:S(2)}, u32[]{:S(2)}) %collective-permute-start.8) | collective-permute-done | bytes 327712 | tf_op jit(solution)/shard_map/ppermute | solution.py:863
  84.7 15.0 %convolution_convert_fusion.1.xs_ref.bc_ref.dt_ref.refs_0_.refs_1_.refs_2_ = bf16[2048,1296]{1,0:T(8,128)(2,1)} fusion(bf16[2048,2048]{1,0:T(8,128)(2,1)S(1)} %pad_maximum_fusion.norm_ref.b_ref, bf16[1296,2048]{1,0:T(8,128)(2,1)S(1)} %copy-done.22), kind=kOutput, calls=%fused_computation.4 | convolution fusion | flops 10874290176 | bytes 19005440 | tf_op jit(solution)/shard_map/dot_general | solution.py:37
  110.0 16.4 %shard_map.242.refs_6_ = f32[2048,1024]{1,0:T(8,128)} custom-call(s32[2,2]{1,0:T(2,128)S(1)} %pad_add_fusion.bnd, bf16[2048,1296]{1,0:T(8,128)(2,1)S(1)} %copy-done.2, bf16[2048,1296]{1,0:T(8,128)(2,1)S(1)} %copy-done.2, bf16[2048,1296]{1,0:T(8,128)(2,1)S(1)} %copy-done.2, f32[8,1280]{1,0:T(8,128)S(1)} %pad_maximum_fusion.10.cwx_ref.cwb_ref.refs_3_.refs_4_, ...), custom_call_target="tpu_custom_call" | custom-call | flops 1000000000 | bytes 500000 | tf_op jit(solution)/shard_map/pallas_call | solution.py:350
  135.5 16.3 %shard_map.243.scan_ref.refs_6_ = f32[2048,1024]{1,0:T(8,128)} custom-call(s32[2,2]{1,0:T(2,128)S(1)} %pad_add_fusion.1.bnd, bf16[2048,1296]{1,0:T(8,128)(2,1)S(1)} %copy-done.3, bf16[2048,1296]{1,0:T(8,128)(2,1)S(1)} %copy-done.3, bf16[2048,1296]{1,0:T(8,128)(2,1)S(1)} %copy-done.3, ...), custom_call_target="tpu_custom_call", output_to_operand_aliasing={{}: (7, {})} | custom-call | flops 1000000000 | bytes 500000 | tf_op jit(solution)/shard_map/pallas_call | solution.py:350
  158.3 6.0 %pad_maximum_fusion.1.gout_ref = bf16[2048,2048]{1,0:T(8,128)(2,1)} fusion(bf16[512,2048]{1,0:T(8,128)(2,1)S(1)} %collective-permute-done.22, bf16[512,2048]{1,0:T(8,128)(2,1)} %collective-permute-done.16, bf16[512,2048]{1,0:T(8,128)(2,1)} %collective-permute-done.17, bf16[512,2048]{1,0:T(8,128)(2,1)S(1)} %copy-done.25), kind=kLoop, calls=%fused_computation.2 | loop fusion | flops 33554432 | bytes 16777216 | tf_op jit(solution)/shard_map/concatenate | solution.py:990
  170.8 15.8 %shard_map.244 = (bf16[2048,1024]{1,0:T(8,128)(2,1)}, bf16[1024,2048]{1,0:T(8,128)(2,1)}, bf16[1024,2048]{1,0:T(8,128)(2,1)}) custom-call(s32[8]{0:T(128)S(1)} %fusion.11.perm, bf16[2048,2048]{1,0:T(8,128)(2,1)} %pad_maximum_fusion.1.gout_ref, bf16[2048,256]{1,0:T(8,128)(2,1)S(1)} %shard_map.241.refs_0_, bf16[2048,256]{1,0:T(8,128)(2,1)} %collective-permute-done.11.refs_1_, ...), custom_call_target="tpu_custom_call" | custom-call | flops 536870912 | bytes 1835008 | tf_op jit(solution)/shard_map/pallas_call | solution.py:426
  186.6 16.5 %shard_map.245 = (bf16[2048,1024]{1,0:T(8,128)(2,1)S(1)}, f32[4,8,512]{2,1,0:T(8,128)S(1)}) custom-call(bf16[2048,2048]{1,0:T(8,128)(2,1)} %copy-done.20, bf16[1024,2048]{1,0:T(8,128)(2,1)} %get-tuple-element.180.w_ref.wb_ref, f32[2048,1024]{1,0:T(8,128)} %shard_map.243.scan_ref.refs_6_, bf16[2048,1024]{1,0:T(8,128)(2,1)} %get-tuple-element.182.gin_ref, ...), custom_call_target="tpu_custom_call" | custom-call | flops 536870912 | bytes 1835008 | tf_op jit(solution)/shard_map/pallas_call | solution.py:488
  210.7 13.4 %shard_map.246 = (bf16[2048,1024]{1,0:T(8,128)(2,1)S(1)}, bf16[2048,1024]{1,0:T(8,128)(2,1)}, bf16[2048,1024]{1,0:T(8,128)(2,1)}, f32[8,1024]{1,0:T(8,128)S(1)}) custom-call(f32[4,8,512]{2,1,0:T(8,128)S(1)} %pad_maximum_fusion.9.sum_ref, f32[2048,1024]{1,0:T(8,128)} %shard_map.243.scan_ref.refs_6_, bf16[2048,1024]{1,0:T(8,128)(2,1)} %copy-done.12, ...), custom_call_target="tpu_custom_call" | custom-call | bytes 1835008 | tf_op jit(solution)/shard_map/pallas_call | solution.py:537
  226.2 15.0 %shard_map.247 = bf16[1024,2048]{1,0:T(8,128)(2,1)S(1)} custom-call(s32[8]{0:T(128)S(1)} %fusion.11.perm, bf16[2048,1024]{1,0:T(8,128)(2,1)} %copy-done.13, bf16[2048,2048]{1,0:T(8,128)(2,1)} %pad_maximum_fusion.1.gout_ref), custom_call_target="tpu_custom_call" | custom-call | flops 536870912 | bytes 1048576 | tf_op jit(solution)/shard_map/pallas_call | solution.py:453
  243.6 11.5 %convolution_convert_fusion.2 = bf16[1024,2048]{1,0:T(8,128)(2,1)S(1)} fusion(bf16[2048,1024]{1,0:T(8,128)(2,1)S(1)} %copy-done.23, bf16[2048,2048]{1,0:T(8,128)(2,1)} %copy-done.20), kind=kOutput, calls=%fused_computation.9 | convolution fusion | flops 8592031744 | bytes 16777216 | tf_op jit(solution)/shard_map/dot_general | solution.py:1041
  258.4 10.7 %convolution_convert_fusion = bf16[2048,2048]{1,0:T(8,128)(2,1)S(1)} fusion(bf16[2048,1024]{1,0:T(8,128)(2,1)S(1)} %copy-done.14, bf16[1024,2048]{1,0:T(8,128)(2,1)} %get-tuple-element.192), kind=kOutput, calls=%fused_computation.3 | convolution fusion | flops 8594128896 | bytes 16777216 | tf_op jit(solution)/shard_map/dot_general | solution.py:33
  277.4 32.1 %shard_map.248 = (bf16[2048,1296]{1,0:T(8,128)(2,1)}, f32[8,1280]{1,0:T(8,128)S(1)}, f32[8,128]{1,0:T(8,128)S(1)}) custom-call(s32[2,2]{1,0:T(2,128)S(1)} %pad_add_fusion.1.bnd, bf16[2048,1296]{1,0:T(8,128)(2,1)} %convolution_convert_fusion.1.xs_ref.bc_ref.dt_ref.refs_0_.refs_1_.refs_2_, ...), custom_call_target="tpu_custom_call" | custom-call | flops 2000000000 | bytes 750000 | tf_op jit(solution)/shard_map/pallas_call | solution.py:372
  316.7 16.7 %shard_map.249 = (bf16[1024,2048]{1,0:T(8,128)(2,1)S(1)}, f32[8,2048]{1,0:T(8,128)S(1)}) custom-call(bf16[2048,1296]{1,0:T(8,128)(2,1)} %get-tuple-element.216.a_ref.refs_8_, bf16[1296,2048]{1,0:T(8,128)(2,1)} %maximum_dynamic-update-slice_fusion.wa_ref, bf16[2048,1024]{1,0:T(8,128)(2,1)} %get-tuple-element.187.b_ref, ...), custom_call_target="tpu_custom_call" | custom-call | flops 608174080 | bytes 593920 | tf_op jit(solution)/shard_map/pallas_call | solution.py:569
  333.4 7.0 %collective-permute-done.33 = bf16[2048,256]{1,0:T(8,128)(2,1)S(1)} collective-permute-done((bf16[2048,256]{1,0:T(8,128)(2,1)}, bf16[2048,256]{1,0:T(8,128)(2,1)S(1)}, u32[]{:S(2)}, u32[]{:S(2)}) %collective-permute-start.33) | collective-permute-done | bytes 1048608 | tf_op jit(solution)/shard_map/ppermute | solution.py:859
  348.2 18.1 %shard_map.250 = (bf16[2048,1296]{1,0:T(8,128)(2,1)}, f32[8,1280]{1,0:T(8,128)S(1)}, f32[8,128]{1,0:T(8,128)S(1)}) custom-call(s32[1,2]{1,0:T(1,128)S(1)} %add_bitcast_fusion.bnd, bf16[2048,1296]{1,0:T(8,128)(2,1)} %convolution_convert_fusion.1.xs_ref.bc_ref.dt_ref.refs_0_.refs_1_.refs_2_, ...), custom_call_target="tpu_custom_call", output_to_operand_aliasing={{0}: (9, {})} | custom-call | flops 1000000000 | bytes 375000 | tf_op jit(solution)/shard_map/pallas_call | solution.py:372
  367.2 17.8 %shard_map.251 = (bf16[2048,1296]{1,0:T(8,128)(2,1)}, f32[8,1280]{1,0:T(8,128)S(1)}, f32[8,128]{1,0:T(8,128)S(1)}) custom-call(s32[1,2]{1,0:T(1,128)S(1)} %collective-permute-done.15.bnd, bf16[2048,1296]{1,0:T(8,128)(2,1)} %convolution_convert_fusion.1.xs_ref.bc_ref.dt_ref.refs_0_.refs_1_.refs_2_, ...), custom_call_target="tpu_custom_call", output_to_operand_aliasing={{0}: (9, {})} | custom-call | flops 1000000000 | bytes 375000 | tf_op jit(solution)/shard_map/pallas_call | solution.py:372
  401.4 13.8 %shard_map.253 = bf16[7,1296,256]{2,1,0:T(8,128)(2,1)S(1)} custom-call(bf16[1296,2048]{1,0:T(8,128)(2,1)} %copy-done.10, bf16[2048,2048]{1,0:T(8,128)(2,1)} %copy-done.20), custom_call_target="tpu_custom_call" | custom-call | flops 594542592 | bytes 1080832 | tf_op jit(solution)/shard_map/pallas_call | solution.py:605
  424.6 16.7 %shard_map.254 = (bf16[1024,2048]{1,0:T(8,128)(2,1)S(1)}, f32[8,2048]{1,0:T(8,128)S(1)}) custom-call(bf16[2048,1296]{1,0:T(8,128)(2,1)} %get-tuple-element.242.a_ref, bf16[1296,2048]{1,0:T(8,128)(2,1)} %maximum_dynamic-update-slice_fusion.wa_ref, bf16[2048,1024]{1,0:T(8,128)(2,1)} %get-tuple-element.187.b_ref, ...), custom_call_target="tpu_custom_call" | custom-call | flops 608174080 | bytes 593920 | tf_op jit(solution)/shard_map/pallas_call | solution.py:569
  454.5 6.1 %multiply_convert_fusion = bf16[512,2048]{1,0:T(8,128)(2,1)} fusion(bf16[512,2048]{1,0:T(8,128)(2,1)} %collective-permute-done.42, bf16[512,2048]{1,0:T(8,128)(2,1)} %copy-done.31, bf16[512,2048]{1,0:T(8,128)(2,1)S(1)} %copy-done.6, bf16[2048,2048]{1,0:T(8,128)(2,1)} %copy-done.24, f32[512]{0:T(512)S(1)} %copy-done.41), kind=kLoop, calls=%fused_computation.5 | loop fusion | flops 9437184 | bytes 10487808 | tf_op jit(solution)/shard_map/convert_element_type | solution.py:1090
  461.1 8.8 %collective-permute-done.46 = bf16[1296,256]{1,0:T(8,128)(2,1)S(1)} collective-permute-done((bf16[1296,256]{1,0:T(8,128)(2,1)}, bf16[1296,256]{1,0:T(8,128)(2,1)S(1)}, u32[]{:S(2)}, u32[]{:S(2)}) %collective-permute-start.46) | collective-permute-done | bytes 663584 | tf_op jit(solution)/shard_map/ppermute | solution.py:859
  483.4 7.1 %shard_map.255 = f32[512,2048]{1,0:T(8,128)} custom-call(s32[8]{0:T(128)S(1)} %fusion.11.perm, bf16[512,2048]{1,0:T(8,128)(2,1)S(1)} %copy-done.6, bf16[512,2048]{1,0:T(8,128)(2,1)S(1)} %copy-done.9, f32[512,1]{1,0:T(8,128)S(1)} %copy.35.keep_ref, f32[1,2048]{1,0:T(1,128)S(1)} %bitcast.77, bf16[512,2048]{1,0:T(8,128)(2,1)} %get-tuple-element.297.one_ref, ...), custom_call_target="tpu_custom_call" | custom-call | bytes 14680064 | tf_op jit(solution)/shard_map/pallas_call | solution.py:744
  (340 shorter events, 196.1 us)
Async XLA Ops:
  10.2 53.5 %collective-permute-start.9 = (bf16[512,2048]{1,0:T(8,128)(2,1)S(1)}, bf16[512,2048]{1,0:T(8,128)(2,1)}, u32[]{:S(2)}, u32[]{:S(2)}) collective-permute-start(bf16[512,2048]{1,0:T(8,128)(2,1)S(1)} %shard_map.239), channel_id=1, source_target_pairs={{0,16},{8,24},{16,0},{24,8},{1,17},{9,25},{17,1},{25,9},{2,18},{10... | collective-permute-start | bytes 6291464 | tf_op jit(solution)/shard_map/ppermute | solution.py:855
  72.8 34.5 %collective-permute-start.15 = (s32[1,2]{1,0:T(1,128)S(1)}, s32[1,2]{1,0:T(1,128)S(1)}, u32[]{:S(2)}, u32[]{:S(2)}) collective-permute-start(s32[1,2]{1,0:T(1,128)S(1)} %add_bitcast_fusion.bnd), channel_id=1, source_target_pairs={{0,8},{8,0},{16,24},{24,16},{1,9},{9,1},{17,25},{25,17},{2,10},{10... | collective-permute-start | bytes 32 | tf_op jit(solution)/shard_map/ppermute | solution.py:855
  74.9 51.5 %collective-permute-start.16 = (bf16[512,2048]{1,0:T(8,128)(2,1)}, bf16[512,2048]{1,0:T(8,128)(2,1)}, u32[]{:S(2)}, u32[]{:S(2)}) collective-permute-start(bf16[512,2048]{1,0:T(8,128)(2,1)} %multiply_convert_fusion.1), channel_id=1, source_target_pairs={{0,16},{8,24},{16,0},{24,8},{1,17},{9,25},{17,1},{25,9},{2,18},{10... | collective-permute-start | bytes 6291464 | tf_op jit(solution)/shard_map/ppermute | solution.py:855
  76.4 50.0 %collective-permute-start.17 = (bf16[512,2048]{1,0:T(8,128)(2,1)}, bf16[512,2048]{1,0:T(8,128)(2,1)}, u32[]{:S(2)}, u32[]{:S(2)}) collective-permute-start(bf16[512,2048]{1,0:T(8,128)(2,1)} %multiply_convert_fusion.1), channel_id=1, source_target_pairs={{0,8},{8,0},{16,24},{24,16},{1,9},{9,1},{17,25},{25,17},{2,10},{10... | collective-permute-start | bytes 6291464 | tf_op jit(solution)/shard_map/ppermute | solution.py:855
  76.4 25.7 %collective-permute-start.11 = (bf16[2048,256]{1,0:T(8,128)(2,1)S(1)}, bf16[2048,256]{1,0:T(8,128)(2,1)}, u32[]{:S(2)}, u32[]{:S(2)}) collective-permute-start(bf16[2048,256]{1,0:T(8,128)(2,1)S(1)} %shard_map.241.refs_0_), channel_id=1, source_target_pairs={{0,2},{2,4},{4,6},{6,7},{7,5},{5,3},{3,1},{1,0},{8,10},{10,12},{12... | collective-permute-start | bytes 3145736 | tf_op jit(solution)/shard_map/ppermute | solution.py:859
  79.1 25.4 %collective-permute-start.12 = (bf16[2048,256]{1,0:T(8,128)(2,1)S(1)}, bf16[2048,256]{1,0:T(8,128)(2,1)}, u32[]{:S(2)}, u32[]{:S(2)}) collective-permute-start(bf16[2048,256]{1,0:T(8,128)(2,1)S(1)} %shard_map.241.refs_0_), channel_id=1, source_target_pairs={{2,0},{4,2},{6,4},{7,6},{5,7},{3,5},{1,3},{0,1},{10,8},{12,10},{14... | collective-permute-start | bytes 3145736 | tf_op jit(solution)/shard_map/ppermute | solution.py:863
  104.5 24.7 %collective-permute-start.13 = (bf16[2048,256]{1,0:T(8,128)(2,1)}, bf16[2048,256]{1,0:T(8,128)(2,1)S(1)}, u32[]{:S(2)}, u32[]{:S(2)}) collective-permute-start(bf16[2048,256]{1,0:T(8,128)(2,1)} %collective-permute-done.11.refs_1_), channel_id=1, source_target_pairs={{0,2},{2,4},{4,6},{6,7},{7,5},{5,3},{3,1},{1,0},{8,10},{10,12},{12... | collective-permute-start | bytes 3145736 | tf_op jit(solution)/shard_map/ppermute | solution.py:859
  105.1 24.6 %collective-permute-start.14 = (bf16[2048,256]{1,0:T(8,128)(2,1)}, bf16[2048,256]{1,0:T(8,128)(2,1)S(1)}, u32[]{:S(2)}, u32[]{:S(2)}) collective-permute-start(bf16[2048,256]{1,0:T(8,128)(2,1)} %collective-permute-done.12.refs_2_), channel_id=1, source_target_pairs={{2,0},{4,2},{6,4},{7,6},{5,7},{3,5},{1,3},{0,1},{10,8},{12,10},{14... | collective-permute-start | bytes 3145736 | tf_op jit(solution)/shard_map/ppermute | solution.py:863
  129.7 26.0 %collective-permute-start.22 = (bf16[512,2048]{1,0:T(8,128)(2,1)}, bf16[512,2048]{1,0:T(8,128)(2,1)S(1)}, u32[]{:S(2)}, u32[]{:S(2)}) collective-permute-start(bf16[512,2048]{1,0:T(8,128)(2,1)} %collective-permute-done.16), channel_id=1, source_target_pairs={{0,8},{8,0},{16,24},{24,16},{1,9},{9,1},{17,25},{25,17},{2,10},{10... | collective-permute-start | bytes 6291464 | tf_op jit(solution)/shard_map/ppermute | solution.py:855
  129.7 25.6 %collective-permute-start.18 = (bf16[2048,256]{1,0:T(8,128)(2,1)S(1)}, bf16[2048,256]{1,0:T(8,128)(2,1)S(1)}, u32[]{:S(2)}, u32[]{:S(2)}) collective-permute-start(bf16[2048,256]{1,0:T(8,128)(2,1)S(1)} %collective-permute-done.13.refs_3_), channel_id=1, source_target_pairs={{0,2},{2,4},{4,6},{6,7},{7,5},{5,3},{3,1},{1,0},{8,10},{10,12},{12... | collective-permute-start | bytes 3145736 | tf_op jit(solution)/shard_map/ppermute | solution.py:859
  130.1 25.5 %collective-permute-start.19 = (bf16[2048,256]{1,0:T(8,128)(2,1)S(1)}, bf16[2048,256]{1,0:T(8,128)(2,1)S(1)}, u32[]{:S(2)}, u32[]{:S(2)}) collective-permute-start(bf16[2048,256]{1,0:T(8,128)(2,1)S(1)} %collective-permute-done.14.refs_4_), channel_id=1, source_target_pairs={{2,0},{4,2},{6,4},{7,6},{5,7},{3,5},{1,3},{0,1},{10,8},{12,10},{14... | collective-permute-start | bytes 3145736 | tf_op jit(solution)/shard_map/ppermute | solution.py:863
  275.3 34.2 %collective-permute-start.32 = (bf16[512,2048]{1,0:T(8,128)(2,1)}, bf16[512,2048]{1,0:T(8,128)(2,1)S(1)}, u32[]{:S(2)}, u32[]{:S(2)}) collective-permute-start(bf16[512,2048]{1,0:T(8,128)(2,1)} %get-tuple-element.201), channel_id=1, source_target_pairs={{0,8},{8,0},{16,24},{24,16},{1,9},{9,1},{17,25},{25,17},{2,10},{10... | collective-permute-start | bytes 6291464 | tf_op jit(solution)/shard_map/ppermute | solution.py:855
  275.3 34.2 %collective-permute-start.30 = (bf16[2048,256]{1,0:T(8,128)(2,1)}, bf16[2048,256]{1,0:T(8,128)(2,1)S(1)}, u32[]{:S(2)}, u32[]{:S(2)}) collective-permute-start(bf16[2048,256]{1,0:T(8,128)(2,1)} %pad_maximum_fusion.4), channel_id=1, source_target_pairs={{0,2},{2,4},{4,6},{6,7},{7,5},{5,3},{3,1},{1,0},{8,10},{10,12},{12... | collective-permute-start | bytes 3145736 | tf_op jit(solution)/shard_map/ppermute | solution.py:859
  276.9 32.6 %collective-permute-start.31 = (bf16[2048,256]{1,0:T(8,128)(2,1)S(1)}, bf16[2048,256]{1,0:T(8,128)(2,1)S(1)}, u32[]{:S(2)}, u32[]{:S(2)}) collective-permute-start(bf16[2048,256]{1,0:T(8,128)(2,1)S(1)} %pad_maximum_fusion.5), channel_id=1, source_target_pairs={{2,0},{4,2},{6,4},{7,6},{5,7},{3,5},{1,3},{0,1},{10,8},{12,10},{14... | collective-permute-start | bytes 3145736 | tf_op jit(solution)/shard_map/ppermute | solution.py:863
  277.4 56.0 %collective-permute-start.35 = (bf16[512,2048]{1,0:T(8,128)(2,1)}, bf16[512,2048]{1,0:T(8,128)(2,1)S(1)}, u32[]{:S(2)}, u32[]{:S(2)}) collective-permute-start(bf16[512,2048]{1,0:T(8,128)(2,1)} %get-tuple-element.291), channel_id=1, source_target_pairs={{0,8},{8,0},{16,24},{24,16},{1,9},{9,1},{17,25},{25,17},{2,10},{10... | collective-permute-start | bytes 6291464 | tf_op jit(solution)/shard_map/ppermute | solution.py:855
  314.6 25.8 %collective-permute-start.33 = (bf16[2048,256]{1,0:T(8,128)(2,1)}, bf16[2048,256]{1,0:T(8,128)(2,1)S(1)}, u32[]{:S(2)}, u32[]{:S(2)}) collective-permute-start(bf16[2048,256]{1,0:T(8,128)(2,1)} %add_convert_fusion.6), channel_id=1, source_target_pairs={{0,2},{2,4},{4,6},{6,7},{7,5},{5,3},{3,1},{1,0},{8,10},{10,12},{12... | collective-permute-start | bytes 3145736 | tf_op jit(solution)/shard_map/ppermute | solution.py:859
  316.2 25.3 %collective-permute-start.34 = (bf16[2048,256]{1,0:T(8,128)(2,1)S(1)}, bf16[2048,256]{1,0:T(8,128)(2,1)S(1)}, u32[]{:S(2)}, u32[]{:S(2)}) collective-permute-start(bf16[2048,256]{1,0:T(8,128)(2,1)S(1)} %add_convert_fusion.5), channel_id=1, source_target_pairs={{2,0},{4,2},{6,4},{7,6},{5,7},{3,5},{1,3},{0,1},{10,8},{12,10},{14... | collective-permute-start | bytes 3145736 | tf_op jit(solution)/shard_map/ppermute | solution.py:863
  345.6 39.4 %collective-permute-start.36 = (bf16[2048,256]{1,0:T(8,128)(2,1)}, bf16[2048,256]{1,0:T(8,128)(2,1)}, u32[]{:S(2)}, u32[]{:S(2)}) collective-permute-start(bf16[2048,256]{1,0:T(8,128)(2,1)} %add_convert_fusion.4), channel_id=1, source_target_pairs={{0,2},{2,4},{4,6},{6,7},{7,5},{5,3},{3,1},{1,0},{8,10},{10,12},{12... | collective-permute-start | bytes 3145736 | tf_op jit(solution)/shard_map/ppermute | solution.py:859
  347.2 37.8 %collective-permute-start.37 = (bf16[2048,256]{1,0:T(8,128)(2,1)S(1)}, bf16[2048,256]{1,0:T(8,128)(2,1)}, u32[]{:S(2)}, u32[]{:S(2)}) collective-permute-start(bf16[2048,256]{1,0:T(8,128)(2,1)S(1)} %add_convert_fusion.3), channel_id=1, source_target_pairs={{2,0},{4,2},{6,4},{7,6},{5,7},{3,5},{1,3},{0,1},{10,8},{12,10},{14... | collective-permute-start | bytes 3145736 | tf_op jit(solution)/shard_map/ppermute | solution.py:863
  347.6 67.5 %collective-permute-start.42 = (bf16[512,2048]{1,0:T(8,128)(2,1)}, bf16[512,2048]{1,0:T(8,128)(2,1)}, u32[]{:S(2)}, u32[]{:S(2)}) collective-permute-start(bf16[512,2048]{1,0:T(8,128)(2,1)} %add_convert_fusion.1), channel_id=1, source_target_pairs={{0,16},{8,24},{16,0},{24,8},{1,17},{9,25},{17,1},{25,9},{2,18},{10... | collective-permute-start | bytes 6291464 | tf_op jit(solution)/shard_map/ppermute | solution.py:855
  386.5 31.3 %collective-permute-start.41 = (bf16[256,2048]{1,0:T(8,128)(2,1)}, bf16[256,2048]{1,0:T(8,128)(2,1)S(1)}, u32[]{:S(2)}, u32[]{:S(2)}) collective-permute-start(bf16[256,2048]{1,0:T(8,128)(2,1)} %get-tuple-element.314), channel_id=1, source_target_pairs={{0,16},{8,24},{16,0},{24,8},{1,17},{9,25},{17,1},{25,9},{2,18},{10... | collective-permute-start | bytes 3145736 | tf_op jit(solution)/shard_map/ppermute | solution.py:855
  401.4 104.6 %collective-permute-start.55 = (bf16[2048,256]{1,0:T(8,128)(2,1)S(1)}, bf16[2048,256]{1,0:T(8,128)(2,1)}, u32[]{:S(2)}, u32[]{:S(2)}) collective-permute-start(bf16[2048,256]{1,0:T(8,128)(2,1)S(1)} %add_convert_fusion.2.refs_0_), channel_id=1, source_target_pairs={{0,8},{8,0},{16,24},{24,16},{1,9},{9,1},{17,25},{25,17},{2,10},{10... | collective-permute-start | bytes 3145736 | tf_op jit(solution)/shard_map/ppermute | solution.py:855
  420.1 24.4 %collective-permute-start.45 = (bf16[256,2048]{1,0:T(8,128)(2,1)}, bf16[256,2048]{1,0:T(8,128)(2,1)}, u32[]{:S(2)}, u32[]{:S(2)}) collective-permute-start(bf16[256,2048]{1,0:T(8,128)(2,1)} %get-tuple-element.244), channel_id=1, source_target_pairs={{0,16},{8,24},{16,0},{24,8},{1,17},{9,25},{17,1},{25,9},{2,18},{10... | collective-permute-start | bytes 3145736 | tf_op jit(solution)/shard_map/ppermute | solution.py:855
  460.6 29.9 %collective-permute-start.51 = (bf16[2048,256]{1,0:T(8,128)(2,1)S(1)}, bf16[2048,256]{1,0:T(8,128)(2,1)}, u32[]{:S(2)}, u32[]{:S(2)}) collective-permute-start(bf16[2048,256]{1,0:T(8,128)(2,1)S(1)} %add_convert_fusion.2.refs_0_), channel_id=1, source_target_pairs={{0,16},{8,24},{16,0},{24,8},{1,17},{9,25},{17,1},{25,9},{2,18},{10... | collective-permute-start | bytes 3145736 | tf_op jit(solution)/shard_map/ppermute | solution.py:855
  (86 other events, 1221.7 us)

commit v5 on v4

--- a/solution.py
+++ b/solution.py
@@ -1092,6 +1092,7 @@
         sent, core, dgo = launch(steps, sent, core, dgo)
         small = small_vector(dcw, dhp, dgo, dgain)
         small = small + swap(small, 1)
+        small = small + swap(small, 2)
         parts = [early[:TOK], core, jnp.concatenate([upper, lower], 0)]
         grad_tokens = last_rows(perm, tokens, cotangent, keep, gain_outer[None, :], parts)
         *sent, gates[2], grad_tokens, small = tie(*sent, gates[2], grad_tokens, small)
@@ -1102,7 +1103,6 @@
             small = flip(small, d)
         grad_in, grad_out_weight = first_join(me, gates, width)
         rests[2], grad_in = tie(rests[2], grad_in)
-        small = small + swap(small, 2)
         rests.append(swap(rests[2], 1))
     else:
         side = lambda x: jnp.concatenate(list(x), 1)

time: 531 us -> 535 us (level)
  waiting for transfers between devices: 110 us -> 120 us
  local copies, waits for them, and re-layouts: 38.5 us -> 30.9 us
    unnamed x106 -> x100, local copies, waits for them, and re-layouts: 14.5 us -> 13.5 us
  transfers between devices with their start and end apart: 62 -> 62, of which waited for: 31 -> 31; matrix products, arithmetic and copies ran while one was open for 17% -> 14% of each run, Pallas kernels for 32% -> 32%
where the time goes in v5:
time: 535 us; the launch traced here: 528 us
  Pallas kernels  234 us (44%)
  waiting for transfers between devices  120 us (22%)
  other arithmetic  52.2 us (10%)
  starting transfers between devices  50.6 us (9%)
  matrix products  37.2 us (7%)
  local copies, waits for them, and re-layouts  30.9 us (6%)
    ppermute x16, waiting for transfers between devices, fw(): lax.ppermute(x, 'shard', [(RING[i], RING[(i + 1) % 8]) for i in range(8)])  70.2 us
    pallas_call x3, Pallas kernels, scan_backward(): pl.pallas_call(bwd_kernel if into is None else bwd_into, out_shape=(jax.S...  68 us
    pallas_call x2, Pallas kernels, normed_gradient(): pl.pallas_call(back_kernel, out_shape=(jax.ShapeDtypeStruct((count * TOK,...  33.4 us
    pallas_call x2, Pallas kernels, scan_forward(): pl.pallas_call(fwd_kernel if into is None else fwd_into, out_shape=jax.Sh...  32.7 us
    ppermute x16, starting transfers between devices, fw(): lax.ppermute(x, 'shard', [(RING[i], RING[(i + 1) % 8]) for i in range(8)])  22.1 us
    ppermute x16, waiting for transfers between devices, bw(): lax.ppermute(x, 'shard', [(RING[(i + 1) % 8], RING[i]) for i in range(8)])  19.2 us
    pallas_call x2, Pallas kernels, across_rows(): pl.pallas_call(across_kernel, out_shape=(part, jax.ShapeDtypeStruct((m, r...  18.4 us
    ppermute x27, waiting for transfers between devices, swap(): return lax.ppermute(x, 'rep', [(i, i ^ d) for i in range(4)])  18.2 us
  transfers between devices with their start and end apart: 62, of which 31 were waited for; matrix products, arithmetic and copies ran while one was open for 14% of the time, Pallas kernels for 32%

profile of v5, /device:TPU:0, one launch (start us, length us, event | category | flops | bytes accessed | tf_op | source)
XLA Modules:
  0.0 528.3 jit_solution(8524900122822087969)
XLA Ops:
  13.5 12.1 %collective-permute-done = bf16[1296,256]{1,0:T(8,128)(2,1)S(1)} collective-permute-done((bf16[1296,256]{1,0:T(8,128)(2,1)S(1)}, bf16[1296,256]{1,0:T(8,128)(2,1)S(1)}, u32[]{:S(2)}, u32[]{:S(2)}) %collective-permute-start) | collective-permute-done | bytes 663584 | tf_op jit(solution)/shard_map/ppermute | solution.py:859
  31.1 12.3 %collective-permute-done.3 = bf16[1296,256]{1,0:T(8,128)(2,1)S(1)} collective-permute-done((bf16[1296,256]{1,0:T(8,128)(2,1)S(1)}, bf16[1296,256]{1,0:T(8,128)(2,1)S(1)}, u32[]{:S(2)}, u32[]{:S(2)}) %collective-permute-start.3) | collective-permute-done | bytes 663584 | tf_op jit(solution)/shard_map/ppermute | solution.py:859
  47.0 12.9 %collective-permute-done.5 = bf16[1296,256]{1,0:T(8,128)(2,1)S(1)} collective-permute-done((bf16[1296,256]{1,0:T(8,128)(2,1)S(1)}, bf16[1296,256]{1,0:T(8,128)(2,1)S(1)}, u32[]{:S(2)}, u32[]{:S(2)}) %collective-permute-start.5) | collective-permute-done | bytes 663584 | tf_op jit(solution)/shard_map/ppermute | solution.py:859
  63.7 6.3 %collective-permute-done.8 = bf16[640,256]{1,0:T(8,128)(2,1)S(1)} collective-permute-done((bf16[640,256]{1,0:T(8,128)(2,1)S(1)}, bf16[640,256]{1,0:T(8,128)(2,1)S(1)}, u32[]{:S(2)}, u32[]{:S(2)}) %collective-permute-start.8) | collective-permute-done | bytes 327712 | tf_op jit(solution)/shard_map/ppermute | solution.py:863
  84.7 15.0 %convolution_convert_fusion.1.xs_ref.bc_ref.dt_ref.refs_0_.refs_1_.refs_2_ = bf16[2048,1296]{1,0:T(8,128)(2,1)} fusion(bf16[2048,2048]{1,0:T(8,128)(2,1)S(1)} %pad_maximum_fusion.norm_ref.b_ref, bf16[1296,2048]{1,0:T(8,128)(2,1)S(1)} %copy-done.19), kind=kOutput, calls=%fused_computation.4 | convolution fusion | flops 10874290176 | bytes 19005440 | tf_op jit(solution)/shard_map/dot_general | solution.py:37
  110.0 16.3 %shard_map.242.refs_6_ = f32[2048,1024]{1,0:T(8,128)} custom-call(s32[2,2]{1,0:T(2,128)S(1)} %pad_add_fusion.bnd, bf16[2048,1296]{1,0:T(8,128)(2,1)S(1)} %copy-done.2, bf16[2048,1296]{1,0:T(8,128)(2,1)S(1)} %copy-done.2, bf16[2048,1296]{1,0:T(8,128)(2,1)S(1)} %copy-done.2, f32[8,1280]{1,0:T(8,128)S(1)} %pad_maximum_fusion.10.cwx_ref.cwb_ref.refs_3_.refs_4_, ...), custom_call_target="tpu_custom_call" | custom-call | flops 1000000000 | bytes 500000 | tf_op jit(solution)/shard_map/pallas_call | solution.py:350
  135.5 16.3 %shard_map.243.scan_ref.refs_6_ = f32[2048,1024]{1,0:T(8,128)} custom-call(s32[2,2]{1,0:T(2,128)S(1)} %pad_add_fusion.1.bnd, bf16[2048,1296]{1,0:T(8,128)(2,1)S(1)} %copy-done.3, bf16[2048,1296]{1,0:T(8,128)(2,1)S(1)} %copy-done.3, bf16[2048,1296]{1,0:T(8,128)(2,1)S(1)} %copy-done.3, ...), custom_call_target="tpu_custom_call", output_to_operand_aliasing={{}: (7, {})} | custom-call | flops 1000000000 | bytes 500000 | tf_op jit(solution)/shard_map/pallas_call | solution.py:350
  170.8 15.8 %shard_map.244 = (bf16[2048,1024]{1,0:T(8,128)(2,1)}, bf16[1024,2048]{1,0:T(8,128)(2,1)}, bf16[1024,2048]{1,0:T(8,128)(2,1)}) custom-call(s32[8]{0:T(128)S(1)} %fusion.11.perm, bf16[2048,2048]{1,0:T(8,128)(2,1)} %pad_maximum_fusion.1.gout_ref, bf16[2048,256]{1,0:T(8,128)(2,1)S(1)} %shard_map.241.refs_0_, bf16[2048,256]{1,0:T(8,128)(2,1)} %collective-permute-done.11.refs_1_, ...), custom_call_target="tpu_custom_call" | custom-call | flops 536870912 | bytes 1835008 | tf_op jit(solution)/shard_map/pallas_call | solution.py:426
  186.6 16.5 %shard_map.245 = (bf16[2048,1024]{1,0:T(8,128)(2,1)S(1)}, f32[4,8,512]{2,1,0:T(8,128)S(1)}) custom-call(bf16[2048,2048]{1,0:T(8,128)(2,1)} %copy-done.17, bf16[1024,2048]{1,0:T(8,128)(2,1)} %get-tuple-element.180.w_ref.wb_ref, f32[2048,1024]{1,0:T(8,128)} %shard_map.243.scan_ref.refs_6_, bf16[2048,1024]{1,0:T(8,128)(2,1)} %get-tuple-element.182.gin_ref, ...), custom_call_target="tpu_custom_call" | custom-call | flops 536870912 | bytes 1835008 | tf_op jit(solution)/shard_map/pallas_call | solution.py:488
  210.7 13.4 %shard_map.246 = (bf16[2048,1024]{1,0:T(8,128)(2,1)S(1)}, bf16[2048,1024]{1,0:T(8,128)(2,1)}, bf16[2048,1024]{1,0:T(8,128)(2,1)}, f32[8,1024]{1,0:T(8,128)S(1)}) custom-call(f32[4,8,512]{2,1,0:T(8,128)S(1)} %pad_maximum_fusion.9.sum_ref, f32[2048,1024]{1,0:T(8,128)} %shard_map.243.scan_ref.refs_6_, bf16[2048,1024]{1,0:T(8,128)(2,1)} %copy-done.12, ...), custom_call_target="tpu_custom_call" | custom-call | bytes 1835008 | tf_op jit(solution)/shard_map/pallas_call | solution.py:537
  226.2 15.0 %shard_map.247 = bf16[1024,2048]{1,0:T(8,128)(2,1)S(1)} custom-call(s32[8]{0:T(128)S(1)} %fusion.11.perm, bf16[2048,1024]{1,0:T(8,128)(2,1)} %copy-done.13, bf16[2048,2048]{1,0:T(8,128)(2,1)} %pad_maximum_fusion.1.gout_ref), custom_call_target="tpu_custom_call" | custom-call | flops 536870912 | bytes 1048576 | tf_op jit(solution)/shard_map/pallas_call | solution.py:453
  243.5 11.5 %convolution_convert_fusion.2 = bf16[1024,2048]{1,0:T(8,128)(2,1)S(1)} fusion(bf16[2048,1024]{1,0:T(8,128)(2,1)S(1)} %copy-done.20, bf16[2048,2048]{1,0:T(8,128)(2,1)} %copy-done.17), kind=kOutput, calls=%fused_computation.9 | convolution fusion | flops 8592031744 | bytes 16777216 | tf_op jit(solution)/shard_map/dot_general | solution.py:1041
  258.4 10.7 %convolution_convert_fusion = bf16[2048,2048]{1,0:T(8,128)(2,1)S(1)} fusion(bf16[2048,1024]{1,0:T(8,128)(2,1)S(1)} %copy-done.14, bf16[1024,2048]{1,0:T(8,128)(2,1)} %get-tuple-element.192), kind=kOutput, calls=%fused_computation.3 | convolution fusion | flops 8594128896 | bytes 16777216 | tf_op jit(solution)/shard_map/dot_general | solution.py:33
  277.3 32.1 %shard_map.248 = (bf16[2048,1296]{1,0:T(8,128)(2,1)}, f32[8,1280]{1,0:T(8,128)S(1)}, f32[8,128]{1,0:T(8,128)S(1)}) custom-call(s32[2,2]{1,0:T(2,128)S(1)} %pad_add_fusion.1.bnd, bf16[2048,1296]{1,0:T(8,128)(2,1)} %convolution_convert_fusion.1.xs_ref.bc_ref.dt_ref.refs_0_.refs_1_.refs_2_, ...), custom_call_target="tpu_custom_call" | custom-call | flops 2000000000 | bytes 750000 | tf_op jit(solution)/shard_map/pallas_call | solution.py:372
  316.3 16.7 %shard_map.249 = (bf16[1024,2048]{1,0:T(8,128)(2,1)S(1)}, f32[8,2048]{1,0:T(8,128)S(1)}) custom-call(bf16[2048,1296]{1,0:T(8,128)(2,1)} %get-tuple-element.216.a_ref.refs_8_, bf16[1296,2048]{1,0:T(8,128)(2,1)} %maximum_dynamic-update-slice_fusion.wa_ref, bf16[2048,1024]{1,0:T(8,128)(2,1)} %get-tuple-element.187.b_ref, ...), custom_call_target="tpu_custom_call" | custom-call | flops 608174080 | bytes 593920 | tf_op jit(solution)/shard_map/pallas_call | solution.py:569
  333.0 7.1 %collective-permute-done.33 = bf16[2048,256]{1,0:T(8,128)(2,1)} collective-permute-done((bf16[2048,256]{1,0:T(8,128)(2,1)}, bf16[2048,256]{1,0:T(8,128)(2,1)}, u32[]{:S(2)}, u32[]{:S(2)}) %collective-permute-start.33) | collective-permute-done | bytes 1048608 | tf_op jit(solution)/shard_map/ppermute | solution.py:859
  349.3 18.1 %shard_map.250 = (bf16[2048,1296]{1,0:T(8,128)(2,1)}, f32[8,1280]{1,0:T(8,128)S(1)}, f32[8,128]{1,0:T(8,128)S(1)}) custom-call(s32[1,2]{1,0:T(1,128)S(1)} %add_bitcast_fusion.bnd, bf16[2048,1296]{1,0:T(8,128)(2,1)} %convolution_convert_fusion.1.xs_ref.bc_ref.dt_ref.refs_0_.refs_1_.refs_2_, ...), custom_call_target="tpu_custom_call", output_to_operand_aliasing={{0}: (9, {})} | custom-call | flops 1000000000 | bytes 375000 | tf_op jit(solution)/shard_map/pallas_call | solution.py:372
  368.2 17.8 %shard_map.251 = (bf16[2048,1296]{1,0:T(8,128)(2,1)}, f32[8,1280]{1,0:T(8,128)S(1)}, f32[8,128]{1,0:T(8,128)S(1)}) custom-call(s32[1,2]{1,0:T(1,128)S(1)} %collective-permute-done.15.bnd, bf16[2048,1296]{1,0:T(8,128)(2,1)} %convolution_convert_fusion.1.xs_ref.bc_ref.dt_ref.refs_0_.refs_1_.refs_2_, ...), custom_call_target="tpu_custom_call", output_to_operand_aliasing={{0}: (9, {})} | custom-call | flops 1000000000 | bytes 375000 | tf_op jit(solution)/shard_map/pallas_call | solution.py:372
  400.2 13.8 %shard_map.253 = bf16[7,1296,256]{2,1,0:T(8,128)(2,1)S(1)} custom-call(bf16[1296,2048]{1,0:T(8,128)(2,1)} %copy-done.10, bf16[2048,2048]{1,0:T(8,128)(2,1)} %copy-done.17), custom_call_target="tpu_custom_call" | custom-call | flops 594542592 | bytes 1080832 | tf_op jit(solution)/shard_map/pallas_call | solution.py:605
  425.1 16.7 %shard_map.254 = (bf16[1024,2048]{1,0:T(8,128)(2,1)S(1)}, f32[8,2048]{1,0:T(8,128)S(1)}) custom-call(bf16[2048,1296]{1,0:T(8,128)(2,1)} %get-tuple-element.242.a_ref, bf16[1296,2048]{1,0:T(8,128)(2,1)} %maximum_dynamic-update-slice_fusion.wa_ref, bf16[2048,1024]{1,0:T(8,128)(2,1)} %get-tuple-element.187.b_ref, ...), custom_call_target="tpu_custom_call" | custom-call | flops 608174080 | bytes 593920 | tf_op jit(solution)/shard_map/pallas_call | solution.py:569
  453.1 6.1 %multiply_convert_fusion = bf16[512,2048]{1,0:T(8,128)(2,1)} fusion(bf16[512,2048]{1,0:T(8,128)(2,1)} %collective-permute-done.42, bf16[512,2048]{1,0:T(8,128)(2,1)} %copy-done.29, bf16[512,2048]{1,0:T(8,128)(2,1)S(1)} %copy-done.6, bf16[2048,2048]{1,0:T(8,128)(2,1)} %copy-done.21, f32[512]{0:T(512)S(1)} %copy-done.37), kind=kLoop, calls=%fused_computation.5 | loop fusion | flops 9437184 | bytes 10487808 | tf_op jit(solution)/shard_map/convert_element_type | solution.py:1090
  459.7 8.9 %collective-permute-done.46 = bf16[1296,256]{1,0:T(8,128)(2,1)S(1)} collective-permute-done((bf16[1296,256]{1,0:T(8,128)(2,1)}, bf16[1296,256]{1,0:T(8,128)(2,1)S(1)}, u32[]{:S(2)}, u32[]{:S(2)}) %collective-permute-start.46) | collective-permute-done | bytes 663584 | tf_op jit(solution)/shard_map/ppermute | solution.py:859
  481.4 7.1 %shard_map.255 = f32[512,2048]{1,0:T(8,128)} custom-call(s32[8]{0:T(128)S(1)} %fusion.11.perm, bf16[512,2048]{1,0:T(8,128)(2,1)S(1)} %copy-done.6, bf16[512,2048]{1,0:T(8,128)(2,1)S(1)} %copy-done.9, f32[512,1]{1,0:T(8,128)S(1)} %copy.35.keep_ref, f32[1,2048]{1,0:T(1,128)S(1)} %bitcast.79, bf16[512,2048]{1,0:T(8,128)(2,1)} %get-tuple-element.297.one_ref, ...), custom_call_target="tpu_custom_call" | custom-call | bytes 14680064 | tf_op jit(solution)/shard_map/pallas_call | solution.py:744
  513.4 7.5 %collective-permute-done.61 = f32[224,128]{1,0:T(8,128)S(1)} collective-permute-done((f32[224,128]{1,0:T(8,128)S(1)}, f32[224,128]{1,0:T(8,128)S(1)}, u32[]{:S(2)}, u32[]{:S(2)}) %collective-permute-start.61) | collective-permute-done | bytes 114720 | tf_op jit(solution)/shard_map/ppermute | solution.py:1089
  (334 shorter events, 199.0 us)
Async XLA Ops:
  10.2 53.5 %collective-permute-start.9 = (bf16[512,2048]{1,0:T(8,128)(2,1)S(1)}, bf16[512,2048]{1,0:T(8,128)(2,1)}, u32[]{:S(2)}, u32[]{:S(2)}) collective-permute-start(bf16[512,2048]{1,0:T(8,128)(2,1)S(1)} %shard_map.239), channel_id=1, source_target_pairs={{0,16},{8,24},{16,0},{24,8},{1,17},{9,25},{17,1},{25,9},{2,18},{10... | collective-permute-start | bytes 6291464 | tf_op jit(solution)/shard_map/ppermute | solution.py:855
  72.8 34.6 %collective-permute-start.15 = (s32[1,2]{1,0:T(1,128)S(1)}, s32[1,2]{1,0:T(1,128)S(1)}, u32[]{:S(2)}, u32[]{:S(2)}) collective-permute-start(s32[1,2]{1,0:T(1,128)S(1)} %add_bitcast_fusion.bnd), channel_id=1, source_target_pairs={{0,8},{8,0},{16,24},{24,16},{1,9},{9,1},{17,25},{25,17},{2,10},{10... | collective-permute-start | bytes 32 | tf_op jit(solution)/shard_map/ppermute | solution.py:855
  74.9 51.5 %collective-permute-start.16 = (bf16[512,2048]{1,0:T(8,128)(2,1)}, bf16[512,2048]{1,0:T(8,128)(2,1)}, u32[]{:S(2)}, u32[]{:S(2)}) collective-permute-start(bf16[512,2048]{1,0:T(8,128)(2,1)} %multiply_convert_fusion.1), channel_id=1, source_target_pairs={{0,16},{8,24},{16,0},{24,8},{1,17},{9,25},{17,1},{25,9},{2,18},{10... | collective-permute-start | bytes 6291464 | tf_op jit(solution)/shard_map/ppermute | solution.py:855
  76.4 50.0 %collective-permute-start.17 = (bf16[512,2048]{1,0:T(8,128)(2,1)}, bf16[512,2048]{1,0:T(8,128)(2,1)}, u32[]{:S(2)}, u32[]{:S(2)}) collective-permute-start(bf16[512,2048]{1,0:T(8,128)(2,1)} %multiply_convert_fusion.1), channel_id=1, source_target_pairs={{0,8},{8,0},{16,24},{24,16},{1,9},{9,1},{17,25},{25,17},{2,10},{10... | collective-permute-start | bytes 6291464 | tf_op jit(solution)/shard_map/ppermute | solution.py:855
  76.4 25.7 %collective-permute-start.11 = (bf16[2048,256]{1,0:T(8,128)(2,1)S(1)}, bf16[2048,256]{1,0:T(8,128)(2,1)}, u32[]{:S(2)}, u32[]{:S(2)}) collective-permute-start(bf16[2048,256]{1,0:T(8,128)(2,1)S(1)} %shard_map.241.refs_0_), channel_id=1, source_target_pairs={{0,2},{2,4},{4,6},{6,7},{7,5},{5,3},{3,1},{1,0},{8,10},{10,12},{12... | collective-permute-start | bytes 3145736 | tf_op jit(solution)/shard_map/ppermute | solution.py:859
  79.1 25.4 %collective-permute-start.12 = (bf16[2048,256]{1,0:T(8,128)(2,1)S(1)}, bf16[2048,256]{1,0:T(8,128)(2,1)}, u32[]{:S(2)}, u32[]{:S(2)}) collective-permute-start(bf16[2048,256]{1,0:T(8,128)(2,1)S(1)} %shard_map.241.refs_0_), channel_id=1, source_target_pairs={{2,0},{4,2},{6,4},{7,6},{5,7},{3,5},{1,3},{0,1},{10,8},{12,10},{14... | collective-permute-start | bytes 3145736 | tf_op jit(solution)/shard_map/ppermute | solution.py:863
  104.5 24.7 %collective-permute-start.13 = (bf16[2048,256]{1,0:T(8,128)(2,1)}, bf16[2048,256]{1,0:T(8,128)(2,1)S(1)}, u32[]{:S(2)}, u32[]{:S(2)}) collective-permute-start(bf16[2048,256]{1,0:T(8,128)(2,1)} %collective-permute-done.11.refs_1_), channel_id=1, source_target_pairs={{0,2},{2,4},{4,6},{6,7},{7,5},{5,3},{3,1},{1,0},{8,10},{10,12},{12... | collective-permute-start | bytes 3145736 | tf_op jit(solution)/shard_map/ppermute | solution.py:859
  105.1 24.6 %collective-permute-start.14 = (bf16[2048,256]{1,0:T(8,128)(2,1)}, bf16[2048,256]{1,0:T(8,128)(2,1)S(1)}, u32[]{:S(2)}, u32[]{:S(2)}) collective-permute-start(bf16[2048,256]{1,0:T(8,128)(2,1)} %collective-permute-done.12.refs_2_), channel_id=1, source_target_pairs={{2,0},{4,2},{6,4},{7,6},{5,7},{3,5},{1,3},{0,1},{10,8},{12,10},{14... | collective-permute-start | bytes 3145736 | tf_op jit(solution)/shard_map/ppermute | solution.py:863
  129.7 26.0 %collective-permute-start.22 = (bf16[512,2048]{1,0:T(8,128)(2,1)}, bf16[512,2048]{1,0:T(8,128)(2,1)S(1)}, u32[]{:S(2)}, u32[]{:S(2)}) collective-permute-start(bf16[512,2048]{1,0:T(8,128)(2,1)} %collective-permute-done.16), channel_id=1, source_target_pairs={{0,8},{8,0},{16,24},{24,16},{1,9},{9,1},{17,25},{25,17},{2,10},{10... | collective-permute-start | bytes 6291464 | tf_op jit(solution)/shard_map/ppermute | solution.py:855
  129.7 25.6 %collective-permute-start.18 = (bf16[2048,256]{1,0:T(8,128)(2,1)S(1)}, bf16[2048,256]{1,0:T(8,128)(2,1)S(1)}, u32[]{:S(2)}, u32[]{:S(2)}) collective-permute-start(bf16[2048,256]{1,0:T(8,128)(2,1)S(1)} %collective-permute-done.13.refs_3_), channel_id=1, source_target_pairs={{0,2},{2,4},{4,6},{6,7},{7,5},{5,3},{3,1},{1,0},{8,10},{10,12},{12... | collective-permute-start | bytes 3145736 | tf_op jit(solution)/shard_map/ppermute | solution.py:859
  130.1 25.5 %collective-permute-start.19 = (bf16[2048,256]{1,0:T(8,128)(2,1)S(1)}, bf16[2048,256]{1,0:T(8,128)(2,1)S(1)}, u32[]{:S(2)}, u32[]{:S(2)}) collective-permute-start(bf16[2048,256]{1,0:T(8,128)(2,1)S(1)} %collective-permute-done.14.refs_4_), channel_id=1, source_target_pairs={{2,0},{4,2},{6,4},{7,6},{5,7},{3,5},{1,3},{0,1},{10,8},{12,10},{14... | collective-permute-start | bytes 3145736 | tf_op jit(solution)/shard_map/ppermute | solution.py:863
  275.3 34.2 %collective-permute-start.32 = (bf16[512,2048]{1,0:T(8,128)(2,1)}, bf16[512,2048]{1,0:T(8,128)(2,1)S(1)}, u32[]{:S(2)}, u32[]{:S(2)}) collective-permute-start(bf16[512,2048]{1,0:T(8,128)(2,1)} %get-tuple-element.201), channel_id=1, source_target_pairs={{0,8},{8,0},{16,24},{24,16},{1,9},{9,1},{17,25},{25,17},{2,10},{10... | collective-permute-start | bytes 6291464 | tf_op jit(solution)/shard_map/ppermute | solution.py:855
  275.3 34.2 %collective-permute-start.30 = (bf16[2048,256]{1,0:T(8,128)(2,1)}, bf16[2048,256]{1,0:T(8,128)(2,1)S(1)}, u32[]{:S(2)}, u32[]{:S(2)}) collective-permute-start(bf16[2048,256]{1,0:T(8,128)(2,1)} %pad_maximum_fusion.4), channel_id=1, source_target_pairs={{0,2},{2,4},{4,6},{6,7},{7,5},{5,3},{3,1},{1,0},{8,10},{10,12},{12... | collective-permute-start | bytes 3145736 | tf_op jit(solution)/shard_map/ppermute | solution.py:859
  276.9 32.6 %collective-permute-start.31 = (bf16[2048,256]{1,0:T(8,128)(2,1)S(1)}, bf16[2048,256]{1,0:T(8,128)(2,1)S(1)}, u32[]{:S(2)}, u32[]{:S(2)}) collective-permute-start(bf16[2048,256]{1,0:T(8,128)(2,1)S(1)} %pad_maximum_fusion.5), channel_id=1, source_target_pairs={{2,0},{4,2},{6,4},{7,6},{5,7},{3,5},{1,3},{0,1},{10,8},{12,10},{14... | collective-permute-start | bytes 3145736 | tf_op jit(solution)/shard_map/ppermute | solution.py:863
  277.3 55.7 %collective-permute-start.35 = (bf16[512,2048]{1,0:T(8,128)(2,1)}, bf16[512,2048]{1,0:T(8,128)(2,1)S(1)}, u32[]{:S(2)}, u32[]{:S(2)}) collective-permute-start(bf16[512,2048]{1,0:T(8,128)(2,1)} %get-tuple-element.291), channel_id=1, source_target_pairs={{0,8},{8,0},{16,24},{24,16},{1,9},{9,1},{17,25},{25,17},{2,10},{10... | collective-permute-start | bytes 6291464 | tf_op jit(solution)/shard_map/ppermute | solution.py:855
  314.2 25.9 %collective-permute-start.33 = (bf16[2048,256]{1,0:T(8,128)(2,1)}, bf16[2048,256]{1,0:T(8,128)(2,1)}, u32[]{:S(2)}, u32[]{:S(2)}) collective-permute-start(bf16[2048,256]{1,0:T(8,128)(2,1)} %add_convert_fusion.6), channel_id=1, source_target_pairs={{0,2},{2,4},{4,6},{6,7},{7,5},{5,3},{3,1},{1,0},{8,10},{10,12},{12... | collective-permute-start | bytes 3145736 | tf_op jit(solution)/shard_map/ppermute | solution.py:859
  315.9 25.6 %collective-permute-start.34 = (bf16[2048,256]{1,0:T(8,128)(2,1)}, bf16[2048,256]{1,0:T(8,128)(2,1)}, u32[]{:S(2)}, u32[]{:S(2)}) collective-permute-start(bf16[2048,256]{1,0:T(8,128)(2,1)} %add_convert_fusion.5), channel_id=1, source_target_pairs={{2,0},{4,2},{6,4},{7,6},{5,7},{3,5},{1,3},{0,1},{10,8},{12,10},{14... | collective-permute-start | bytes 3145736 | tf_op jit(solution)/shard_map/ppermute | solution.py:863
  346.7 39.2 %collective-permute-start.36 = (bf16[2048,256]{1,0:T(8,128)(2,1)}, bf16[2048,256]{1,0:T(8,128)(2,1)}, u32[]{:S(2)}, u32[]{:S(2)}) collective-permute-start(bf16[2048,256]{1,0:T(8,128)(2,1)} %add_convert_fusion.4), channel_id=1, source_target_pairs={{0,2},{2,4},{4,6},{6,7},{7,5},{5,3},{3,1},{1,0},{8,10},{10,12},{12... | collective-permute-start | bytes 3145736 | tf_op jit(solution)/shard_map/ppermute | solution.py:859
  348.3 37.6 %collective-permute-start.37 = (bf16[2048,256]{1,0:T(8,128)(2,1)}, bf16[2048,256]{1,0:T(8,128)(2,1)}, u32[]{:S(2)}, u32[]{:S(2)}) collective-permute-start(bf16[2048,256]{1,0:T(8,128)(2,1)} %add_convert_fusion.3), channel_id=1, source_target_pairs={{2,0},{4,2},{6,4},{7,6},{5,7},{3,5},{1,3},{0,1},{10,8},{12,10},{14... | collective-permute-start | bytes 3145736 | tf_op jit(solution)/shard_map/ppermute | solution.py:863
  348.8 65.2 %collective-permute-start.42 = (bf16[512,2048]{1,0:T(8,128)(2,1)S(1)}, bf16[512,2048]{1,0:T(8,128)(2,1)}, u32[]{:S(2)}, u32[]{:S(2)}) collective-permute-start(bf16[512,2048]{1,0:T(8,128)(2,1)S(1)} %add_convert_fusion.1), channel_id=1, source_target_pairs={{0,16},{8,24},{16,0},{24,8},{1,17},{9,25},{17,1},{25,9},{2,18},{10... | collective-permute-start | bytes 6291464 | tf_op jit(solution)/shard_map/ppermute | solution.py:855
  386.1 32.6 %collective-permute-start.41 = (bf16[256,2048]{1,0:T(8,128)(2,1)S(1)}, bf16[256,2048]{1,0:T(8,128)(2,1)S(1)}, u32[]{:S(2)}, u32[]{:S(2)}) collective-permute-start(bf16[256,2048]{1,0:T(8,128)(2,1)S(1)} %get-tuple-element.314), channel_id=1, source_target_pairs={{0,16},{8,24},{16,0},{24,8},{1,17},{9,25},{17,1},{25,9},{2,18},{10... | collective-permute-start | bytes 3145736 | tf_op jit(solution)/shard_map/ppermute | solution.py:855
  420.7 24.1 %collective-permute-start.45 = (bf16[256,2048]{1,0:T(8,128)(2,1)S(1)}, bf16[256,2048]{1,0:T(8,128)(2,1)S(1)}, u32[]{:S(2)}, u32[]{:S(2)}) collective-permute-start(bf16[256,2048]{1,0:T(8,128)(2,1)S(1)} %get-tuple-element.244), channel_id=1, source_target_pairs={{0,16},{8,24},{16,0},{24,8},{1,17},{9,25},{17,1},{25,9},{2,18},{10... | collective-permute-start | bytes 3145736 | tf_op jit(solution)/shard_map/ppermute | solution.py:855
  459.2 30.2 %collective-permute-start.51 = (bf16[2048,256]{1,0:T(8,128)(2,1)S(1)}, bf16[2048,256]{1,0:T(8,128)(2,1)}, u32[]{:S(2)}, u32[]{:S(2)}) collective-permute-start(bf16[2048,256]{1,0:T(8,128)(2,1)S(1)} %add_convert_fusion.2.refs_0_), channel_id=1, source_target_pairs={{0,16},{8,24},{16,0},{24,8},{1,17},{9,25},{17,1},{25,9},{2,18},{10... | collective-permute-start | bytes 3145736 | tf_op jit(solution)/shard_map/ppermute | solution.py:855
  474.2 27.5 %collective-permute-start.56 = (bf16[2048,256]{1,0:T(8,128)(2,1)S(1)}, bf16[2048,256]{1,0:T(8,128)(2,1)S(1)}, u32[]{:S(2)}, u32[]{:S(2)}) collective-permute-start(bf16[2048,256]{1,0:T(8,128)(2,1)S(1)} %add_convert_fusion.2.refs_0_), channel_id=1, source_target_pairs={{0,8},{8,0},{16,24},{24,16},{1,9},{9,1},{17,25},{25,17},{2,10},{10... | collective-permute-start | bytes 3145736 | tf_op jit(solution)/shard_map/ppermute | solution.py:855
  (83 other events, 1207.2 us)
